TPU v7x, 32 devices: a whole 2x2x4 slice. The times are simulated.
32 devices in a mesh: tm: 8 (over z, x), space: 4 (over y, core).
Axes of the slice: x: 2, y: 2, z: 4, core: 2. Of those that a mesh axis runs over, the one named last changes fastest.
Arguments:
- state: float32 [16, 3, 128, 1024], P('tm', None, 'space'), may hold values from -2.5 to 2.5
- initial: float32 [3, 128, 1024], P(None, 'space'), may hold values from -2.5 to 2.5
Outputs:
- updated: float32 [16, 3, 128, 1024], P('tm', None, 'space')
All inputs are finite; a program needn't handle non-finite values.
Results may differ from a plain program's by a relative error of at most 0.0003.
Values sent between devices are 32-bit elements; how exact they have to be, the bound alone decides.
No kernel may reach another device: no remote copies, remote signals or barrier semaphores. Data moves between devices by JAX's collectives and lax.ppermute only.
A program may use at most 128 MiB of HBM per device.

v0:
```python
import math

import jax
import jax.numpy as jnp
from jax import lax
from jax.sharding import PartitionSpec as P

SWEEPS = 4


circulant_alpha = 0.1
time_step = 0.5
coriolis = 0.3
viscous = 0.2
highest = lax.Precision.HIGHEST


def from_behind(block, axis, distance):
    devices = range(lax.axis_size(axis))
    route = [(i - distance, i) for i in devices if i - distance in devices]
    return lax.ppermute(block, axis, route)


def extended(cells, sides, width):
    for axis, dim in sides:
        count = lax.axis_size(axis)
        head = lax.slice_in_dim(cells, 0, width, axis=dim)
        tail = lax.slice_in_dim(cells, cells.shape[dim] - width, cells.shape[dim], axis=dim)
        cells = jnp.concatenate(
            [
                lax.ppermute(tail, axis, [(i, (i + 1) % count) for i in range(count)]),
                cells,
                lax.ppermute(head, axis, [((i + 1) % count, i) for i in range(count)]),
            ],
            axis=dim,
        )
    return cells


def interior(values):
    return values[..., 1:-1, :]


def column_diff(values):
    return 0.5 * (jnp.roll(values, -1, axis=-1) - jnp.roll(values, 1, axis=-1))[..., 1:-1, :]


def row_diff(values):
    return 0.5 * (values[..., 2:, :] - values[..., :-2, :])


def laplace(values):
    return (
        values[..., 2:, :]
        + values[..., :-2, :]
        + jnp.roll(values, -1, axis=-1)[..., 1:-1, :]
        + jnp.roll(values, 1, axis=-1)[..., 1:-1, :]
        - 4.0 * values[..., 1:-1, :]
    )


def tendency(padded):
    surface = padded[..., 0, :, :]
    eastward = padded[..., 1, :, :]
    northward = padded[..., 2, :, :]
    column_depth = 1.0 + surface
    east_inner = interior(eastward)
    north_inner = interior(northward)
    mass_change = time_step * (
        column_diff(column_depth * eastward) + row_diff(column_depth * northward)
    ) - viscous * laplace(surface)
    east_change = (
        time_step
        * (
            east_inner * column_diff(eastward)
            + north_inner * row_diff(eastward)
            + column_diff(surface)
        )
        - coriolis * north_inner
        - viscous * laplace(eastward)
    )
    north_change = (
        time_step
        * (
            east_inner * column_diff(northward)
            + north_inner * row_diff(northward)
            + row_diff(surface)
        )
        + coriolis * east_inner
        - viscous * laplace(northward)
    )
    return jnp.stack([mass_change, east_change, north_change], axis=-3)


def linear_part(padded):
    surface = padded[..., 0, :, :]
    eastward = padded[..., 1, :, :]
    northward = padded[..., 2, :, :]
    mass_change = time_step * (column_diff(eastward) + row_diff(northward)) - viscous * laplace(
        surface
    )
    east_change = (
        time_step * column_diff(surface)
        - coriolis * interior(northward)
        - viscous * laplace(eastward)
    )
    north_change = (
        time_step * row_diff(surface) + coriolis * interior(eastward) - viscous * laplace(northward)
    )
    return jnp.stack([mass_change, east_change, north_change], axis=-3)


def pair_apply(factors, values):
    factor = factors[:, :, None, None, None]
    return jnp.stack(
        [
            factor[0] * values[0] - factor[1] * values[1],
            factor[2] * values[1] + factor[3] * values[0],
        ]
    )


def sweep_weights():
    return [
        1.0 / (1.15 - 0.85 * math.cos(math.pi * (2 * sweep + 1) / (2 * SWEEPS)))
        for sweep in range(SWEEPS)
    ]


def slot_factors(slot_index, total_steps):
    decay_base = circulant_alpha ** (1.0 / total_steps)
    angles = 2.0 * math.pi / total_steps * slot_index.astype(jnp.float32)
    real_eigen = 1.0 - decay_base * jnp.cos(angles)
    imaginary_eigen = decay_base * jnp.sin(angles)
    real_shift = real_eigen + 4.0 * viscous
    modulus = real_shift * real_shift + imaginary_eigen * imaginary_eigen
    eigen = jnp.stack([real_eigen, imaginary_eigen, real_eigen, imaginary_eigen])
    jacobi = jnp.stack(
        [
            real_shift / modulus,
            -imaginary_eigen / modulus,
            real_shift / modulus,
            -imaginary_eigen / modulus,
        ]
    )
    leading = (slot_index == 0)[None, :]
    zero_part = jnp.zeros_like(real_eigen)
    packed_eigen = jnp.stack(
        [zero_part + (1.0 - decay_base), zero_part, zero_part + (1.0 + decay_base), zero_part]
    )
    packed_jacobi = jnp.stack(
        [
            zero_part + 1.0 / (1.0 - decay_base + 4.0 * viscous),
            zero_part,
            zero_part + 1.0 / (1.0 + decay_base + 4.0 * viscous),
            zero_part,
        ]
    )
    eigen = jnp.where(leading, packed_eigen, eigen)
    jacobi = jnp.where(leading, packed_jacobi, jacobi)
    return (eigen, jacobi)


def time_tables(total_steps):
    slot_total = total_steps // 2
    step_ids = jnp.arange(total_steps, dtype=jnp.int32)
    slot_ids = jnp.arange(slot_total, dtype=jnp.int32)
    phase = slot_ids[:, None] * step_ids[None, :] % total_steps
    angles = 2.0 * math.pi / total_steps * phase.astype(jnp.float32)
    decay_base = circulant_alpha ** (1.0 / total_steps)
    growth = decay_base ** step_ids.astype(jnp.float32)
    cosine = jnp.cos(angles)
    sines = jnp.sin(angles)
    forward_real = cosine * growth[None, :]
    forward_imaginary = -sines * growth[None, :]
    inverse_imaginary = -sines
    alternate = 1.0 - 2.0 * (step_ids % 2).astype(jnp.float32)
    leading = (slot_ids == 0)[:, None]
    forward_imaginary = jnp.where(leading, (alternate * growth)[None, :], forward_imaginary)
    inverse_real = jnp.where(leading, 1.0, 2.0 * cosine)
    inverse_imaginary = jnp.where(leading, alternate[None, :], -2.0 * sines)
    forward = jnp.concatenate([forward_real, forward_imaginary], axis=0)
    inverse = jnp.concatenate([inverse_real, inverse_imaginary], axis=0).T
    inverse = inverse * (1.0 / (total_steps * growth))[:, None]
    return (forward, inverse)


def on_device(state, initial):
    steps_dev, fields, band_rows, columns = state.shape
    width_tm = lax.axis_size("tm")
    total_steps = steps_dev * width_tm
    previous = from_behind(state[-1], "tm", 1)
    previous = jnp.where(lax.axis_index("tm") == 0, initial, previous)
    before = jnp.concatenate([previous[None], state[:-1]], axis=0)
    padded = extended(state, (("space", 2),), 1)
    residual = state - before + tendency(padded)
    forward, inverse = time_tables(total_steps)
    slot_total = forward.shape[0] // 2
    per_device = slot_total // width_tm
    spectrum = jnp.einsum(
        "rj,jnc->rnc",
        forward,
        lax.all_to_all(
            residual.reshape(steps_dev, fields, band_rows * columns),
            "tm",
            split_axis=2,
            concat_axis=0,
            tiled=True,
        ),
        precision=highest,
    )
    spectrum = spectrum.reshape(2, slot_total, fields, spectrum.shape[-1])
    banded = lax.all_to_all(spectrum, "tm", split_axis=1, concat_axis=3, tiled=True).reshape(
        2, per_device, fields, band_rows, columns
    )
    slot_index = lax.axis_index("tm") * per_device + jnp.arange(per_device, dtype=jnp.int32)
    eigen, jacobi = slot_factors(slot_index, total_steps)
    weights = sweep_weights()
    iterate = weights[0] * pair_apply(jacobi, banded)
    for sweep in range(1, SWEEPS):
        border = extended(iterate, (("space", 3),), 1)
        applied = pair_apply(eigen, iterate) + linear_part(border)
        iterate = iterate + weights[sweep] * pair_apply(jacobi, banded - applied)
    flat_solution = iterate.reshape(2, per_device, fields, band_rows * columns)
    blocks = lax.all_to_all(flat_solution, "tm", split_axis=3, concat_axis=1, tiled=True)
    merged = blocks.reshape(2 * blocks.shape[1], blocks.shape[2], blocks.shape[3])
    all_steps = jnp.einsum("jr,rnc->jnc", inverse, merged, precision=highest)
    correction = lax.all_to_all(all_steps, "tm", split_axis=0, concat_axis=2, tiled=True)
    return state - correction.reshape(state.shape)


def solution(mesh):
    in_specs = (P("tm", None, "space", None), P(None, "space", None))
    out_specs = P("tm", None, "space", None)
    return jax.shard_map(
        on_device, mesh=mesh, in_specs=in_specs, out_specs=out_specs, check_vma=False
    )
```

profile of v0, /device:TPU:0, one launch (start us, length us, event | category | flops | bytes accessed | tf_op | source)
XLA Modules:
  0.0 523.8 jit_solution(6862087459454074944)
XLA Ops:
  1.6 2.0 collective-permute-start.2
  4.8 4.1 collective-permute-start
  12.3 5.0 collective-permute-done
  19.7 22.5 %copy.200 = f32[2,3,32,1024]{1,0,3,2:T(2,128)} copy(f32[2,3,32,1024]{3,2,1,0:T(8,128)S(1)} %fusion) | data formatting | bytes 1572864 | tf_op jit(solution)/shard_map/reshape | solution.py:204
  42.2 53.4 %reshape.1343 = f32[8,1,24576]{2,1,0:T(1,128)} reshape(f32[32768,2,3]{2,1,0:T(2,128)} %bitcast.191) | data formatting | bytes 1572864
  95.6 6.0 %all-to-all-start = ((f32[8,1,24576]{2,1,0:T(1,128)}), f32[8,1,24576]{2,1,0:T(1,128)S(1)}, u32[]{:S(2)}, u32[]{:S(2)}) async-start(f32[8,1,24576]{2,1,0:T(1,128)} %reshape.1343), calls=%async_computation | async-start | bytes 1572864 | tf_op jit(solution)/shard_map/all_to_all | solution.py:203
  101.8 19.0 %all-to-all-done = f32[8,1,24576]{2,1,0:T(1,128)S(1)} async-done(((f32[8,1,24576]{2,1,0:T(1,128)}), f32[8,1,24576]{2,1,0:T(1,128)S(1)}, u32[]{:S(2)}, u32[]{:S(2)}) %all-to-all-start) | async-done | bytes 786464 | tf_op jit(solution)/shard_map/all_to_all | solution.py:203
  121.3 2.4 reduce
  123.7 61.6 %reshape.1344 = f32[32768,2,3]{2,1,0:T(2,128)} reshape(f32[8,24576]{1,0:T(8,128)S(1)} %reduce) | data formatting | bytes 1572864
  185.4 26.6 %copy.198 = f32[2,3,8,4096]{3,2,0,1:T(8,128)S(1)} copy(f32[2,3,8,4096]{1,0,3,2:T(2,128)} %bitcast.192) | data formatting | bytes 1572864 | tf_op jit(solution)/shard_map/all_to_all | solution.py:203
  213.9 1.5 copy.172
  215.4 3.8 all-to-all-start.1
  220.9 18.6 %all-to-all-done.1 = f32[2,8,3,4096]{3,0,2,1:T(2,128)S(1)} async-done(((f32[2,8,3,4096]{3,0,2,1:T(2,128)}), f32[2,8,3,4096]{3,0,2,1:T(2,128)S(1)}, u32[]{:S(2)}, u32[]{:S(2)}) %all-to-all-start.1) | async-done | bytes 786464 | tf_op jit(solution)/shard_map/all_to_all | solution.py:213
  240.0 2.8 multiply_subtract_fusion.3
  244.4 1.7 collective-permute-start.4
  246.1 3.6 multiply_subtract_fusion.2
  250.0 2.2 stack.138
  257.3 2.8 fusion.13
  261.0 1.7 collective-permute-start.6
  262.7 3.5 multiply_subtract_fusion.1
  276.1 2.7 multiply_subtract_fusion
  278.9 2.1 collective-permute-start.8
  286.3 2.8 fusion.11
  290.0 4.5 fusion.7
  294.5 29.3 %copy.191 = f32[2,1,3,32768]{2,0,1,3:T(2,128)} copy(f32[2,1,3,32768]{3,1,2,0:T(1,128)S(1)} %fusion.7) | data formatting | bytes 1572864 | tf_op jit(solution)/shard_map/add | solution.py:223
  323.8 53.4 %reshape.1345 = f32[8,1,24576]{2,1,0:T(1,128)} reshape(f32[32768,1,2,3]{3,2,1,0:T(2,128)} %bitcast.193) | data formatting | bytes 1572864
  377.1 3.7 all-to-all-start.2
  380.9 19.7 %all-to-all-done.2 = f32[8,1,24576]{2,1,0:T(1,128)S(1)} async-done(((f32[8,1,24576]{2,1,0:T(1,128)}), f32[8,1,24576]{2,1,0:T(1,128)S(1)}, u32[]{:S(2)}, u32[]{:S(2)}) %all-to-all-start.2) | async-done | bytes 786464 | tf_op jit(solution)/shard_map/all_to_all | solution.py:225
  400.6 2.4 reduce.1
  403.0 61.5 %reshape.1346 = f32[32768,1,2,3]{3,2,1,0:T(2,128)} reshape(f32[8,24576]{1,0:T(8,128)S(1)} %reduce.1) | data formatting | bytes 1572864
  464.5 26.6 %copy.199 = f32[2,1,3,8,4096]{4,3,0,2,1:T(8,128)S(1)} copy(f32[2,1,3,8,4096]{2,0,4,3,1:T(2,128)} %bitcast.194) | data formatting | bytes 1572864 | tf_op jit(solution)/shard_map/all_to_all | solution.py:225
  492.5 29.2 %all_to_all.63 = f32[16,3,4096]{2,1,0:T(4,128)S(1)} all-to-all(f32[16,3,4096]{2,1,0:T(4,128)S(1)} %copy.193), channel_id=1, replica_groups=mesh['tm'=8,'space'=4] {'tm'}, dimensions={0} | all-to-all | bytes 1572864 | tf_op jit(solution)/shard_map/all_to_all | solution.py:228
  (111 shorter events, 39.8 us)
Async XLA Ops:
  1.1 7.9 %collective-permute-start.1 = (f32[2,3,1,1024]{3,2,0,1:T(1,128)S(1)}, f32[2,3,1,1024]{3,2,0,1:T(1,128)S(1)}, u32[]{:S(2)}, u32[]{:S(2)}) collective-permute-start(f32[2,3,1,1024]{3,2,0,1:T(1,128)S(1)} %get-tuple-element.37), channel_id=1, source_target_pairs={{0,1},{1,2},{2,3},{3,0},{4,5},{5,6},{6,7},{7,4},{8,9},{9,10},{10,1... | collective-permute-start | bytes 73736 | tf_op jit(solution)/shard_map/ppermute | solution.py:31
  1.6 7.4 %collective-permute-start.2 = (f32[2,3,1,1024]{3,2,0,1:T(1,128)S(1)}, f32[2,3,1,1024]{3,2,0,1:T(1,128)S(1)}, u32[]{:S(2)}, u32[]{:S(2)}) collective-permute-start(f32[2,3,1,1024]{3,2,0,1:T(1,128)S(1)} %get-tuple-element.38), channel_id=1, source_target_pairs={{1,0},{2,1},{3,2},{0,3},{5,4},{6,5},{7,6},{4,7},{9,8},{10,9},{11,1... | collective-permute-start | bytes 73736 | tf_op jit(solution)/shard_map/ppermute | solution.py:33
  4.8 12.5 %collective-permute-start = (f32[3,32,1024]{2,1,0:T(8,128)S(1)}, f32[3,32,1024]{2,1,0:T(8,128)S(1)}, u32[]{:S(2)}, u32[]{:S(2)}) collective-permute-start(f32[3,32,1024]{2,1,0:T(8,128)S(1)} %get-tuple-element.39), channel_id=1, source_target_pairs={{0,4},{4,8},{8,12},{12,16},{16,20},{20,24},{24,28},{1,5},{5,9},{9,... | collective-permute-start | bytes 1179656 | tf_op jit(solution)/shard_map/ppermute | solution.py:21
  95.6 25.2 %all-to-all-start = ((f32[8,1,24576]{2,1,0:T(1,128)}), f32[8,1,24576]{2,1,0:T(1,128)S(1)}, u32[]{:S(2)}, u32[]{:S(2)}) async-start(f32[8,1,24576]{2,1,0:T(1,128)} %reshape.1343), calls=%async_computation | async-start | bytes 1572864 | tf_op jit(solution)/shard_map/all_to_all | solution.py:203
  123.7 95.7 %copy-start.2 = (f32[4,1]{0,1:T(1,128)S(1)}, f32[4,1]{0,1:T(1,128)}, u32[]{:S(2)}) copy-start(f32[4,1]{0,1:T(1,128)} %constant.104.clone.1) | copy-start | bytes 52
  123.7 95.7 %copy-start.3 = (f32[4,1]{0,1:T(1,128)S(1)}, f32[4,1]{0,1:T(1,128)}, u32[]{:S(2)}) copy-start(f32[4,1]{0,1:T(1,128)} %constant.113.clone.1) | copy-start | bytes 52
  215.4 24.1 %all-to-all-start.1 = ((f32[2,8,3,4096]{3,0,2,1:T(2,128)}), f32[2,8,3,4096]{3,0,2,1:T(2,128)S(1)}, u32[]{:S(2)}, u32[]{:S(2)}) async-start(f32[2,8,3,4096]{3,0,2,1:T(2,128)} %copy.172), calls=%async_computation.1 | async-start | bytes 1572864 | tf_op jit(solution)/shard_map/all_to_all | solution.py:213
  242.7 0.8 copy-start.1
  244.4 9.0 %collective-permute-start.3 = (f32[2,1,3,1,1024]{4,3,0,2,1:T(1,128)}, f32[2,1,3,1,1024]{4,3,0,2,1:T(1,128)}, u32[]{:S(2)}, u32[]{:S(2)}) collective-permute-start(f32[2,1,3,1,1024]{4,3,0,2,1:T(1,128)} %get-tuple-element.31), channel_id=1, source_target_pairs={{0,1},{1,2},{2,3},{3,0},{4,5},{5,6},{6,7},{7,4},{8,9},{9,10},{10,1... | collective-permute-start | bytes 73736 | tf_op jit(solution)/shard_map/ppermute | solution.py:31
  244.4 9.0 %collective-permute-start.4 = (f32[2,1,3,1,1024]{4,3,0,2,1:T(1,128)}, f32[2,1,3,1,1024]{4,3,0,2,1:T(1,128)}, u32[]{:S(2)}, u32[]{:S(2)}) collective-permute-start(f32[2,1,3,1,1024]{4,3,0,2,1:T(1,128)} %get-tuple-element.32), channel_id=1, source_target_pairs={{1,0},{2,1},{3,2},{0,3},{5,4},{6,5},{7,6},{4,7},{9,8},{10,9},{11,1... | collective-permute-start | bytes 73736 | tf_op jit(solution)/shard_map/ppermute | solution.py:33
  260.9 7.6 %collective-permute-start.5 = (f32[2,1,3,1,1024]{4,3,0,2,1:T(1,128)}, f32[2,1,3,1,1024]{4,3,0,2,1:T(1,128)}, u32[]{:S(2)}, u32[]{:S(2)}) collective-permute-start(f32[2,1,3,1,1024]{4,3,0,2,1:T(1,128)} %get-tuple-element.25), channel_id=1, source_target_pairs={{0,1},{1,2},{2,3},{3,0},{4,5},{5,6},{6,7},{7,4},{8,9},{9,10},{10,1... | collective-permute-start | bytes 73736 | tf_op jit(solution)/shard_map/ppermute | solution.py:31
  261.0 7.6 %collective-permute-start.6 = (f32[2,1,3,1,1024]{4,3,0,2,1:T(1,128)}, f32[2,1,3,1,1024]{4,3,0,2,1:T(1,128)}, u32[]{:S(2)}, u32[]{:S(2)}) collective-permute-start(f32[2,1,3,1,1024]{4,3,0,2,1:T(1,128)} %get-tuple-element.26), channel_id=1, source_target_pairs={{1,0},{2,1},{3,2},{0,3},{5,4},{6,5},{7,6},{4,7},{9,8},{10,9},{11,1... | collective-permute-start | bytes 73736 | tf_op jit(solution)/shard_map/ppermute | solution.py:33
  278.9 4.6 collective-permute-start.7
  278.9 4.5 collective-permute-start.8
  377.1 23.4 %all-to-all-start.2 = ((f32[8,1,24576]{2,1,0:T(1,128)}), f32[8,1,24576]{2,1,0:T(1,128)S(1)}, u32[]{:S(2)}, u32[]{:S(2)}) async-start(f32[8,1,24576]{2,1,0:T(1,128)} %reshape.1345), calls=%async_computation.2 | async-start | bytes 1572864 | tf_op jit(solution)/shard_map/all_to_all | solution.py:225
  403.0 119.4 %copy-start = (f32[2,3,32,1024]{3,2,1,0:T(8,128)S(1)}, f32[2,3,32,1024]{3,2,1,0:T(8,128)}, u32[]{:S(2)}) copy-start(f32[2,3,32,1024]{3,2,1,0:T(8,128)} %param.2) | copy-start | bytes 2359300
where the time goes:
time: 532 us; the launch traced here: 524 us
  local copies, waits for them, and re-layouts  357 us (67%)
  waiting for transfers between devices  62.3 us (12%)
  other arithmetic  46.3 us (9%)
  blocking collectives  29.2 us (5%)
  starting transfers between devices  25.8 us (5%)
    unnamed x12, local copies, waits for them, and re-layouts  231 us
    add x1, local copies, waits for them, and re-layouts, on_device(): iterate = iterate + weights[sweep] * pair_apply(jacobi, banded - applied)  29.3 us
    all_to_all x1, blocking collectives, on_device(): lax.all_to_all(all_steps, 'tm', split_axis=0, concat_axis=2, tiled=True)  29.2 us
    all_to_all x4, local copies, waits for them, and re-layouts, on_device(): lax.all_to_all(residual.reshape(steps_dev, fields, band_rows * columns),...  28.2 us
    all_to_all x1, local copies, waits for them, and re-layouts, on_device(): lax.all_to_all(flat_solution, 'tm', split_axis=3, concat_axis=1, tiled=True)  26.6 us
    reshape x1, local copies, waits for them, and re-layouts, on_device(): residual.reshape(steps_dev, fields, band_rows * columns)  22.5 us
    all_to_all x1, waiting for transfers between devices, on_device(): lax.all_to_all(flat_solution, 'tm', split_axis=3, concat_axis=1, tiled=True)  19.7 us
    sub x7, other arithmetic, pair_apply(): factor[0] * values[0] - factor[1] * values[1]  19.5 us
  transfers between devices with their start and end apart: 12, of which 4 were waited for; matrix products, arithmetic and copies ran while one was open for 4% of the time, Pallas kernels for 0%

commit v1 on v0

--- a/solution.py
+++ b/solution.py
@@ -1,8 +1,11 @@
+import functools
 import math
 
 import jax
 import jax.numpy as jnp
 from jax import lax
+from jax.experimental import pallas as pl
+from jax.experimental.pallas import tpu as pltpu
 from jax.sharding import PartitionSpec as P
 
 SWEEPS = 4
@@ -229,9 +232,387 @@
     return state - correction.reshape(state.shape)
 
 
+LANES = 128
+HALO = SWEEPS
+GROUP = 2 * HALO
+ROW0 = 8
+MAIN = ROW0 + HALO
+SHIFT = 1.0 + 4.0 * viscous
+VMEM_BYTES = 48 * 1024 * 1024
+
+
+def fits_fast_plan(state, width_tm):
+    steps_dev, fields, band_rows, columns = state.shape
+    total_steps = steps_dev * width_tm
+    return (
+        columns == LANES * width_tm
+        and GROUP * total_steps == LANES
+        and width_tm & (width_tm - 1) == 0
+        and band_rows % 8 == 0
+        and fields == 3
+    )
+
+
+def lanes():
+    return lax.broadcasted_iota(jnp.int32, (8, LANES), 1)
+
+
+def step_of_lane(lane):
+    return ((lane + HALO) & (LANES - 1)) // GROUP
+
+
+def turn(values, shift):
+    return pltpu.roll(values, shift % LANES, 1)
+
+
+def tile_at(index):
+    return pl.ds(pl.multiple_of(index * LANES, LANES), LANES)
+
+
+def pack_kernel(count, state_ref, *outs):
+    steps_dev, fields, rows, _ = state_ref.shape
+    me = lax.axis_index("tm")
+    lane = lanes()
+    step = step_of_lane(lane)
+    blocks = rows // 8
+    main = steps_dev * fields * rows
+    for b in range(count):
+        tile = me ^ b
+        here = tile_at(tile)
+        after = tile_at((tile + 1) & (count - 1))
+        prior = tile_at((tile + count - 1) & (count - 1))
+        out = outs[b]
+        for i in range(steps_dev):
+            for f in range(fields):
+                at = (i * fields + f) * rows
+                out[at : at + rows, :] = state_ref[i, f, :, here]
+        for first in range(0, fields * blocks, count):
+            packed = jnp.zeros((8, LANES), jnp.float32)
+            for g in range(first, min(first + count, fields * blocks)):
+                f, r = divmod(g, blocks)
+                for i in range(steps_dev):
+                    slot = steps_dev * (g - first) + i
+                    sides = jnp.where(
+                        lane < LANES // 2,
+                        state_ref[i, f, 8 * r : 8 * r + 8, after],
+                        state_ref[i, f, 8 * r : 8 * r + 8, prior],
+                    )
+                    packed = jnp.where(step == slot, turn(sides, GROUP * slot), packed)
+            at = main + 8 * (first // count)
+            out[at : at + 8, :] = packed
+
+
+def edge_kernel(count, steps_dev, *refs):
+    pieces, initial_ref = refs[:count], refs[count]
+    up, down, side, side_initial = refs[count + 1 :]
+    fields, rows, _ = initial_ref.shape
+    me = lax.axis_index("tm")
+    lane = lanes()
+    owner = step_of_lane(lane) // steps_dev
+    blocks = rows // 8
+    main = steps_dev * fields * rows
+    here = tile_at(me)
+    after = tile_at((me + 1) & (count - 1))
+    prior = tile_at((me + count - 1) & (count - 1))
+    for g in range(fields * blocks):
+        f, r = divmod(g, blocks)
+        word, place = divmod(g, count)
+        found = jnp.zeros((8, LANES), jnp.float32)
+        for b in range(count):
+            source = me ^ b
+            value = pieces[b][main + 8 * word : main + 8 * word + 8, :]
+            shift = (GROUP * steps_dev * (source - place)) & (LANES - 1)
+            found = jnp.where(owner == source, pltpu.roll(value, shift, 1), found)
+        side[f, 8 * r : 8 * r + 8, :] = found
+        side_initial[f, 8 * r : 8 * r + 8, :] = jnp.where(
+            lane < LANES // 2,
+            initial_ref[f, 8 * r : 8 * r + 8, after],
+            initial_ref[f, 8 * r : 8 * r + 8, prior],
+        )
+    low, high = slice(0, HALO), slice(rows - HALO, rows)
+    for out, part in ((up, low), (down, high)):
+        k = 0
+        for b in range(count):
+            for at in range(0, main, rows):
+                out[k : k + HALO, :] = pieces[b][at + part.start : at + part.stop, :]
+                k += HALO
+        for f in range(fields):
+            out[k : k + HALO, :] = initial_ref[f, part, here]
+            k += HALO
+        for f in range(fields):
+            out[k : k + HALO, :] = side[f, part, :]
+            k += HALO
+        for f in range(fields):
+            out[k : k + HALO, :] = side_initial[f, part, :]
+            k += HALO
+
+
+def full_tendency(own, east, west, north, south):
+    e, u, v = own
+    around = [east[f] + west[f] + (north[f] + south[f]) for f in range(3)]
+    quarter = 0.5 * time_step
+    flux = ((1.0 + east[0]) * east[1] - (1.0 + west[0]) * west[1]) + (
+        (1.0 + south[0]) * south[2] - (1.0 + north[0]) * north[2]
+    )
+    carry1 = u * (east[1] - west[1]) + v * (south[1] - north[1]) + (east[0] - west[0])
+    carry2 = u * (east[2] - west[2]) + v * (south[2] - north[2]) + (south[0] - north[0])
+    diagonal = 1.0 + 4.0 * viscous
+    return (
+        diagonal * e + quarter * flux - viscous * around[0],
+        diagonal * u + quarter * carry1 - coriolis * v - viscous * around[1],
+        diagonal * v + quarter * carry2 + coriolis * u - viscous * around[2],
+    )
+
+
+def off_diagonal(own, east, west, north, south):
+    _, u, v = own
+    around = [east[f] + west[f] + (north[f] + south[f]) for f in range(3)]
+    quarter = 0.5 * time_step
+    return (
+        viscous * around[0] - quarter * ((east[1] - west[1]) + (south[2] - north[2])),
+        viscous * around[1] - quarter * (east[0] - west[0]) + coriolis * v,
+        viscous * around[2] - quarter * (south[0] - north[0]) - coriolis * u,
+    )
+
+
+def solve_kernel(count, steps_dev, *refs):
+    pieces, initial_ref = refs[:count], refs[count]
+    side_in, side_initial_in, above, below = refs[count + 1 : count + 5]
+    outs = refs[count + 5 : 2 * count + 5]
+    state, rhs, ya, yb, hstate, hbefore, hrhs, hya, hyb = refs[2 * count + 5 :]
+    fields, rows, _ = initial_ref.shape
+    total = count * steps_dev
+    me = lax.axis_index("tm")
+    lane = lanes()
+    step = step_of_lane(lane)
+    is_first, is_last = lane == 0, lane == LANES - 1
+    after_seam, before_seam = (lane & (GROUP - 1)) == 0, (lane & (GROUP - 1)) == GROUP - 1
+    q = 1.0 / SHIFT
+    wrap = circulant_alpha * q**total
+    wrap = wrap / (1.0 - wrap)
+    weights = sweep_weights()
+    body = slice(MAIN, MAIN + rows)
+    top, bottom = slice(ROW0, MAIN), slice(MAIN + rows, MAIN + rows + HALO)
+
+    k = 0
+    for b in range(count):
+        for i in range(steps_dev):
+            n = steps_dev * (me ^ b) + i
+            for f in range(fields):
+                at = (i * fields + f) * rows
+                state[n + 1, f, body, :] = pieces[b][at : at + rows, :]
+                state[n + 1, f, top, :] = above[k : k + HALO, :]
+                state[n + 1, f, bottom, :] = below[k : k + HALO, :]
+                k += HALO
+    for f in range(fields):
+        state[0, f, body, :] = initial_ref[f, :, tile_at(me)]
+        state[0, f, top, :] = above[k : k + HALO, :]
+        state[0, f, bottom, :] = below[k : k + HALO, :]
+        k += HALO
+    for held, given in ((hstate, side_in), (hbefore, side_initial_in)):
+        for f in range(fields):
+            held[f, body, :] = given[f, :, :]
+            held[f, top, :] = above[k : k + HALO, :]
+            held[f, bottom, :] = below[k : k + HALO, :]
+            k += HALO
+
+    def around(load, halves):
+        own = [load(f, 0) for f in range(fields)]
+        north = [load(f, -1) for f in range(fields)]
+        south = [load(f, 1) for f in range(fields)]
+        east, west = halves(own)
+        return own, east, west, north, south
+
+    def main_sides(seam, n):
+        def halves(own):
+            across = [turn(seam[f], -GROUP * n) for f in range(fields)]
+            east = [jnp.where(is_last, across[f], turn(own[f], -1)) for f in range(fields)]
+            west = [jnp.where(is_first, across[f], turn(own[f], 1)) for f in range(fields)]
+            return east, west
+
+        return halves
+
+    def side_sides(ends):
+        def halves(own):
+            east = [jnp.where(before_seam, turn(ends[f], -1), turn(own[f], -1)) for f in range(fields)]
+            west = [jnp.where(after_seam, turn(ends[f], 1), turn(own[f], 1)) for f in range(fields)]
+            return east, west
+
+        return halves
+
+    def seam_of(held, start):
+        values = [held[f, pl.ds(start, 8), :] for f in range(fields)]
+        return [jnp.where(after_seam, turn(v, 1), turn(v, -1)) for v in values]
+
+    def lane_sums(value):
+        reach = 1
+        while reach < total:
+            value = value + jnp.where(step >= reach, turn(value, GROUP * reach), 0.0)
+            reach *= 2
+        last = jnp.where(step == total - 1, value, 0.0)
+        reach = 1
+        while reach < total:
+            last = last + turn(last, -GROUP * reach)
+            reach *= 2
+        return value + wrap * last
+
+    lane_growth = jnp.exp(step.astype(jnp.float32) * math.log(SHIFT))
+    blocks = (rows + 2 * HALO) // 8
+
+    @pl.loop(0, blocks)
+    def _(t):
+        start = ROW0 + 8 * t
+        seam = seam_of(hstate, start)
+        ends = [jnp.zeros((8, LANES), jnp.float32)] * fields
+        sums = [jnp.zeros((8, LANES), jnp.float32)] * fields
+        for n in range(total):
+            load = lambda f, d: state[n + 1, f, pl.ds(start + d, 8), :]
+            parts = around(load, main_sides(seam, n))
+            value = full_tendency(*parts)
+            for f in range(fields):
+                ends[f] = jnp.where(step == n, turn(parts[0][f], GROUP * n), ends[f])
+                value_f = (value[f] - state[n, f, pl.ds(start, 8), :]) * SHIFT**n
+                rhs[n, f, pl.ds(start, 8), :] = value_f
+                sums[f] = sums[f] + value_f
+                ya[n, f, pl.ds(start, 8), :] = sums[f]
+        extra = [wrap * sums[f] for f in range(fields)]
+        for n in range(total):
+            for f in range(fields):
+                at = (n, f, pl.ds(start, 8), slice(None))
+                ya[at] = (weights[0] * q) * (ya[at] + extra[f])
+        load = lambda f, d: hstate[f, pl.ds(start + d, 8), :]
+        parts = around(load, side_sides(ends))
+        value = full_tendency(*parts)
+        for f in range(fields):
+            before = jnp.where(step == 0, hbefore[f, pl.ds(start, 8), :], turn(parts[0][f], GROUP))
+            value_f = (value[f] - before) * lane_growth
+            hrhs[f, pl.ds(start, 8), :] = value_f
+            hya[f, pl.ds(start, 8), :] = (weights[0] * q) * lane_sums(value_f)
+
+    def sweep(weight, old, hold, new, hnew, final):
+        first = MAIN if final else ROW0
+
+        @pl.loop(0, rows // 8 if final else blocks)
+        def _(t):
+            start = first + 8 * t
+            seam = seam_of(hold, start)
+            ends = [jnp.zeros((8, LANES), jnp.float32)] * fields
+            sums = [jnp.zeros((8, LANES), jnp.float32)] * fields
+            for n in range(total):
+                load = lambda f, d: old[n, f, pl.ds(start + d, 8), :]
+                parts = around(load, main_sides(seam, n))
+                value = off_diagonal(*parts)
+                for f in range(fields):
+                    if not final:
+                        ends[f] = jnp.where(step == n, turn(parts[0][f], GROUP * n), ends[f])
+                    sums[f] = sums[f] + (value[f] + rhs[n, f, pl.ds(start, 8), :])
+                    new[n, f, pl.ds(start, 8), :] = sums[f]
+            extra = [wrap * sums[f] for f in range(fields)]
+            for n in range(total):
+                for f in range(fields):
+                    at = (n, f, pl.ds(start, 8), slice(None))
+                    value_f = (1.0 - weight) * old[at] + (weight * q) * (new[at] + extra[f])
+                    if final:
+                        value_f = state[n + 1, f, pl.ds(start, 8), :] - value_f * q**n
+                    new[at] = value_f
+            if not final:
+                load = lambda f, d: hold[f, pl.ds(start + d, 8), :]
+                parts = around(load, side_sides(ends))
+                value = off_diagonal(*parts)
+                for f in range(fields):
+                    total_f = lane_sums(value[f] + hrhs[f, pl.ds(start, 8), :])
+                    hnew[f, pl.ds(start, 8), :] = (1.0 - weight) * parts[0][f] + (weight * q) * total_f
+
+    buffers = [(ya, hya), (yb, hyb)]
+    for m in range(1, SWEEPS):
+        (old, hold), (new, hnew) = buffers[(m + 1) % 2], buffers[m % 2]
+        sweep(weights[m], old, hold, new, hnew, m == SWEEPS - 1)
+    result = buffers[(SWEEPS - 1) % 2][0]
+    for b in range(count):
+        for i in range(steps_dev):
+            n = steps_dev * (me ^ b) + i
+            for f in range(fields):
+                at = (i * fields + f) * rows
+                outs[b][at : at + rows, :] = result[n, f, body, :]
+
+
+def unpack_kernel(count, *refs):
+    pieces, out = refs[:count], refs[count]
+    steps_dev, fields, rows, _ = out.shape
+    me = lax.axis_index("tm")
+    for b in range(count):
+        here = tile_at(me ^ b)
+        for i in range(steps_dev):
+            for f in range(fields):
+                at = (i * fields + f) * rows
+                out[i, f, :, here] = pieces[b][at : at + rows, :]
+
+
+def call(kernel, out_shapes, operands, scratch=()):
+    whole = pl.BlockSpec(memory_space=pltpu.VMEM)
+    shapes = [jax.ShapeDtypeStruct(shape, jnp.float32) for shape in out_shapes]
+    moved = 4 * sum(math.prod(x.shape) for x in list(shapes) + list(operands))
+    return pl.pallas_call(
+        kernel,
+        out_shape=shapes,
+        in_specs=[whole] * len(operands),
+        out_specs=[whole] * len(shapes),
+        scratch_shapes=[pltpu.VMEM(shape, jnp.float32) for shape in scratch],
+        compiler_params=pltpu.CompilerParams(vmem_limit_bytes=VMEM_BYTES),
+        cost_estimate=pl.CostEstimate(flops=moved, bytes_accessed=moved, transcendentals=0),
+    )(*operands)
+
+
+def exchange(pieces):
+    count = len(pieces)
+    found = list(pieces)
+    for b in reversed(range(1, count)):
+        found[b] = lax.ppermute(pieces[b], "tm", [(k, k ^ b) for k in range(count)])
+    return found
+
+
+def fast_on_device(state, initial):
+    steps_dev, fields, rows, columns = state.shape
+    count = lax.axis_size("tm")
+    bands = lax.axis_size("space")
+    total = steps_dev * count
+    main = steps_dev * fields * rows
+    words = -(-fields * rows // 8 // count)
+    pieces = call(
+        functools.partial(pack_kernel, count), [(main + 8 * words, LANES)] * count, [state]
+    )
+    pieces = exchange(pieces)
+    edge_rows = -(-HALO * fields * (total + 3) // 8) * 8
+    up, down, side, side_initial = call(
+        functools.partial(edge_kernel, count, steps_dev),
+        [(edge_rows, LANES)] * 2 + [(fields, rows, LANES)] * 2,
+        pieces + [initial],
+    )
+    above = lax.ppermute(down, "space", [(i, (i + 1) % bands) for i in range(bands)])
+    below = lax.ppermute(up, "space", [((i + 1) % bands, i) for i in range(bands)])
+    tall = rows + 2 * HALO + 2 * ROW0
+    results = call(
+        functools.partial(solve_kernel, count, steps_dev),
+        [(main, LANES)] * count,
+        pieces + [initial, side, side_initial, above, below],
+        [(total + 1, fields, tall, LANES)]
+        + [(total, fields, tall, LANES)] * 3
+        + [(fields, tall, LANES)] * 5,
+    )
+    results = exchange(results)
+    (updated,) = call(functools.partial(unpack_kernel, count), [state.shape], results)
+    return updated
+
+
+def choose(state, initial):
+    if fits_fast_plan(state, lax.axis_size("tm")):
+        return fast_on_device(state, initial)
+    return on_device(state, initial)
+
+
 def solution(mesh):
     in_specs = (P("tm", None, "space", None), P(None, "space", None))
     out_specs = P("tm", None, "space", None)
     return jax.shard_map(
-        on_device, mesh=mesh, in_specs=in_specs, out_specs=out_specs, check_vma=False
-    )
+        choose, mesh=mesh, in_specs=in_specs, out_specs=out_specs, check_vma=False
+    )

time: 532 us -> 70.3 us (0.13); the launches traced: 524 us -> 69 us
  local copies, waits for them, and re-layouts: 357 us -> 1.14 us
  other arithmetic: 46.3 us -> 0 us
  waiting for transfers between devices: 62.3 us -> 25.2 us
  blocking collectives: 29.2 us -> 0 us
  Pallas kernels: 0 us -> 14.6 us
    unnamed x12 -> x4, local copies, waits for them, and re-layouts: 231 us -> 1.14 us
    all_to_all x3 -> x0, waiting for transfers between devices: 57.3 us -> none  [the longest x1 19.7 us: on_device(): lax.all_to_all(flat_solution, 'tm', split_axis=3, concat_axis=1, tiled=True)]
    all_to_all x7 -> x0, local copies, waits for them, and re-layouts: 55.7 us -> none  [the longest x4 28.2 us: on_device(): lax.all_to_all(residual.reshape(steps_dev, fields, band_rows * columns),...]
    add x1 -> x0, local copies, waits for them, and re-layouts: 29.3 us -> none  [on_device(): iterate = iterate + weights[sweep] * pair_apply(jacobi, banded - applied)]
    all_to_all x1 -> x0, blocking collectives: 29.2 us -> none  [on_device(): lax.all_to_all(all_steps, 'tm', split_axis=0, concat_axis=2, tiled=True)]
    sub x12 -> x0, other arithmetic: 23.2 us -> none  [the longest x7 19.5 us: pair_apply(): factor[0] * values[0] - factor[1] * values[1]]
    reshape x3 -> x0, local copies, waits for them, and re-layouts: 23 us -> none  [the longest x1 22.5 us: on_device(): residual.reshape(steps_dev, fields, band_rows * columns)]
    ppermute x9 -> x16, waiting for transfers between devices: 4.99 us -> 25.2 us  [the longest x14 22.3 us: exchange(): found[b] = lax.ppermute(pieces[b], 'tm', [(k, k ^ b) for k in range(count)])]
  transfers between devices with their start and end apart: 12 -> 16, of which waited for: 4 -> 5; matrix products, arithmetic and copies ran while one was open for 4% -> 0% of each run, Pallas kernels for 0% -> 0%
where the time goes in v1:
time: 70.3 us; the launch traced here: 69 us
  starting transfers between devices  28.1 us (40%)
  waiting for transfers between devices  25.2 us (36%)
  Pallas kernels  14.6 us (21%)
  local copies, waits for them, and re-layouts  1.14 us (2%)
    ppermute x14, starting transfers between devices, exchange(): found[b] = lax.ppermute(pieces[b], 'tm', [(k, k ^ b) for k in range(count)])  26.3 us
    ppermute x14, waiting for transfers between devices, exchange(): found[b] = lax.ppermute(pieces[b], 'tm', [(k, k ^ b) for k in range(count)])  22.3 us
    pallas_call x4, Pallas kernels, call(): pl.pallas_call(kernel, out_shape=shapes, in_specs=[whole] * len(operands)...  14.6 us
    ppermute x1, waiting for transfers between devices, fast_on_device(): lax.ppermute(down, 'space', [(i, (i + 1) % bands) for i in range(bands)])  2.51 us
    ppermute x1, starting transfers between devices, fast_on_device(): lax.ppermute(up, 'space', [((i + 1) % bands, i) for i in range(bands)])  1.73 us
  transfers between devices with their start and end apart: 16, of which 5 were waited for; matrix products, arithmetic and copies ran while one was open for 0% of the time, Pallas kernels for 0%

profile of v1, /device:TPU:0, one launch (start us, length us, event | category | flops | bytes accessed | tf_op | source)
XLA Modules:
  0.0 69.0 jit_solution(1872268451252586447)
XLA Ops:
  0.0 1.1 %copy-done.1 = f32[2,3,32,1024]{3,2,1,0:T(8,128)S(1)} copy-done((f32[2,3,32,1024]{3,2,1,0:T(8,128)S(1)}, f32[2,3,32,1024]{3,2,1,0:T(8,128)}, u32[]{:S(2)}) %copy-start.1) | copy-done | bytes 786456
  1.1 0.4 shard_map.28
  1.5 3.0 %collective-permute-start = (f32[208,128]{1,0:T(8,128)S(1)}, f32[208,128]{1,0:T(8,128)S(1)}, u32[]{:S(2)}, u32[]{:S(2)}) collective-permute-start(f32[208,128]{1,0:T(8,128)S(1)} %get-tuple-element.26), channel_id=1, source_target_pairs={{0,4},{4,0},{8,12},{12,8},{16,20},{20,16},{24,28},{28,24},{1,5},{5... | collective-permute-start | bytes 319496 | tf_op jit(solution)/shard_map/ppermute | solution.py:570
  4.5 1.6 %collective-permute-start.1 = (f32[208,128]{1,0:T(8,128)S(1)}, f32[208,128]{1,0:T(8,128)S(1)}, u32[]{:S(2)}, u32[]{:S(2)}) collective-permute-start(f32[208,128]{1,0:T(8,128)S(1)} %get-tuple-element.27), channel_id=1, source_target_pairs={{0,8},{4,12},{8,0},{12,4},{16,24},{20,28},{24,16},{28,20},{1,9},{5... | collective-permute-start | bytes 319496 | tf_op jit(solution)/shard_map/ppermute | solution.py:570
  6.1 0.0 collective-permute-start.2
  6.1 3.0 %collective-permute-start.3 = (f32[208,128]{1,0:T(8,128)S(1)}, f32[208,128]{1,0:T(8,128)S(1)}, u32[]{:S(2)}, u32[]{:S(2)}) collective-permute-start(f32[208,128]{1,0:T(8,128)S(1)} %get-tuple-element.29), channel_id=1, source_target_pairs={{0,16},{4,20},{8,24},{12,28},{16,0},{20,4},{24,8},{28,12},{1,17},{... | collective-permute-start | bytes 319496 | tf_op jit(solution)/shard_map/ppermute | solution.py:570
  9.1 1.3 %collective-permute-start.4 = (f32[208,128]{1,0:T(8,128)S(1)}, f32[208,128]{1,0:T(8,128)S(1)}, u32[]{:S(2)}, u32[]{:S(2)}) collective-permute-start(f32[208,128]{1,0:T(8,128)S(1)} %get-tuple-element.30), channel_id=1, source_target_pairs={{0,20},{4,16},{8,28},{12,24},{16,4},{20,0},{24,12},{28,8},{1,21},{... | collective-permute-start | bytes 319496 | tf_op jit(solution)/shard_map/ppermute | solution.py:570
  10.3 0.0 collective-permute-done.refs_1_
  10.3 3.6 %collective-permute-start.5 = (f32[208,128]{1,0:T(8,128)S(1)}, f32[208,128]{1,0:T(8,128)S(1)}, u32[]{:S(2)}, u32[]{:S(2)}) collective-permute-start(f32[208,128]{1,0:T(8,128)S(1)} %get-tuple-element.31), channel_id=1, source_target_pairs={{0,24},{4,28},{8,16},{12,20},{16,8},{20,12},{24,0},{28,4},{1,25},{... | collective-permute-start | bytes 319496 | tf_op jit(solution)/shard_map/ppermute | solution.py:570
  13.9 0.0 collective-permute-done.1.refs_2_
  14.0 0.0 collective-permute-start.6
  14.0 0.0 collective-permute-done.2.refs_3_
  14.0 0.1 collective-permute-done.3.refs_4_
  14.1 11.2 %collective-permute-done.4.refs_5_ = f32[208,128]{1,0:T(8,128)S(1)} collective-permute-done((f32[208,128]{1,0:T(8,128)S(1)}, f32[208,128]{1,0:T(8,128)S(1)}, u32[]{:S(2)}, u32[]{:S(2)}) %collective-permute-start.4) | collective-permute-done | bytes 106528 | tf_op jit(solution)/shard_map/ppermute | solution.py:570
  25.3 0.0 collective-permute-done.5.refs_6_
  25.3 0.0 collective-permute-done.6.refs_7_
  25.3 0.2 shard_map.29
  25.5 0.1 collective-permute-start.7
  25.6 1.7 %collective-permute-start.8 = (f32[232,128]{1,0:T(8,128)S(1)}, f32[232,128]{1,0:T(8,128)S(1)}, u32[]{:S(2)}, u32[]{:S(2)}) collective-permute-start(f32[232,128]{1,0:T(8,128)S(1)} %get-tuple-element.36), channel_id=1, source_target_pairs={{1,0},{2,1},{3,2},{0,3},{5,4},{6,5},{7,6},{4,7},{9,8},{10,9},{11,1... | collective-permute-start | bytes 356360 | tf_op jit(solution)/shard_map/ppermute | solution.py:592
  27.3 2.5 %collective-permute-done.7.refs_11_ = f32[232,128]{1,0:T(8,128)S(1)} collective-permute-done((f32[232,128]{1,0:T(8,128)S(1)}, f32[232,128]{1,0:T(8,128)S(1)}, u32[]{:S(2)}, u32[]{:S(2)}) %collective-permute-start.7) | collective-permute-done | bytes 118816 | tf_op jit(solution)/shard_map/ppermute | solution.py:591
  29.8 0.3 collective-permute-done.8.refs_12_
  30.1 13.0 %shard_map.30 = (f32[192,128]{1,0:T(8,128)S(1)}, f32[192,128]{1,0:T(8,128)S(1)}, f32[192,128]{1,0:T(8,128)S(1)}, f32[192,128]{1,0:T(8,128)S(1)}, f32[192,128]{1,...) custom-call(f32[208,128]{1,0:T(8,128)S(1)} %get-tuple-element.25.refs_0_, ...), custom_call_target="tpu_custom_call" | custom-call | flops 2367488 | bytes 2367488 | tf_op jit(solution)/shard_map/pallas_call | solution.py:555
  43.1 1.0 %collective-permute-start.9 = (f32[192,128]{1,0:T(8,128)S(1)}, f32[192,128]{1,0:T(8,128)S(1)}, u32[]{:S(2)}, u32[]{:S(2)}) collective-permute-start(f32[192,128]{1,0:T(8,128)S(1)} %get-tuple-element.38), channel_id=1, source_target_pairs={{0,4},{4,0},{8,12},{12,8},{16,20},{20,16},{24,28},{28,24},{1,5},{5... | collective-permute-start | bytes 294920 | tf_op jit(solution)/shard_map/ppermute | solution.py:570
  44.1 3.9 %collective-permute-start.10 = (f32[192,128]{1,0:T(8,128)S(1)}, f32[192,128]{1,0:T(8,128)S(1)}, u32[]{:S(2)}, u32[]{:S(2)}) collective-permute-start(f32[192,128]{1,0:T(8,128)S(1)} %get-tuple-element.39), channel_id=1, source_target_pairs={{0,8},{4,12},{8,0},{12,4},{16,24},{20,28},{24,16},{28,20},{1,9},{5... | collective-permute-start | bytes 294920 | tf_op jit(solution)/shard_map/ppermute | solution.py:570
  48.1 0.9 %collective-permute-start.11 = (f32[192,128]{1,0:T(8,128)S(1)}, f32[192,128]{1,0:T(8,128)S(1)}, u32[]{:S(2)}, u32[]{:S(2)}) collective-permute-start(f32[192,128]{1,0:T(8,128)S(1)} %get-tuple-element.40), channel_id=1, source_target_pairs={{0,12},{4,8},{8,4},{12,0},{16,28},{20,24},{24,20},{28,16},{1,13},{... | collective-permute-start | bytes 294920 | tf_op jit(solution)/shard_map/ppermute | solution.py:570
  48.9 3.3 %collective-permute-start.12 = (f32[192,128]{1,0:T(8,128)S(1)}, f32[192,128]{1,0:T(8,128)S(1)}, u32[]{:S(2)}, u32[]{:S(2)}) collective-permute-start(f32[192,128]{1,0:T(8,128)S(1)} %get-tuple-element.41), channel_id=1, source_target_pairs={{0,16},{4,20},{8,24},{12,28},{16,0},{20,4},{24,8},{28,12},{1,17},{... | collective-permute-start | bytes 294920 | tf_op jit(solution)/shard_map/ppermute | solution.py:570
  52.2 2.4 %collective-permute-start.14 = (f32[192,128]{1,0:T(8,128)S(1)}, f32[192,128]{1,0:T(8,128)S(1)}, u32[]{:S(2)}, u32[]{:S(2)}) collective-permute-start(f32[192,128]{1,0:T(8,128)S(1)} %get-tuple-element.43), channel_id=1, source_target_pairs={{0,24},{4,28},{8,16},{12,20},{16,8},{20,12},{24,0},{28,4},{1,25},{... | collective-permute-start | bytes 294920 | tf_op jit(solution)/shard_map/ppermute | solution.py:570
  54.6 2.4 %collective-permute-start.15 = (f32[192,128]{1,0:T(8,128)S(1)}, f32[192,128]{1,0:T(8,128)S(1)}, u32[]{:S(2)}, u32[]{:S(2)}) collective-permute-start(f32[192,128]{1,0:T(8,128)S(1)} %get-tuple-element.44), channel_id=1, source_target_pairs={{0,28},{4,24},{8,20},{12,16},{16,12},{20,8},{24,4},{28,0},{1,29},{... | collective-permute-start | bytes 294920 | tf_op jit(solution)/shard_map/ppermute | solution.py:570
  57.0 0.0 collective-permute-done.11.refs_3_
  57.0 0.0 collective-permute-done.12.refs_4_
  57.0 11.0 %collective-permute-done.13.refs_5_ = f32[192,128]{1,0:T(8,128)S(1)} collective-permute-done((f32[192,128]{1,0:T(8,128)S(1)}, f32[192,128]{1,0:T(8,128)S(1)}, u32[]{:S(2)}, u32[]{:S(2)}) %collective-permute-start.13) | collective-permute-done | bytes 98336 | tf_op jit(solution)/shard_map/ppermute | solution.py:570
  68.0 1.0 %shard_map.31 = f32[2,3,32,1024]{3,2,1,0:T(8,128)} custom-call(f32[192,128]{1,0:T(8,128)S(1)} %get-tuple-element.37.refs_0_, f32[192,128]{1,0:T(8,128)S(1)} %collective-permute-done.9.refs_1_, f32[192,128]{1,0:T(8,128)S(1)} %collective-permute-done.10.refs_2_, f32[192,128]{1,0:T(8,128)S(1)} %collective-permute-done.11.refs_3_, ...), custom_call_target="tpu_custom_call" | custom-call | flops 1572864 | bytes 1572864 | tf_op jit(solution)/shard_map/pallas_call | solution.py:555
  (8 shorter events, 0.0 us)
Async XLA Ops:
  0.0 1.1 %copy-start.1 = (f32[2,3,32,1024]{3,2,1,0:T(8,128)S(1)}, f32[2,3,32,1024]{3,2,1,0:T(8,128)}, u32[]{:S(2)}) copy-start(f32[2,3,32,1024]{3,2,1,0:T(8,128)} %state_ref.1) | copy-start | bytes 2359300
  1.1 24.1 %copy-start = (f32[3,32,1024]{2,1,0:T(8,128)S(1)}, f32[3,32,1024]{2,1,0:T(8,128)}, u32[]{:S(2)}) copy-start(f32[3,32,1024]{2,1,0:T(8,128)} %refs_8_.3) | copy-start | bytes 1179652
  1.5 8.8 %collective-permute-start = (f32[208,128]{1,0:T(8,128)S(1)}, f32[208,128]{1,0:T(8,128)S(1)}, u32[]{:S(2)}, u32[]{:S(2)}) collective-permute-start(f32[208,128]{1,0:T(8,128)S(1)} %get-tuple-element.26), channel_id=1, source_target_pairs={{0,4},{4,0},{8,12},{12,8},{16,20},{20,16},{24,28},{28,24},{1,5},{5... | collective-permute-start | bytes 319496 | tf_op jit(solution)/shard_map/ppermute | solution.py:570
  4.5 9.5 %collective-permute-start.1 = (f32[208,128]{1,0:T(8,128)S(1)}, f32[208,128]{1,0:T(8,128)S(1)}, u32[]{:S(2)}, u32[]{:S(2)}) collective-permute-start(f32[208,128]{1,0:T(8,128)S(1)} %get-tuple-element.27), channel_id=1, source_target_pairs={{0,8},{4,12},{8,0},{12,4},{16,24},{20,28},{24,16},{28,20},{1,9},{5... | collective-permute-start | bytes 319496 | tf_op jit(solution)/shard_map/ppermute | solution.py:570
  6.1 7.9 %collective-permute-start.2 = (f32[208,128]{1,0:T(8,128)S(1)}, f32[208,128]{1,0:T(8,128)S(1)}, u32[]{:S(2)}, u32[]{:S(2)}) collective-permute-start(f32[208,128]{1,0:T(8,128)S(1)} %get-tuple-element.28), channel_id=1, source_target_pairs={{0,12},{4,8},{8,4},{12,0},{16,28},{20,24},{24,20},{28,16},{1,13},{... | collective-permute-start | bytes 319496 | tf_op jit(solution)/shard_map/ppermute | solution.py:570
  6.1 8.0 %collective-permute-start.3 = (f32[208,128]{1,0:T(8,128)S(1)}, f32[208,128]{1,0:T(8,128)S(1)}, u32[]{:S(2)}, u32[]{:S(2)}) collective-permute-start(f32[208,128]{1,0:T(8,128)S(1)} %get-tuple-element.29), channel_id=1, source_target_pairs={{0,16},{4,20},{8,24},{12,28},{16,0},{20,4},{24,8},{28,12},{1,17},{... | collective-permute-start | bytes 319496 | tf_op jit(solution)/shard_map/ppermute | solution.py:570
  9.1 16.2 %collective-permute-start.4 = (f32[208,128]{1,0:T(8,128)S(1)}, f32[208,128]{1,0:T(8,128)S(1)}, u32[]{:S(2)}, u32[]{:S(2)}) collective-permute-start(f32[208,128]{1,0:T(8,128)S(1)} %get-tuple-element.30), channel_id=1, source_target_pairs={{0,20},{4,16},{8,28},{12,24},{16,4},{20,0},{24,12},{28,8},{1,21},{... | collective-permute-start | bytes 319496 | tf_op jit(solution)/shard_map/ppermute | solution.py:570
  10.3 14.9 %collective-permute-start.5 = (f32[208,128]{1,0:T(8,128)S(1)}, f32[208,128]{1,0:T(8,128)S(1)}, u32[]{:S(2)}, u32[]{:S(2)}) collective-permute-start(f32[208,128]{1,0:T(8,128)S(1)} %get-tuple-element.31), channel_id=1, source_target_pairs={{0,24},{4,28},{8,16},{12,20},{16,8},{20,12},{24,0},{28,4},{1,25},{... | collective-permute-start | bytes 319496 | tf_op jit(solution)/shard_map/ppermute | solution.py:570
  14.0 11.3 %collective-permute-start.6 = (f32[208,128]{1,0:T(8,128)S(1)}, f32[208,128]{1,0:T(8,128)S(1)}, u32[]{:S(2)}, u32[]{:S(2)}) collective-permute-start(f32[208,128]{1,0:T(8,128)S(1)} %get-tuple-element.32), channel_id=1, source_target_pairs={{0,28},{4,24},{8,20},{12,16},{16,12},{20,8},{24,4},{28,0},{1,29},{... | collective-permute-start | bytes 319496 | tf_op jit(solution)/shard_map/ppermute | solution.py:570
  25.5 4.3 %collective-permute-start.7 = (f32[232,128]{1,0:T(8,128)S(1)}, f32[232,128]{1,0:T(8,128)S(1)}, u32[]{:S(2)}, u32[]{:S(2)}) collective-permute-start(f32[232,128]{1,0:T(8,128)S(1)} %get-tuple-element.35), channel_id=1, source_target_pairs={{0,1},{1,2},{2,3},{3,0},{4,5},{5,6},{6,7},{7,4},{8,9},{9,10},{10,1... | collective-permute-start | bytes 356360 | tf_op jit(solution)/shard_map/ppermute | solution.py:591
  25.6 4.6 %collective-permute-start.8 = (f32[232,128]{1,0:T(8,128)S(1)}, f32[232,128]{1,0:T(8,128)S(1)}, u32[]{:S(2)}, u32[]{:S(2)}) collective-permute-start(f32[232,128]{1,0:T(8,128)S(1)} %get-tuple-element.36), channel_id=1, source_target_pairs={{1,0},{2,1},{3,2},{0,3},{5,4},{6,5},{7,6},{4,7},{9,8},{10,9},{11,1... | collective-permute-start | bytes 356360 | tf_op jit(solution)/shard_map/ppermute | solution.py:592
  43.1 9.1 %collective-permute-start.9 = (f32[192,128]{1,0:T(8,128)S(1)}, f32[192,128]{1,0:T(8,128)S(1)}, u32[]{:S(2)}, u32[]{:S(2)}) collective-permute-start(f32[192,128]{1,0:T(8,128)S(1)} %get-tuple-element.38), channel_id=1, source_target_pairs={{0,4},{4,0},{8,12},{12,8},{16,20},{20,16},{24,28},{28,24},{1,5},{5... | collective-permute-start | bytes 294920 | tf_op jit(solution)/shard_map/ppermute | solution.py:570
  44.1 10.5 %collective-permute-start.10 = (f32[192,128]{1,0:T(8,128)S(1)}, f32[192,128]{1,0:T(8,128)S(1)}, u32[]{:S(2)}, u32[]{:S(2)}) collective-permute-start(f32[192,128]{1,0:T(8,128)S(1)} %get-tuple-element.39), channel_id=1, source_target_pairs={{0,8},{4,12},{8,0},{12,4},{16,24},{20,28},{24,16},{28,20},{1,9},{5... | collective-permute-start | bytes 294920 | tf_op jit(solution)/shard_map/ppermute | solution.py:570
  48.1 8.9 %collective-permute-start.11 = (f32[192,128]{1,0:T(8,128)S(1)}, f32[192,128]{1,0:T(8,128)S(1)}, u32[]{:S(2)}, u32[]{:S(2)}) collective-permute-start(f32[192,128]{1,0:T(8,128)S(1)} %get-tuple-element.40), channel_id=1, source_target_pairs={{0,12},{4,8},{8,4},{12,0},{16,28},{20,24},{24,20},{28,16},{1,13},{... | collective-permute-start | bytes 294920 | tf_op jit(solution)/shard_map/ppermute | solution.py:570
  48.9 8.0 %collective-permute-start.12 = (f32[192,128]{1,0:T(8,128)S(1)}, f32[192,128]{1,0:T(8,128)S(1)}, u32[]{:S(2)}, u32[]{:S(2)}) collective-permute-start(f32[192,128]{1,0:T(8,128)S(1)} %get-tuple-element.41), channel_id=1, source_target_pairs={{0,16},{4,20},{8,24},{12,28},{16,0},{20,4},{24,8},{28,12},{1,17},{... | collective-permute-start | bytes 294920 | tf_op jit(solution)/shard_map/ppermute | solution.py:570
  52.2 15.8 %collective-permute-start.13 = (f32[192,128]{1,0:T(8,128)S(1)}, f32[192,128]{1,0:T(8,128)S(1)}, u32[]{:S(2)}, u32[]{:S(2)}) collective-permute-start(f32[192,128]{1,0:T(8,128)S(1)} %get-tuple-element.42), channel_id=1, source_target_pairs={{0,20},{4,16},{8,28},{12,24},{16,4},{20,0},{24,12},{28,8},{1,21},{... | collective-permute-start | bytes 294920 | tf_op jit(solution)/shard_map/ppermute | solution.py:570
  52.2 15.8 %collective-permute-start.14 = (f32[192,128]{1,0:T(8,128)S(1)}, f32[192,128]{1,0:T(8,128)S(1)}, u32[]{:S(2)}, u32[]{:S(2)}) collective-permute-start(f32[192,128]{1,0:T(8,128)S(1)} %get-tuple-element.43), channel_id=1, source_target_pairs={{0,24},{4,28},{8,16},{12,20},{16,8},{20,12},{24,0},{28,4},{1,25},{... | collective-permute-start | bytes 294920 | tf_op jit(solution)/shard_map/ppermute | solution.py:570
  54.6 13.4 %collective-permute-start.15 = (f32[192,128]{1,0:T(8,128)S(1)}, f32[192,128]{1,0:T(8,128)S(1)}, u32[]{:S(2)}, u32[]{:S(2)}) collective-permute-start(f32[192,128]{1,0:T(8,128)S(1)} %get-tuple-element.44), channel_id=1, source_target_pairs={{0,28},{4,24},{8,20},{12,16},{16,12},{20,8},{24,4},{28,0},{1,29},{... | collective-permute-start | bytes 294920 | tf_op jit(solution)/shard_map/ppermute | solution.py:570

commit v2 on v1

--- a/solution.py
+++ b/solution.py
@@ -379,14 +379,13 @@
     pieces, initial_ref = refs[:count], refs[count]
     side_in, side_initial_in, above, below = refs[count + 1 : count + 5]
     outs = refs[count + 5 : 2 * count + 5]
-    state, rhs, ya, yb, hstate, hbefore, hrhs, hya, hyb = refs[2 * count + 5 :]
+    state, rhs, ya, yb, hstate, hbefore, hrhs, hya, hyb, ends, seams = refs[2 * count + 5 :]
     fields, rows, _ = initial_ref.shape
     total = count * steps_dev
     me = lax.axis_index("tm")
     lane = lanes()
     step = step_of_lane(lane)
     is_first, is_last = lane == 0, lane == LANES - 1
-    after_seam, before_seam = (lane & (GROUP - 1)) == 0, (lane & (GROUP - 1)) == GROUP - 1
     q = 1.0 / SHIFT
     wrap = circulant_alpha * q**total
     wrap = wrap / (1.0 - wrap)
@@ -432,62 +431,79 @@
 
         return halves
 
-    def side_sides(ends):
-        def halves(own):
-            east = [jnp.where(before_seam, turn(ends[f], -1), turn(own[f], -1)) for f in range(fields)]
-            west = [jnp.where(after_seam, turn(ends[f], 1), turn(own[f], 1)) for f in range(fields)]
-            return east, west
-
-        return halves
-
-    def seam_of(held, start):
-        values = [held[f, pl.ds(start, 8), :] for f in range(fields)]
-        return [jnp.where(after_seam, turn(v, 1), turn(v, -1)) for v in values]
-
-    def lane_sums(value):
-        reach = 1
-        while reach < total:
-            value = value + jnp.where(step >= reach, turn(value, GROUP * reach), 0.0)
-            reach *= 2
-        last = jnp.where(step == total - 1, value, 0.0)
-        reach = 1
-        while reach < total:
-            last = last + turn(last, -GROUP * reach)
-            reach *= 2
-        return value + wrap * last
-
-    lane_growth = jnp.exp(step.astype(jnp.float32) * math.log(SHIFT))
     blocks = (rows + 2 * HALO) // 8
+    whole = slice(ROW0, ROW0 + 8 * blocks)
+    wide = lax.broadcasted_iota(jnp.int32, (8 * blocks, LANES), 1)
+    wide_step = step_of_lane(wide)
+    wide_after = (wide & (GROUP - 1)) == 0
+    wide_before = (wide & (GROUP - 1)) == GROUP - 1
+    source = lax.broadcasted_iota(jnp.int32, (LANES, LANES), 0)
+    target = lax.broadcasted_iota(jnp.int32, (LANES, LANES), 1)
+    same = ((source - target) & (GROUP - 1)) == 0
+    running = jnp.where(
+        same, jnp.where(step_of_lane(source) <= step_of_lane(target), 1.0 + wrap, wrap), 0.0
+    ).astype(jnp.float32)
+
+    def side_parts(held):
+        own, north, south = (
+            [held[f, ROW0 + d : ROW0 + d + 8 * blocks, :] for f in range(fields)] for d in (0, -1, 1)
+        )
+        last = [ends[f, whole, :] for f in range(fields)]
+        east = [jnp.where(wide_before, turn(last[f], -1), turn(own[f], -1)) for f in range(fields)]
+        west = [jnp.where(wide_after, turn(last[f], 1), turn(own[f], 1)) for f in range(fields)]
+        return own, east, west, north, south
+
+    def running_sums(values):
+        tall_sums = jnp.dot(
+            jnp.concatenate(values, axis=0),
+            running,
+            precision=highest,
+            preferred_element_type=jnp.float32,
+        )
+        return [tall_sums[8 * blocks * f : 8 * blocks * (f + 1), :] for f in range(fields)]
+
+    def set_seam(values):
+        for f in range(fields):
+            seams[f, whole, :] = jnp.where(wide_after, turn(values[f], 1), turn(values[f], -1))
+
+    set_seam([hstate[f, whole, :] for f in range(fields)])
 
     @pl.loop(0, blocks)
     def _(t):
         start = ROW0 + 8 * t
-        seam = seam_of(hstate, start)
-        ends = [jnp.zeros((8, LANES), jnp.float32)] * fields
+        seam = [seams[f, pl.ds(start, 8), :] for f in range(fields)]
+        last = [jnp.zeros((8, LANES), jnp.float32)] * fields
         sums = [jnp.zeros((8, LANES), jnp.float32)] * fields
         for n in range(total):
             load = lambda f, d: state[n + 1, f, pl.ds(start + d, 8), :]
             parts = around(load, main_sides(seam, n))
             value = full_tendency(*parts)
             for f in range(fields):
-                ends[f] = jnp.where(step == n, turn(parts[0][f], GROUP * n), ends[f])
+                last[f] = jnp.where(step == n, turn(parts[0][f], GROUP * n), last[f])
                 value_f = (value[f] - state[n, f, pl.ds(start, 8), :]) * SHIFT**n
                 rhs[n, f, pl.ds(start, 8), :] = value_f
                 sums[f] = sums[f] + value_f
                 ya[n, f, pl.ds(start, 8), :] = sums[f]
+        for f in range(fields):
+            ends[f, pl.ds(start, 8), :] = last[f]
         extra = [wrap * sums[f] for f in range(fields)]
         for n in range(total):
             for f in range(fields):
                 at = (n, f, pl.ds(start, 8), slice(None))
                 ya[at] = (weights[0] * q) * (ya[at] + extra[f])
-        load = lambda f, d: hstate[f, pl.ds(start + d, 8), :]
-        parts = around(load, side_sides(ends))
-        value = full_tendency(*parts)
-        for f in range(fields):
-            before = jnp.where(step == 0, hbefore[f, pl.ds(start, 8), :], turn(parts[0][f], GROUP))
-            value_f = (value[f] - before) * lane_growth
-            hrhs[f, pl.ds(start, 8), :] = value_f
-            hya[f, pl.ds(start, 8), :] = (weights[0] * q) * lane_sums(value_f)
+
+    parts = side_parts(hstate)
+    value = full_tendency(*parts)
+    lane_growth = jnp.exp(wide_step.astype(jnp.float32) * math.log(SHIFT))
+    side_rhs = []
+    for f in range(fields):
+        before = jnp.where(wide_step == 0, hbefore[f, whole, :], turn(parts[0][f], GROUP))
+        side_rhs.append((value[f] - before) * lane_growth)
+        hrhs[f, whole, :] = side_rhs[f]
+    side_new = [(weights[0] * q) * x for x in running_sums(side_rhs)]
+    for f in range(fields):
+        hya[f, whole, :] = side_new[f]
+    set_seam(side_new)
 
     def sweep(weight, old, hold, new, hnew, final):
         first = MAIN if final else ROW0
@@ -495,8 +511,8 @@
         @pl.loop(0, rows // 8 if final else blocks)
         def _(t):
             start = first + 8 * t
-            seam = seam_of(hold, start)
-            ends = [jnp.zeros((8, LANES), jnp.float32)] * fields
+            seam = [seams[f, pl.ds(start, 8), :] for f in range(fields)]
+            last = [jnp.zeros((8, LANES), jnp.float32)] * fields
             sums = [jnp.zeros((8, LANES), jnp.float32)] * fields
             for n in range(total):
                 load = lambda f, d: old[n, f, pl.ds(start + d, 8), :]
@@ -504,9 +520,12 @@
                 value = off_diagonal(*parts)
                 for f in range(fields):
                     if not final:
-                        ends[f] = jnp.where(step == n, turn(parts[0][f], GROUP * n), ends[f])
+                        last[f] = jnp.where(step == n, turn(parts[0][f], GROUP * n), last[f])
                     sums[f] = sums[f] + (value[f] + rhs[n, f, pl.ds(start, 8), :])
                     new[n, f, pl.ds(start, 8), :] = sums[f]
+            if not final:
+                for f in range(fields):
+                    ends[f, pl.ds(start, 8), :] = last[f]
             extra = [wrap * sums[f] for f in range(fields)]
             for n in range(total):
                 for f in range(fields):
@@ -515,13 +534,17 @@
                     if final:
                         value_f = state[n + 1, f, pl.ds(start, 8), :] - value_f * q**n
                     new[at] = value_f
-            if not final:
-                load = lambda f, d: hold[f, pl.ds(start + d, 8), :]
-                parts = around(load, side_sides(ends))
-                value = off_diagonal(*parts)
-                for f in range(fields):
-                    total_f = lane_sums(value[f] + hrhs[f, pl.ds(start, 8), :])
-                    hnew[f, pl.ds(start, 8), :] = (1.0 - weight) * parts[0][f] + (weight * q) * total_f
+
+        if not final:
+            parts = side_parts(hold)
+            value = off_diagonal(*parts)
+            total_sums = running_sums([value[f] + hrhs[f, whole, :] for f in range(fields)])
+            side_next = [
+                (1.0 - weight) * parts[0][f] + (weight * q) * total_sums[f] for f in range(fields)
+            ]
+            for f in range(fields):
+                hnew[f, whole, :] = side_next[f]
+            set_seam(side_next)
 
     buffers = [(ya, hya), (yb, hyb)]
     for m in range(1, SWEEPS):
@@ -597,7 +620,7 @@
         pieces + [initial, side, side_initial, above, below],
         [(total + 1, fields, tall, LANES)]
         + [(total, fields, tall, LANES)] * 3
-        + [(fields, tall, LANES)] * 5,
+        + [(fields, tall, LANES)] * 7,
     )
     results = exchange(results)
     (updated,) = call(functools.partial(unpack_kernel, count), [state.shape], results)

time: 70.3 us -> 64.2 us (0.913)
  Pallas kernels: 14.6 us -> 8.53 us
    pallas_call x4, Pallas kernels: 14.6 us -> 8.53 us  [call(): pl.pallas_call(kernel, out_shape=shapes, in_specs=[whole] * len(operands)...]
where the time goes in v2:
time: 64.2 us; the launch traced here: 63 us
  starting transfers between devices  28.1 us (44%)
  waiting for transfers between devices  25.2 us (39%)
  Pallas kernels  8.53 us (13%)
  local copies, waits for them, and re-layouts  1.14 us (2%)
    ppermute x14, starting transfers between devices, exchange(): found[b] = lax.ppermute(pieces[b], 'tm', [(k, k ^ b) for k in range(count)])  26.3 us
    ppermute x14, waiting for transfers between devices, exchange(): found[b] = lax.ppermute(pieces[b], 'tm', [(k, k ^ b) for k in range(count)])  22.3 us
    pallas_call x4, Pallas kernels, call(): pl.pallas_call(kernel, out_shape=shapes, in_specs=[whole] * len(operands)...  8.53 us
    ppermute x1, waiting for transfers between devices, fast_on_device(): lax.ppermute(down, 'space', [(i, (i + 1) % bands) for i in range(bands)])  2.51 us
    ppermute x1, starting transfers between devices, fast_on_device(): lax.ppermute(up, 'space', [((i + 1) % bands, i) for i in range(bands)])  1.73 us
  transfers between devices with their start and end apart: 16, of which 5 were waited for; matrix products, arithmetic and copies ran while one was open for 0% of the time, Pallas kernels for 0%

profile of v2, /device:TPU:0, one launch (start us, length us, event | category | flops | bytes accessed | tf_op | source)
XLA Modules:
  0.0 63.0 jit_solution(14393753960388477044)
XLA Ops:
  0.0 1.1 %copy-done.1 = f32[2,3,32,1024]{3,2,1,0:T(8,128)S(1)} copy-done((f32[2,3,32,1024]{3,2,1,0:T(8,128)S(1)}, f32[2,3,32,1024]{3,2,1,0:T(8,128)}, u32[]{:S(2)}) %copy-start.1) | copy-done | bytes 786456
  1.1 0.4 shard_map.28
  1.5 3.0 %collective-permute-start = (f32[208,128]{1,0:T(8,128)S(1)}, f32[208,128]{1,0:T(8,128)S(1)}, u32[]{:S(2)}, u32[]{:S(2)}) collective-permute-start(f32[208,128]{1,0:T(8,128)S(1)} %get-tuple-element.26), channel_id=1, source_target_pairs={{0,4},{4,0},{8,12},{12,8},{16,20},{20,16},{24,28},{28,24},{1,5},{5... | collective-permute-start | bytes 319496 | tf_op jit(solution)/shard_map/ppermute | solution.py:593
  4.5 1.6 %collective-permute-start.1 = (f32[208,128]{1,0:T(8,128)S(1)}, f32[208,128]{1,0:T(8,128)S(1)}, u32[]{:S(2)}, u32[]{:S(2)}) collective-permute-start(f32[208,128]{1,0:T(8,128)S(1)} %get-tuple-element.27), channel_id=1, source_target_pairs={{0,8},{4,12},{8,0},{12,4},{16,24},{20,28},{24,16},{28,20},{1,9},{5... | collective-permute-start | bytes 319496 | tf_op jit(solution)/shard_map/ppermute | solution.py:593
  6.1 0.0 collective-permute-start.2
  6.1 3.0 %collective-permute-start.3 = (f32[208,128]{1,0:T(8,128)S(1)}, f32[208,128]{1,0:T(8,128)S(1)}, u32[]{:S(2)}, u32[]{:S(2)}) collective-permute-start(f32[208,128]{1,0:T(8,128)S(1)} %get-tuple-element.29), channel_id=1, source_target_pairs={{0,16},{4,20},{8,24},{12,28},{16,0},{20,4},{24,8},{28,12},{1,17},{... | collective-permute-start | bytes 319496 | tf_op jit(solution)/shard_map/ppermute | solution.py:593
  9.1 1.3 %collective-permute-start.4 = (f32[208,128]{1,0:T(8,128)S(1)}, f32[208,128]{1,0:T(8,128)S(1)}, u32[]{:S(2)}, u32[]{:S(2)}) collective-permute-start(f32[208,128]{1,0:T(8,128)S(1)} %get-tuple-element.30), channel_id=1, source_target_pairs={{0,20},{4,16},{8,28},{12,24},{16,4},{20,0},{24,12},{28,8},{1,21},{... | collective-permute-start | bytes 319496 | tf_op jit(solution)/shard_map/ppermute | solution.py:593
  10.3 3.6 %collective-permute-start.5 = (f32[208,128]{1,0:T(8,128)S(1)}, f32[208,128]{1,0:T(8,128)S(1)}, u32[]{:S(2)}, u32[]{:S(2)}) collective-permute-start(f32[208,128]{1,0:T(8,128)S(1)} %get-tuple-element.31), channel_id=1, source_target_pairs={{0,24},{4,28},{8,16},{12,20},{16,8},{20,12},{24,0},{28,4},{1,25},{... | collective-permute-start | bytes 319496 | tf_op jit(solution)/shard_map/ppermute | solution.py:593
  13.9 0.0 collective-permute-done.1.refs_2_
  14.0 0.0 collective-permute-start.6
  14.0 0.0 collective-permute-done.2.refs_3_
  14.0 0.1 collective-permute-done.3.refs_4_
  14.1 11.2 %collective-permute-done.4.refs_5_ = f32[208,128]{1,0:T(8,128)S(1)} collective-permute-done((f32[208,128]{1,0:T(8,128)S(1)}, f32[208,128]{1,0:T(8,128)S(1)}, u32[]{:S(2)}, u32[]{:S(2)}) %collective-permute-start.4) | collective-permute-done | bytes 106528 | tf_op jit(solution)/shard_map/ppermute | solution.py:593
  25.3 0.2 shard_map.29
  25.5 0.1 collective-permute-start.7
  25.6 1.7 %collective-permute-start.8 = (f32[232,128]{1,0:T(8,128)S(1)}, f32[232,128]{1,0:T(8,128)S(1)}, u32[]{:S(2)}, u32[]{:S(2)}) collective-permute-start(f32[232,128]{1,0:T(8,128)S(1)} %get-tuple-element.36), channel_id=1, source_target_pairs={{1,0},{2,1},{3,2},{0,3},{5,4},{6,5},{7,6},{4,7},{9,8},{10,9},{11,1... | collective-permute-start | bytes 356360 | tf_op jit(solution)/shard_map/ppermute | solution.py:615
  27.3 2.5 %collective-permute-done.7.refs_11_ = f32[232,128]{1,0:T(8,128)S(1)} collective-permute-done((f32[232,128]{1,0:T(8,128)S(1)}, f32[232,128]{1,0:T(8,128)S(1)}, u32[]{:S(2)}, u32[]{:S(2)}) %collective-permute-start.7) | collective-permute-done | bytes 118816 | tf_op jit(solution)/shard_map/ppermute | solution.py:614
  29.8 0.3 collective-permute-done.8.refs_12_
  30.1 7.0 %shard_map.30 = (f32[192,128]{1,0:T(8,128)S(1)}, f32[192,128]{1,0:T(8,128)S(1)}, f32[192,128]{1,0:T(8,128)S(1)}, f32[192,128]{1,0:T(8,128)S(1)}, f32[192,128]{1,...) custom-call(f32[208,128]{1,0:T(8,128)S(1)} %get-tuple-element.25.refs_0_, ...), custom_call_target="tpu_custom_call" | custom-call | flops 2367488 | bytes 2367488 | tf_op jit(solution)/shard_map/pallas_call | solution.py:578
  37.1 1.0 %collective-permute-start.9 = (f32[192,128]{1,0:T(8,128)S(1)}, f32[192,128]{1,0:T(8,128)S(1)}, u32[]{:S(2)}, u32[]{:S(2)}) collective-permute-start(f32[192,128]{1,0:T(8,128)S(1)} %get-tuple-element.38), channel_id=1, source_target_pairs={{0,4},{4,0},{8,12},{12,8},{16,20},{20,16},{24,28},{28,24},{1,5},{5... | collective-permute-start | bytes 294920 | tf_op jit(solution)/shard_map/ppermute | solution.py:593
  38.1 3.9 %collective-permute-start.10 = (f32[192,128]{1,0:T(8,128)S(1)}, f32[192,128]{1,0:T(8,128)S(1)}, u32[]{:S(2)}, u32[]{:S(2)}) collective-permute-start(f32[192,128]{1,0:T(8,128)S(1)} %get-tuple-element.39), channel_id=1, source_target_pairs={{0,8},{4,12},{8,0},{12,4},{16,24},{20,28},{24,16},{28,20},{1,9},{5... | collective-permute-start | bytes 294920 | tf_op jit(solution)/shard_map/ppermute | solution.py:593
  42.0 0.9 %collective-permute-start.11 = (f32[192,128]{1,0:T(8,128)S(1)}, f32[192,128]{1,0:T(8,128)S(1)}, u32[]{:S(2)}, u32[]{:S(2)}) collective-permute-start(f32[192,128]{1,0:T(8,128)S(1)} %get-tuple-element.40), channel_id=1, source_target_pairs={{0,12},{4,8},{8,4},{12,0},{16,28},{20,24},{24,20},{28,16},{1,13},{... | collective-permute-start | bytes 294920 | tf_op jit(solution)/shard_map/ppermute | solution.py:593
  42.9 3.3 %collective-permute-start.12 = (f32[192,128]{1,0:T(8,128)S(1)}, f32[192,128]{1,0:T(8,128)S(1)}, u32[]{:S(2)}, u32[]{:S(2)}) collective-permute-start(f32[192,128]{1,0:T(8,128)S(1)} %get-tuple-element.41), channel_id=1, source_target_pairs={{0,16},{4,20},{8,24},{12,28},{16,0},{20,4},{24,8},{28,12},{1,17},{... | collective-permute-start | bytes 294920 | tf_op jit(solution)/shard_map/ppermute | solution.py:593
  46.2 0.0 collective-permute-start.13
  46.2 0.0 collective-permute-done.9.refs_1_
  46.2 2.4 %collective-permute-start.14 = (f32[192,128]{1,0:T(8,128)S(1)}, f32[192,128]{1,0:T(8,128)S(1)}, u32[]{:S(2)}, u32[]{:S(2)}) collective-permute-start(f32[192,128]{1,0:T(8,128)S(1)} %get-tuple-element.43), channel_id=1, source_target_pairs={{0,24},{4,28},{8,16},{12,20},{16,8},{20,12},{24,0},{28,4},{1,25},{... | collective-permute-start | bytes 294920 | tf_op jit(solution)/shard_map/ppermute | solution.py:593
  48.6 0.0 collective-permute-done.10.refs_2_
  48.6 2.4 %collective-permute-start.15 = (f32[192,128]{1,0:T(8,128)S(1)}, f32[192,128]{1,0:T(8,128)S(1)}, u32[]{:S(2)}, u32[]{:S(2)}) collective-permute-start(f32[192,128]{1,0:T(8,128)S(1)} %get-tuple-element.44), channel_id=1, source_target_pairs={{0,28},{4,24},{8,20},{12,16},{16,12},{20,8},{24,4},{28,0},{1,29},{... | collective-permute-start | bytes 294920 | tf_op jit(solution)/shard_map/ppermute | solution.py:593
  50.9 0.0 collective-permute-done.11.refs_3_
  50.9 0.0 collective-permute-done.12.refs_4_
  50.9 11.0 %collective-permute-done.13.refs_5_ = f32[192,128]{1,0:T(8,128)S(1)} collective-permute-done((f32[192,128]{1,0:T(8,128)S(1)}, f32[192,128]{1,0:T(8,128)S(1)}, u32[]{:S(2)}, u32[]{:S(2)}) %collective-permute-start.13) | collective-permute-done | bytes 98336 | tf_op jit(solution)/shard_map/ppermute | solution.py:593
  62.0 1.0 %shard_map.31 = f32[2,3,32,1024]{3,2,1,0:T(8,128)} custom-call(f32[192,128]{1,0:T(8,128)S(1)} %get-tuple-element.37.refs_0_, f32[192,128]{1,0:T(8,128)S(1)} %collective-permute-done.9.refs_1_, f32[192,128]{1,0:T(8,128)S(1)} %collective-permute-done.10.refs_2_, f32[192,128]{1,0:T(8,128)S(1)} %collective-permute-done.11.refs_3_, ...), custom_call_target="tpu_custom_call" | custom-call | flops 1572864 | bytes 1572864 | tf_op jit(solution)/shard_map/pallas_call | solution.py:578
  (8 shorter events, 0.0 us)
Async XLA Ops:
  0.0 1.1 %copy-start.1 = (f32[2,3,32,1024]{3,2,1,0:T(8,128)S(1)}, f32[2,3,32,1024]{3,2,1,0:T(8,128)}, u32[]{:S(2)}) copy-start(f32[2,3,32,1024]{3,2,1,0:T(8,128)} %state_ref.1) | copy-start | bytes 2359300
  1.1 24.1 %copy-start = (f32[3,32,1024]{2,1,0:T(8,128)S(1)}, f32[3,32,1024]{2,1,0:T(8,128)}, u32[]{:S(2)}) copy-start(f32[3,32,1024]{2,1,0:T(8,128)} %refs_8_.3) | copy-start | bytes 1179652
  1.5 8.8 %collective-permute-start = (f32[208,128]{1,0:T(8,128)S(1)}, f32[208,128]{1,0:T(8,128)S(1)}, u32[]{:S(2)}, u32[]{:S(2)}) collective-permute-start(f32[208,128]{1,0:T(8,128)S(1)} %get-tuple-element.26), channel_id=1, source_target_pairs={{0,4},{4,0},{8,12},{12,8},{16,20},{20,16},{24,28},{28,24},{1,5},{5... | collective-permute-start | bytes 319496 | tf_op jit(solution)/shard_map/ppermute | solution.py:593
  4.5 9.5 %collective-permute-start.1 = (f32[208,128]{1,0:T(8,128)S(1)}, f32[208,128]{1,0:T(8,128)S(1)}, u32[]{:S(2)}, u32[]{:S(2)}) collective-permute-start(f32[208,128]{1,0:T(8,128)S(1)} %get-tuple-element.27), channel_id=1, source_target_pairs={{0,8},{4,12},{8,0},{12,4},{16,24},{20,28},{24,16},{28,20},{1,9},{5... | collective-permute-start | bytes 319496 | tf_op jit(solution)/shard_map/ppermute | solution.py:593
  6.1 7.9 %collective-permute-start.2 = (f32[208,128]{1,0:T(8,128)S(1)}, f32[208,128]{1,0:T(8,128)S(1)}, u32[]{:S(2)}, u32[]{:S(2)}) collective-permute-start(f32[208,128]{1,0:T(8,128)S(1)} %get-tuple-element.28), channel_id=1, source_target_pairs={{0,12},{4,8},{8,4},{12,0},{16,28},{20,24},{24,20},{28,16},{1,13},{... | collective-permute-start | bytes 319496 | tf_op jit(solution)/shard_map/ppermute | solution.py:593
  6.1 8.0 %collective-permute-start.3 = (f32[208,128]{1,0:T(8,128)S(1)}, f32[208,128]{1,0:T(8,128)S(1)}, u32[]{:S(2)}, u32[]{:S(2)}) collective-permute-start(f32[208,128]{1,0:T(8,128)S(1)} %get-tuple-element.29), channel_id=1, source_target_pairs={{0,16},{4,20},{8,24},{12,28},{16,0},{20,4},{24,8},{28,12},{1,17},{... | collective-permute-start | bytes 319496 | tf_op jit(solution)/shard_map/ppermute | solution.py:593
  9.1 16.2 %collective-permute-start.4 = (f32[208,128]{1,0:T(8,128)S(1)}, f32[208,128]{1,0:T(8,128)S(1)}, u32[]{:S(2)}, u32[]{:S(2)}) collective-permute-start(f32[208,128]{1,0:T(8,128)S(1)} %get-tuple-element.30), channel_id=1, source_target_pairs={{0,20},{4,16},{8,28},{12,24},{16,4},{20,0},{24,12},{28,8},{1,21},{... | collective-permute-start | bytes 319496 | tf_op jit(solution)/shard_map/ppermute | solution.py:593
  10.3 14.9 %collective-permute-start.5 = (f32[208,128]{1,0:T(8,128)S(1)}, f32[208,128]{1,0:T(8,128)S(1)}, u32[]{:S(2)}, u32[]{:S(2)}) collective-permute-start(f32[208,128]{1,0:T(8,128)S(1)} %get-tuple-element.31), channel_id=1, source_target_pairs={{0,24},{4,28},{8,16},{12,20},{16,8},{20,12},{24,0},{28,4},{1,25},{... | collective-permute-start | bytes 319496 | tf_op jit(solution)/shard_map/ppermute | solution.py:593
  14.0 11.3 %collective-permute-start.6 = (f32[208,128]{1,0:T(8,128)S(1)}, f32[208,128]{1,0:T(8,128)S(1)}, u32[]{:S(2)}, u32[]{:S(2)}) collective-permute-start(f32[208,128]{1,0:T(8,128)S(1)} %get-tuple-element.32), channel_id=1, source_target_pairs={{0,28},{4,24},{8,20},{12,16},{16,12},{20,8},{24,4},{28,0},{1,29},{... | collective-permute-start | bytes 319496 | tf_op jit(solution)/shard_map/ppermute | solution.py:593
  25.5 4.3 %collective-permute-start.7 = (f32[232,128]{1,0:T(8,128)S(1)}, f32[232,128]{1,0:T(8,128)S(1)}, u32[]{:S(2)}, u32[]{:S(2)}) collective-permute-start(f32[232,128]{1,0:T(8,128)S(1)} %get-tuple-element.35), channel_id=1, source_target_pairs={{0,1},{1,2},{2,3},{3,0},{4,5},{5,6},{6,7},{7,4},{8,9},{9,10},{10,1... | collective-permute-start | bytes 356360 | tf_op jit(solution)/shard_map/ppermute | solution.py:614
  25.6 4.6 %collective-permute-start.8 = (f32[232,128]{1,0:T(8,128)S(1)}, f32[232,128]{1,0:T(8,128)S(1)}, u32[]{:S(2)}, u32[]{:S(2)}) collective-permute-start(f32[232,128]{1,0:T(8,128)S(1)} %get-tuple-element.36), channel_id=1, source_target_pairs={{1,0},{2,1},{3,2},{0,3},{5,4},{6,5},{7,6},{4,7},{9,8},{10,9},{11,1... | collective-permute-start | bytes 356360 | tf_op jit(solution)/shard_map/ppermute | solution.py:615
  37.1 9.1 %collective-permute-start.9 = (f32[192,128]{1,0:T(8,128)S(1)}, f32[192,128]{1,0:T(8,128)S(1)}, u32[]{:S(2)}, u32[]{:S(2)}) collective-permute-start(f32[192,128]{1,0:T(8,128)S(1)} %get-tuple-element.38), channel_id=1, source_target_pairs={{0,4},{4,0},{8,12},{12,8},{16,20},{20,16},{24,28},{28,24},{1,5},{5... | collective-permute-start | bytes 294920 | tf_op jit(solution)/shard_map/ppermute | solution.py:593
  38.1 10.5 %collective-permute-start.10 = (f32[192,128]{1,0:T(8,128)S(1)}, f32[192,128]{1,0:T(8,128)S(1)}, u32[]{:S(2)}, u32[]{:S(2)}) collective-permute-start(f32[192,128]{1,0:T(8,128)S(1)} %get-tuple-element.39), channel_id=1, source_target_pairs={{0,8},{4,12},{8,0},{12,4},{16,24},{20,28},{24,16},{28,20},{1,9},{5... | collective-permute-start | bytes 294920 | tf_op jit(solution)/shard_map/ppermute | solution.py:593
  42.0 8.9 %collective-permute-start.11 = (f32[192,128]{1,0:T(8,128)S(1)}, f32[192,128]{1,0:T(8,128)S(1)}, u32[]{:S(2)}, u32[]{:S(2)}) collective-permute-start(f32[192,128]{1,0:T(8,128)S(1)} %get-tuple-element.40), channel_id=1, source_target_pairs={{0,12},{4,8},{8,4},{12,0},{16,28},{20,24},{24,20},{28,16},{1,13},{... | collective-permute-start | bytes 294920 | tf_op jit(solution)/shard_map/ppermute | solution.py:593
  42.9 8.0 %collective-permute-start.12 = (f32[192,128]{1,0:T(8,128)S(1)}, f32[192,128]{1,0:T(8,128)S(1)}, u32[]{:S(2)}, u32[]{:S(2)}) collective-permute-start(f32[192,128]{1,0:T(8,128)S(1)} %get-tuple-element.41), channel_id=1, source_target_pairs={{0,16},{4,20},{8,24},{12,28},{16,0},{20,4},{24,8},{28,12},{1,17},{... | collective-permute-start | bytes 294920 | tf_op jit(solution)/shard_map/ppermute | solution.py:593
  46.2 15.8 %collective-permute-start.13 = (f32[192,128]{1,0:T(8,128)S(1)}, f32[192,128]{1,0:T(8,128)S(1)}, u32[]{:S(2)}, u32[]{:S(2)}) collective-permute-start(f32[192,128]{1,0:T(8,128)S(1)} %get-tuple-element.42), channel_id=1, source_target_pairs={{0,20},{4,16},{8,28},{12,24},{16,4},{20,0},{24,12},{28,8},{1,21},{... | collective-permute-start | bytes 294920 | tf_op jit(solution)/shard_map/ppermute | solution.py:593
  46.2 15.8 %collective-permute-start.14 = (f32[192,128]{1,0:T(8,128)S(1)}, f32[192,128]{1,0:T(8,128)S(1)}, u32[]{:S(2)}, u32[]{:S(2)}) collective-permute-start(f32[192,128]{1,0:T(8,128)S(1)} %get-tuple-element.43), channel_id=1, source_target_pairs={{0,24},{4,28},{8,16},{12,20},{16,8},{20,12},{24,0},{28,4},{1,25},{... | collective-permute-start | bytes 294920 | tf_op jit(solution)/shard_map/ppermute | solution.py:593
  48.6 13.4 %collective-permute-start.15 = (f32[192,128]{1,0:T(8,128)S(1)}, f32[192,128]{1,0:T(8,128)S(1)}, u32[]{:S(2)}, u32[]{:S(2)}) collective-permute-start(f32[192,128]{1,0:T(8,128)S(1)} %get-tuple-element.44), channel_id=1, source_target_pairs={{0,28},{4,24},{8,20},{12,16},{16,12},{20,8},{24,4},{28,0},{1,29},{... | collective-permute-start | bytes 294920 | tf_op jit(solution)/shard_map/ppermute | solution.py:593

commit v3 on v0

--- a/solution.py
+++ b/solution.py
@@ -1,8 +1,11 @@
+import functools
 import math
 
 import jax
 import jax.numpy as jnp
 from jax import lax
+from jax.experimental import pallas as pl
+from jax.experimental.pallas import tpu as pltpu
 from jax.sharding import PartitionSpec as P
 
 SWEEPS = 4
@@ -229,9 +232,680 @@
     return state - correction.reshape(state.shape)
 
 
+LANES = 128
+HALO = SWEEPS
+GROUP = 2 * HALO
+ROW0 = 8
+MAIN = ROW0 + HALO
+SHIFT = 1.0 + 4.0 * viscous
+RATE = 1.0 / SHIFT
+VMEM_BYTES = 48 * 1024 * 1024
+SLABS = 2
+FIELDS = 3
+EACH = [(f, c) for f in range(FIELDS) for c in range(SLABS)]
+
+
+def fits_fast_plan(state, width_tm):
+    steps_dev, fields, band_rows, columns = state.shape
+    half = width_tm // 2
+    steps = steps_dev * half
+    return (
+        width_tm > 1
+        and width_tm & (width_tm - 1) == 0
+        and columns == SLABS * LANES * half
+        and SWEEPS * GROUP <= GROUP * steps <= LANES
+        and LANES % (GROUP * steps_dev) == 0
+        and band_rows % 8 == 0
+        and band_rows >= 16
+        and fields == FIELDS
+    )
+
+
+def lanes(rows=8):
+    return lax.broadcasted_iota(jnp.int32, (rows, LANES), 1)
+
+
+def step_of_lane(lane):
+    return ((lane + HALO) & (LANES - 1)) // GROUP
+
+
+def turn(values, shift):
+    return pltpu.roll(values, shift % LANES, 1)
+
+
+def tile_at(index):
+    return pl.ds(pl.multiple_of(index * LANES, LANES), LANES)
+
+
+def binomial(top, bottom):
+    return float(math.comb(top, bottom))
+
+
+def side_places(tile, width_tm):
+    last = width_tm // 2 * SLABS - 1
+    return tile_at((SLABS * tile + SLABS) & last), tile_at((SLABS * tile + last) & last)
+
+
+def pack_kernel(width_tm, state_ref, *outs):
+    steps_dev, fields, rows, _ = state_ref.shape
+    half = width_tm // 2
+    me = lax.axis_index("tm")
+    lane = lanes()
+    step = step_of_lane(lane)
+    blocks = rows // 8
+    per_word = LANES // (GROUP * steps_dev)
+    for b, out in enumerate(outs):
+        tile = (me ^ b) & (half - 1)
+        after, prior = side_places(tile, width_tm)
+        at = 0
+        for c in range(SLABS):
+            for i in range(steps_dev):
+                for f in range(fields):
+                    out[at : at + rows, :] = state_ref[i, f, :, tile_at(SLABS * tile + c)]
+                    at += rows
+        for first in range(0, fields * blocks, per_word):
+            packed = jnp.zeros((8, LANES), jnp.float32)
+            for g in range(first, min(first + per_word, fields * blocks)):
+                f, r = divmod(g, blocks)
+                for i in range(steps_dev):
+                    slot = steps_dev * (g - first) + i
+                    sides = jnp.where(
+                        lane < LANES // 2,
+                        state_ref[i, f, 8 * r : 8 * r + 8, after],
+                        state_ref[i, f, 8 * r : 8 * r + 8, prior],
+                    )
+                    packed = jnp.where(step == slot, turn(sides, GROUP * slot), packed)
+            out[at : at + 8, :] = packed
+            at += 8
+
+
+def edge_kernel(width_tm, steps_dev, *refs):
+    half = width_tm // 2
+    pieces, initial_ref = refs[:half], refs[half]
+    up, down, side, side_initial = refs[half + 1 :]
+    fields, rows, _ = initial_ref.shape
+    me = lax.axis_index("tm")
+    mine = me & (half - 1)
+    lane = lanes()
+    owner = step_of_lane(lane) // steps_dev
+    blocks = rows // 8
+    per_word = LANES // (GROUP * steps_dev)
+    main = SLABS * steps_dev * fields * rows
+    after, prior = side_places(mine, width_tm)
+    for g in range(fields * blocks):
+        f, r = divmod(g, blocks)
+        word, place = divmod(g, per_word)
+        found = jnp.zeros((8, LANES), jnp.float32)
+        for b in range(half):
+            source = mine ^ b
+            value = pieces[b][main + 8 * word : main + 8 * word + 8, :]
+            shift = (GROUP * steps_dev * (source - place)) & (LANES - 1)
+            found = jnp.where(owner == source, pltpu.roll(value, shift, 1), found)
+        side[f, 8 * r : 8 * r + 8, :] = found
+        side_initial[f, 8 * r : 8 * r + 8, :] = jnp.where(
+            lane < LANES // 2,
+            initial_ref[f, 8 * r : 8 * r + 8, after],
+            initial_ref[f, 8 * r : 8 * r + 8, prior],
+        )
+    for out, part in ((up, slice(0, HALO)), (down, slice(rows - HALO, rows))):
+        k = 0
+        for b in range(half):
+            for at in range(0, main, rows):
+                out[k : k + HALO, :] = pieces[b][at + part.start : at + part.stop, :]
+                k += HALO
+        for c in range(SLABS):
+            for f in range(fields):
+                out[k : k + HALO, :] = initial_ref[f, part, tile_at(SLABS * mine + c)]
+                k += HALO
+        for held in (side, side_initial):
+            for f in range(fields):
+                out[k : k + HALO, :] = held[f, part, :]
+                k += HALO
+
+
+def full_tendency(own, east, west, north, south):
+    e, u, v = own
+    around = [east[f] + west[f] + (north[f] + south[f]) for f in range(FIELDS)]
+    quarter = 0.5 * time_step
+    flux = ((1.0 + east[0]) * east[1] - (1.0 + west[0]) * west[1]) + (
+        (1.0 + south[0]) * south[2] - (1.0 + north[0]) * north[2]
+    )
+    carry1 = u * (east[1] - west[1]) + v * (south[1] - north[1]) + (east[0] - west[0])
+    carry2 = u * (east[2] - west[2]) + v * (south[2] - north[2]) + (south[0] - north[0])
+    diagonal = 1.0 + 4.0 * viscous
+    return (
+        diagonal * e + quarter * flux - viscous * around[0],
+        diagonal * u + quarter * carry1 - coriolis * v - viscous * around[1],
+        diagonal * v + quarter * carry2 + coriolis * u - viscous * around[2],
+    )
+
+
+def off_diagonal(own, east, west, north, south):
+    _, u, v = own
+    around = [east[f] + west[f] + (north[f] + south[f]) for f in range(FIELDS)]
+    quarter = 0.5 * time_step
+    return (
+        viscous * around[0] - quarter * ((east[1] - west[1]) + (south[2] - north[2])),
+        viscous * around[1] - quarter * (east[0] - west[0]) + coriolis * v,
+        viscous * around[2] - quarter * (south[0] - north[0]) - coriolis * u,
+    )
+
+
+def chain_factors():
+    gammas = []
+    for weight in sweep_weights():
+        shifted = [1.0] + gammas
+        gammas = [weight * x for x in shifted]
+        for i, x in enumerate(shifted[1:]):
+            gammas[i] += (1.0 - weight) * x
+    scale = RATE * gammas[-1]
+    ratios = []
+    for gamma in reversed(gammas[:-1]):
+        ratios.append(gamma / scale)
+        scale *= RATE
+    return gammas, ratios, scale
+
+
+def series_product(a, b):
+    return [sum(a[i] * b[d - i] for i in range(d + 1)) for d in range(SWEEPS)]
+
+
+def swap_factors(steps):
+    hop = [RATE ** (steps + d) * binomial(steps - 1 + d, d) for d in range(SWEEPS)]
+    lap = [circulant_alpha * x for x in series_product(hop, hop)]
+    inverse = []
+    for d in range(SWEEPS):
+        value = (1.0 if d == 0 else 0.0) + sum(lap[i] * inverse[d - i] for i in range(1, d + 1))
+        inverse.append(value / (1.0 - lap[0]))
+    own = [circulant_alpha * x for x in series_product(inverse, hop)]
+    return own, [circulant_alpha * x for x in inverse], inverse
+
+
+class Side:
+    def __init__(self, rows):
+        self.tall = rows + 2 * HALO
+        self.span = slice(ROW0, ROW0 + self.tall)
+        lane = lanes(self.tall)
+        self.step = step_of_lane(lane)
+        self.after = (lane & (GROUP - 1)) == 0
+        self.before = (lane & (GROUP - 1)) == GROUP - 1
+
+    def parts(self, held, ends):
+        own, north, south = (
+            [held[f, ROW0 + d : ROW0 + d + self.tall, :] for f in range(FIELDS)] for d in (0, -1, 1)
+        )
+        last = [ends[f, self.span, :] for f in range(FIELDS)]
+        east = [jnp.where(self.before, turn(last[f], -1), turn(own[f], -1)) for f in range(FIELDS)]
+        west = [jnp.where(self.after, turn(last[f], 1), turn(own[f], 1)) for f in range(FIELDS)]
+        return own, east, west, north, south
+
+    def set_seams(self, seams, values):
+        for f in range(FIELDS):
+            seams[f, self.span, :] = jnp.where(self.after, turn(values[f], 1), turn(values[f], -1))
+
+    def product(self, values, matrix):
+        done = jnp.dot(
+            jnp.concatenate(values, axis=0),
+            matrix,
+            precision=highest,
+            preferred_element_type=jnp.float32,
+        )
+        return [done[self.tall * f : self.tall * (f + 1), :] for f in range(FIELDS)]
+
+
+def lane_matrix(entry):
+    source = lax.broadcasted_iota(jnp.int32, (LANES, LANES), 0)
+    target = lax.broadcasted_iota(jnp.int32, (LANES, LANES), 1)
+    same = ((source - target) & (GROUP - 1)) == 0
+    return jnp.where(same, entry(step_of_lane(source), step_of_lane(target)), 0.0)
+
+
+def step_parts(held, n, start, seam):
+    lane = lanes()
+    load = lambda d: {k: held[n, k[0], k[1], pl.ds(start + d, 8), :] for k in EACH}
+    own, north, south = load(0), load(-1), load(1)
+    east, west = {}, {}
+    return own, east, west, north, south, lane
+
+
+def neighbours(held, slot, start, seam, n):
+    lane = lanes()
+    is_first, is_last = lane == 0, lane == LANES - 1
+    load = lambda d: {k: held[slot, k[0], k[1], pl.ds(start + d, 8), :] for k in EACH}
+    own, north, south = load(0), load(-1), load(1)
+    east, west = {}, {}
+    for f in range(FIELDS):
+        across = turn(seam[f], -GROUP * n)
+        back = [turn(own[f, c], -1) for c in range(SLABS)] + [across]
+        ahead = [across] + [turn(own[f, c], 1) for c in range(SLABS)]
+        for c in range(SLABS):
+            east[f, c] = jnp.where(is_last, back[c + 1], back[c])
+            west[f, c] = jnp.where(is_first, ahead[c], ahead[c + 1])
+    return own, east, west, north, south
+
+
+def slab(parts, c):
+    return [[part[f, c] for f in range(FIELDS)] for part in parts]
+
+
+def add_ends(last, own, n):
+    lane = lanes()
+    step = step_of_lane(lane)
+    for f in range(FIELDS):
+        both = jnp.where(lane < LANES // 2, own[f, 0], own[f, SLABS - 1])
+        last[f] = jnp.where(step == n, turn(both, GROUP * n), last[f])
+
+
+def zeros(count):
+    return [jnp.zeros((8, LANES), jnp.float32)] * count
+
+
+def residual_tile(steps, first_half, start, state, rhs, seams, ends, send):
+    seam = [seams[f, pl.ds(start, 8), :] for f in range(FIELDS)]
+    last = zeros(FIELDS)
+    sums = {k: zeros(SWEEPS) for k in EACH}
+    for n in range(steps):
+        parts = neighbours(state, n + 1, start, seam, n)
+        add_ends(last, parts[0], n)
+        for c in range(SLABS):
+            value = full_tendency(*slab(parts, c))
+            for f in range(FIELDS):
+                carry = (value[f] - state[n, f, c, pl.ds(start, 8), :]) * SHIFT**n
+                rhs[n, f, c, pl.ds(start, 8), :] = carry
+                for j in range(SWEEPS):
+                    carry = sums[f, c][j] + carry
+                    sums[f, c][j] = carry
+    for f in range(FIELDS):
+        ends[f, pl.ds(start, 8), :] = last[f]
+    for f, c in EACH:
+        for j in range(SWEEPS):
+            value = sums[f, c][j] * RATE ** (steps + j)
+            if j == 0:
+                value = value - jnp.where(first_half, state[steps, f, c, pl.ds(start, 8), :], 0.0)
+            send(SWEEPS - 1 - j, f, c, value)
+
+
+def inner_kernel(width_tm, steps_dev, *refs):
+    half = width_tm // 2
+    pieces, (initial_ref, side) = refs[:half], refs[half : half + 2]
+    state, rhs, ends, sent, seams = refs[half + 2 :]
+    fields, rows, _ = initial_ref.shape
+    steps = half * steps_dev
+    me = lax.axis_index("tm")
+    mine = me & (half - 1)
+    first_half = me < half
+    body = slice(MAIN, MAIN + rows)
+    for b in range(half):
+        at = 0
+        for c in range(SLABS):
+            for i in range(steps_dev):
+                n = steps_dev * (mine ^ b) + i
+                for f in range(fields):
+                    state[n + 1, f, c, body, :] = pieces[b][at : at + rows, :]
+                    at += rows
+    for f, c in EACH:
+        state[0, f, c, body, :] = jnp.where(first_half, initial_ref[f, :, tile_at(SLABS * mine + c)], 0.0)
+    lane = lanes(rows)
+    after = (lane & (GROUP - 1)) == 0
+    for f in range(fields):
+        seams[f, body, :] = jnp.where(after, turn(side[f], 1), turn(side[f], -1))
+
+    @pl.loop(1, rows // 8)
+    def _(t):
+        def send(p, f, c, value):
+            sent[p, f, c, pl.ds(pl.multiple_of(8 * t - 8, 8), 8), :] = value
+
+        residual_tile(steps, first_half, ROW0 + 8 * t, state, rhs, seams, ends, send)
+
+
+def outer_kernel(width_tm, steps_dev, rows, *refs):
+    half = width_tm // 2
+    side, side_initial, above, below = refs[3:7]
+    state, rhs, ends, hrhs, sent, hstate, hbefore, seams = refs[7:]
+    steps = half * steps_dev
+    me = lax.axis_index("tm")
+    mine = me & (half - 1)
+    first_half = me < half
+    body = slice(MAIN, MAIN + rows)
+    top, bottom = slice(ROW0, MAIN), slice(MAIN + rows, MAIN + rows + HALO)
+    k = 0
+    for b in range(half):
+        for c in range(SLABS):
+            for i in range(steps_dev):
+                n = steps_dev * (mine ^ b) + i
+                for f in range(FIELDS):
+                    state[n + 1, f, c, top, :] = above[k : k + HALO, :]
+                    state[n + 1, f, c, bottom, :] = below[k : k + HALO, :]
+                    k += HALO
+    for c in range(SLABS):
+        for f in range(FIELDS):
+            state[0, f, c, top, :] = jnp.where(first_half, above[k : k + HALO, :], 0.0)
+            state[0, f, c, bottom, :] = jnp.where(first_half, below[k : k + HALO, :], 0.0)
+            k += HALO
+    for held, given in ((hstate, side), (hbefore, side_initial)):
+        for f in range(FIELDS):
+            held[f, body, :] = given[f, :, :]
+            held[f, top, :] = above[k : k + HALO, :]
+            held[f, bottom, :] = below[k : k + HALO, :]
+            k += HALO
+    sides = Side(rows)
+    sides.set_seams(seams, [hstate[f, sides.span, :] for f in range(FIELDS)])
+    main = SWEEPS * FIELDS * SLABS * 16
+    for which, start in enumerate((ROW0, ROW0 + rows)):
+
+        def send(p, f, c, value):
+            at = ((p * FIELDS + f) * SLABS + c) * 16 + 8 * which
+            sent[at : at + 8, :] = value
+
+        residual_tile(steps, first_half, start, state, rhs, seams, ends, send)
+    parts = sides.parts(hstate, ends)
+    value = full_tendency(*parts)
+    growth = jnp.where(
+        sides.step < steps, jnp.exp(sides.step.astype(jnp.float32) * math.log(SHIFT)), 0.0
+    )
+    held = []
+    for f in range(FIELDS):
+        first = jnp.where(first_half, hbefore[f, sides.span, :], 0.0)
+        before = jnp.where(sides.step == 0, first, turn(parts[0][f], GROUP))
+        held.append((value[f] - before) * growth)
+        hrhs[f, sides.span, :] = held[f]
+
+    def entry(source, target):
+        result = jnp.zeros((LANES, LANES), jnp.float32)
+        for p in range(SWEEPS):
+            j = SWEEPS - p
+            for n in range(steps):
+                weight = RATE ** (steps - 1 + j) * binomial(steps - 1 - n + j - 1, j - 1)
+                result = jnp.where((target == p) & (source == n), weight, result)
+        return result
+
+    handed = sides.product(held, lane_matrix(entry))
+    for f in range(FIELDS):
+        last = turn(parts[0][f], GROUP * (SWEEPS - steps))
+        last = jnp.where(first_half & (sides.step == SWEEPS - 1), last, 0.0)
+        sent[main + sides.tall * f : main + sides.tall * (f + 1), :] = handed[f] - last
+
+
+def chain_kernel(steps, rows, rhs, hrhs, result, ya, yb, hya, hyb, ends, seams):
+    _, ratios, _ = chain_factors()
+    sides = Side(rows)
+    blocks = sides.tall // 8
+    running = lane_matrix(
+        lambda source, target: jnp.where((source <= target) & (target < steps), 1.0, 0.0)
+    )
+    side_new = sides.product([hrhs[f, sides.span, :] for f in range(FIELDS)], running)
+    for f in range(FIELDS):
+        hya[f, sides.span, :] = side_new[f]
+    sides.set_seams(seams, side_new)
+
+    @pl.loop(0, blocks)
+    def _(t):
+        start = ROW0 + 8 * t
+        for f, c in EACH:
+            total = jnp.zeros((8, LANES), jnp.float32)
+            for n in range(steps):
+                total = total + rhs[n, f, c, pl.ds(start, 8), :]
+                ya[n, f, c, pl.ds(start, 8), :] = total
+
+    def sweep(ratio, old, hold, new, hnew, final):
+        first = MAIN if final else ROW0
+
+        @pl.loop(0, rows // 8 if final else blocks)
+        def _(t):
+            start = first + 8 * t
+            seam = [seams[f, pl.ds(start, 8), :] for f in range(FIELDS)]
+            last = zeros(FIELDS)
+            total = dict(zip(EACH, zeros(len(EACH))))
+            for n in range(steps):
+                parts = neighbours(old, n, start, seam, n)
+                if not final:
+                    add_ends(last, parts[0], n)
+                for c in range(SLABS):
+                    value = off_diagonal(*slab(parts, c))
+                    for f in range(FIELDS):
+                        carry = value[f] + ratio * rhs[n, f, c, pl.ds(start, 8), :]
+                        total[f, c] = total[f, c] + carry
+                        if final:
+                            at = pl.ds(pl.multiple_of(8 * t, 8), 8)
+                            new[n, f, c, at, :] = total[f, c]
+                        else:
+                            new[n, f, c, pl.ds(start, 8), :] = total[f, c]
+            if not final:
+                for f in range(FIELDS):
+                    ends[f, pl.ds(start, 8), :] = last[f]
+
+        if not final:
+            value = off_diagonal(*sides.parts(hold, ends))
+            side_next = sides.product(
+                [value[f] + ratio * hrhs[f, sides.span, :] for f in range(FIELDS)], running
+            )
+            for f in range(FIELDS):
+                hnew[f, sides.span, :] = side_next[f]
+            sides.set_seams(seams, side_next)
+
+    buffers = [(ya, hya), (yb, hyb)]
+    for m in range(1, SWEEPS):
+        old, new = buffers[(m + 1) % 2], buffers[m % 2]
+        final = m == SWEEPS - 1
+        sweep(ratios[m - 1], *old, result if final else new[0], new[1], final)
+
+
+def join_kernel(width_tm, steps_dev, rows, *refs):
+    half = width_tm // 2
+    inner_own, outer_own, inner_other, outer_other, chained, state = refs[:6]
+    outs = refs[6 : 6 + half]
+    given, pa, pb, hgiven, hpa, hpb, ends, seams, result = refs[6 + half :]
+    steps = half * steps_dev
+    me = lax.axis_index("tm")
+    mine = me & (half - 1)
+    gammas, _, scale = chain_factors()
+    own, first, second = swap_factors(steps)
+    other = [jnp.where(me < half, a, b) for a, b in zip(first, second)]
+    sides = Side(rows)
+    blocks = sides.tall // 8
+    middle = slice(ROW0 + 8, ROW0 + rows)
+    main = SWEEPS * FIELDS * SLABS * 16
+
+    def joined(pick_own, pick_other, p):
+        total = None
+        for d in range(SWEEPS - p):
+            term = other[d] * pick_other(p + d) + own[d] * pick_own(p + d)
+            total = term if total is None else total + term
+        return total
+
+    for f, c in EACH:
+        for p in range(SWEEPS):
+            value = joined(lambda k: inner_own[k, f, c], lambda k: inner_other[k, f, c], p)
+            given[p, f, c, middle, :] = value
+            pa[p, f, c, middle, :] = gammas[-1] * value
+            for which, start in enumerate((ROW0, ROW0 + rows)):
+
+                def pick(ref, k):
+                    at = ((k * FIELDS + f) * SLABS + c) * 16 + 8 * which
+                    return ref[at : at + 8, :]
+
+                value = joined(lambda k: pick(outer_own, k), lambda k: pick(outer_other, k), p)
+                given[p, f, c, start : start + 8, :] = value
+                pa[p, f, c, start : start + 8, :] = gammas[-1] * value
+
+    def from_later(value, d):
+        return jnp.where(sides.step < SWEEPS - d, turn(value, -GROUP * d), 0.0)
+
+    side_new = []
+    for f in range(FIELDS):
+        rows_f = slice(main + sides.tall * f, main + sides.tall * (f + 1))
+        value = jnp.zeros((sides.tall, LANES), jnp.float32)
+        for d in range(SWEEPS):
+            value = value + from_later(
+                other[d] * outer_other[rows_f, :] + own[d] * outer_own[rows_f, :], d
+            )
+        hgiven[f, sides.span, :] = value
+        side_new.append(gammas[-1] * value)
+        hpa[f, sides.span, :] = side_new[f]
+    sides.set_seams(seams, side_new)
+
+    buffers = [(pa, hpa), (pb, hpb)]
+    for k in range(1, SWEEPS):
+        (old, hold), (new, hnew) = buffers[(k + 1) % 2], buffers[k % 2]
+        gamma = gammas[SWEEPS - 1 - k]
+        final = k == SWEEPS - 1
+        first_row = MAIN if final else ROW0
+
+        @pl.loop(0, rows // 8 if final else blocks)
+        def _(t):
+            start = first_row + 8 * t
+            here = pl.ds(start, 8)
+            seam = [seams[f, here, :] for f in range(FIELDS)]
+            last = zeros(FIELDS)
+            found = {}
+            for p in range(SWEEPS):
+                parts = neighbours(old, p, start, seam, p)
+                if not final:
+                    add_ends(last, parts[0], p)
+                for c in range(SLABS):
+                    value = off_diagonal(*slab(parts, c))
+                    for f in range(FIELDS):
+                        total = value[f]
+                        if p + k < SWEEPS:
+                            total = total + gamma * given[p + k, f, c, here, :]
+                        if final:
+                            found[p, f, c] = total * RATE ** (p + 1)
+                        else:
+                            new[p, f, c, here, :] = total
+            if not final:
+                for f in range(FIELDS):
+                    ends[f, here, :] = last[f]
+            else:
+                at = pl.ds(pl.multiple_of(8 * t, 8), 8)
+                for f, c in EACH:
+                    for n in range(steps):
+                        total = scale * chained[n, f, c, at, :]
+                        for p in range(SWEEPS):
+                            total = total + binomial(n + p, p) * found[p, f, c]
+                        result[n, f, c, at, :] = state[n + 1, f, c, here, :] - total * RATE**n
+
+        if not final:
+            value = off_diagonal(*sides.parts(hold, ends))
+            side_next = [
+                value[f] + gamma * from_later(hgiven[f, sides.span, :], k) for f in range(FIELDS)
+            ]
+            for f in range(FIELDS):
+                hnew[f, sides.span, :] = side_next[f]
+            sides.set_seams(seams, side_next)
+
+    for b in range(half):
+        at = 0
+        for c in range(SLABS):
+            for i in range(steps_dev):
+                n = steps_dev * (mine ^ b) + i
+                for f in range(FIELDS):
+                    outs[b][at : at + rows, :] = result[n, f, c, :, :]
+                    at += rows
+
+
+def unpack_kernel(width_tm, *refs):
+    half = width_tm // 2
+    pieces, out = refs[:half], refs[half]
+    steps_dev, fields, rows, _ = out.shape
+    mine = lax.axis_index("tm") & (half - 1)
+    for b in range(half):
+        at = 0
+        for c in range(SLABS):
+            for i in range(steps_dev):
+                for f in range(fields):
+                    out[i, f, :, tile_at(SLABS * (mine ^ b) + c)] = pieces[b][at : at + rows, :]
+                    at += rows
+
+
+def call(kernel, out_shapes, operands, scratch=(), aliases=None):
+    whole = pl.BlockSpec(memory_space=pltpu.VMEM)
+    shapes = [jax.ShapeDtypeStruct(shape, jnp.float32) for shape in out_shapes]
+    moved = 4 * sum(math.prod(x.shape) for x in list(shapes) + list(operands))
+    return pl.pallas_call(
+        kernel,
+        out_shape=shapes,
+        in_specs=[whole] * len(operands),
+        out_specs=[whole] * len(shapes),
+        scratch_shapes=[pltpu.VMEM(shape, jnp.float32) for shape in scratch],
+        input_output_aliases=aliases or {},
+        compiler_params=pltpu.CompilerParams(vmem_limit_bytes=VMEM_BYTES),
+        cost_estimate=pl.CostEstimate(flops=moved, bytes_accessed=moved, transcendentals=0),
+    )(*operands)
+
+
+def swap(piece, b):
+    count = lax.axis_size("tm")
+    return lax.ppermute(piece, "tm", [(k, k ^ b) for k in range(count)])
+
+
+def fast_on_device(state, initial):
+    steps_dev, fields, rows, columns = state.shape
+    width_tm = lax.axis_size("tm")
+    bands = lax.axis_size("space")
+    half = width_tm // 2
+    steps = steps_dev * half
+    main = SLABS * steps_dev * fields * rows
+    words = -(-fields * rows // 8 // (LANES // (GROUP * steps_dev)))
+    tall = rows + 2 * HALO + 2 * ROW0
+    sized = (width_tm, steps_dev)
+    pieces = call(
+        functools.partial(pack_kernel, width_tm), [(main + 8 * words, LANES)] * half, [state]
+    )
+    pieces = [pieces[0]] + [swap(pieces[b], b) for b in range(1, half)]
+    edge_rows = -(-HALO * fields * (SLABS * (steps + 1) + 2) // 8) * 8
+    up, down, side, side_initial = call(
+        functools.partial(edge_kernel, *sized),
+        [(edge_rows, LANES)] * 2 + [(fields, rows, LANES)] * 2,
+        pieces + [initial],
+    )
+    above = lax.ppermute(down, "space", [(i, (i + 1) % bands) for i in range(bands)])
+    below = lax.ppermute(up, "space", [((i + 1) % bands, i) for i in range(bands)])
+    flat = (fields, tall, LANES)
+    held = [(steps + 1, fields, SLABS, tall, LANES), (steps, fields, SLABS, tall, LANES), flat]
+    held_shapes = held
+    *held, inner = call(
+        functools.partial(inner_kernel, *sized),
+        held_shapes + [(SWEEPS, fields, SLABS, rows - 8, LANES)],
+        pieces + [initial, side],
+        [flat],
+    )
+    inner_other = swap(inner, half)
+    tall_rows = rows + 2 * HALO
+    solved, rhs, _, hrhs, outer = call(
+        functools.partial(outer_kernel, *sized, rows),
+        held_shapes + [flat, (SWEEPS * fields * SLABS * 16 + fields * tall_rows, LANES)],
+        held + [side, side_initial, above, below],
+        [flat] * 3,
+        aliases={0: 0, 1: 1, 2: 2},
+    )
+    outer_other = swap(outer, half)
+    (chained,) = call(
+        functools.partial(chain_kernel, steps, rows),
+        [(steps, fields, SLABS, rows, LANES)],
+        [rhs, hrhs],
+        [held_shapes[1]] * 2 + [flat] * 4,
+    )
+    four = (SWEEPS, fields, SLABS, tall, LANES)
+    results = call(
+        functools.partial(join_kernel, *sized, rows),
+        [(main, LANES)] * half,
+        [inner, outer, inner_other, outer_other, chained, solved],
+        [four] * 3 + [flat] * 5 + [(steps, fields, SLABS, rows, LANES)],
+    )
+    results = [results[0]] + [swap(results[b], b) for b in range(1, half)]
+    (updated,) = call(functools.partial(unpack_kernel, width_tm), [state.shape], results)
+    return updated
+
+
+def choose(state, initial):
+    if fits_fast_plan(state, lax.axis_size("tm")):
+        return fast_on_device(state, initial)
+    return on_device(state, initial)
+
+
 def solution(mesh):
     in_specs = (P("tm", None, "space", None), P(None, "space", None))
     out_specs = P("tm", None, "space", None)
     return jax.shard_map(
-        on_device, mesh=mesh, in_specs=in_specs, out_specs=out_specs, check_vma=False
-    )
+        choose, mesh=mesh, in_specs=in_specs, out_specs=out_specs, check_vma=False
+    )

time: 532 us -> 61.9 us (0.12); the launches traced: 524 us -> 61.7 us
  local copies, waits for them, and re-layouts: 357 us -> 2.13 us
  other arithmetic: 46.3 us -> 0 us
  blocking collectives: 29.2 us -> 0 us
  waiting for transfers between devices: 62.3 us -> 34.3 us
  starting transfers between devices: 25.8 us -> 14.8 us
  Pallas kernels: 0 us -> 10.4 us
    unnamed x12 -> x4, local copies, waits for them, and re-layouts: 231 us -> 2.13 us
    all_to_all x3 -> x0, waiting for transfers between devices: 57.3 us -> none  [the longest x1 19.7 us: on_device(): lax.all_to_all(flat_solution, 'tm', split_axis=3, concat_axis=1, tiled=True)]
    all_to_all x7 -> x0, local copies, waits for them, and re-layouts: 55.7 us -> none  [the longest x4 28.2 us: on_device(): lax.all_to_all(residual.reshape(steps_dev, fields, band_rows * columns),...]
    ppermute x9 -> x10, waiting for transfers between devices: 4.99 us -> 34.3 us  [the longest x8 34.3 us: swap(): return lax.ppermute(piece, 'tm', [(k, k ^ b) for k in range(count)])]
    add x1 -> x0, local copies, waits for them, and re-layouts: 29.3 us -> none  [on_device(): iterate = iterate + weights[sweep] * pair_apply(jacobi, banded - applied)]
    all_to_all x1 -> x0, blocking collectives: 29.2 us -> none  [on_device(): lax.all_to_all(all_steps, 'tm', split_axis=0, concat_axis=2, tiled=True)]
    sub x12 -> x0, other arithmetic: 23.2 us -> none  [the longest x7 19.5 us: pair_apply(): factor[0] * values[0] - factor[1] * values[1]]
    reshape x3 -> x0, local copies, waits for them, and re-layouts: 23 us -> none  [the longest x1 22.5 us: on_device(): residual.reshape(steps_dev, fields, band_rows * columns)]
  transfers between devices with their start and end apart: 12 -> 10, of which waited for: 4 -> 8; matrix products, arithmetic and copies ran while one was open for 4% -> 0% of each run, Pallas kernels for 0% -> 10%
where the time goes in v3:
time: 61.9 us; the launch traced here: 61.7 us
  waiting for transfers between devices  34.3 us (55%)
  starting transfers between devices  14.8 us (24%)
  Pallas kernels  10.4 us (17%)
  local copies, waits for them, and re-layouts  2.13 us (3%)
    ppermute x8, waiting for transfers between devices, swap(): return lax.ppermute(piece, 'tm', [(k, k ^ b) for k in range(count)])  34.3 us
    ppermute x8, starting transfers between devices, swap(): return lax.ppermute(piece, 'tm', [(k, k ^ b) for k in range(count)])  13 us
    pallas_call x7, Pallas kernels, call(): pl.pallas_call(kernel, out_shape=shapes, in_specs=[whole] * len(operands)...  10.4 us
    unnamed x4, local copies, waits for them, and re-layouts  2.13 us
    ppermute x1, starting transfers between devices, fast_on_device(): lax.ppermute(up, 'space', [((i + 1) % bands, i) for i in range(bands)])  1.73 us
  transfers between devices with their start and end apart: 10, of which 8 were waited for; matrix products, arithmetic and copies ran while one was open for 0% of the time, Pallas kernels for 10%

profile of v3, /device:TPU:0, one launch (start us, length us, event | category | flops | bytes accessed | tf_op | source)
XLA Modules:
  0.0 61.7 jit_solution(10137016443415491650)
XLA Ops:
  0.0 0.0 copy-start.1
  0.0 1.1 %copy-done.1 = f32[2,3,32,1024]{3,2,1,0:T(8,128)S(1)} copy-done((f32[2,3,32,1024]{3,2,1,0:T(8,128)S(1)}, f32[2,3,32,1024]{3,2,1,0:T(8,128)}, u32[]{:S(2)}) %copy-start.1) | copy-done | bytes 786456
  1.1 0.3 shard_map.28
  1.4 3.0 %collective-permute-start = (f32[400,128]{1,0:T(8,128)S(1)}, f32[400,128]{1,0:T(8,128)S(1)}, u32[]{:S(2)}, u32[]{:S(2)}) collective-permute-start(f32[400,128]{1,0:T(8,128)S(1)} %get-tuple-element.26), channel_id=1, source_target_pairs={{0,4},{4,0},{8,12},{12,8},{16,20},{20,16},{24,28},{28,24},{1,5},{5... | collective-permute-start | bytes 614408 | tf_op jit(solution)/shard_map/ppermute | solution.py:838
  4.4 1.6 %collective-permute-start.1 = (f32[400,128]{1,0:T(8,128)S(1)}, f32[400,128]{1,0:T(8,128)S(1)}, u32[]{:S(2)}, u32[]{:S(2)}) collective-permute-start(f32[400,128]{1,0:T(8,128)S(1)} %get-tuple-element.27), channel_id=1, source_target_pairs={{0,8},{4,12},{8,0},{12,4},{16,24},{20,28},{24,16},{28,20},{1,9},{5... | collective-permute-start | bytes 614408 | tf_op jit(solution)/shard_map/ppermute | solution.py:838
  6.0 0.0 collective-permute-start.2
  6.0 3.5 %collective-permute-done.refs_1_ = f32[400,128]{1,0:T(8,128)S(1)} collective-permute-done((f32[400,128]{1,0:T(8,128)S(1)}, f32[400,128]{1,0:T(8,128)S(1)}, u32[]{:S(2)}, u32[]{:S(2)}) %collective-permute-start) | collective-permute-done | bytes 204832 | tf_op jit(solution)/shard_map/ppermute | solution.py:838
  9.5 2.9 %collective-permute-done.1.refs_2_ = f32[400,128]{1,0:T(8,128)S(1)} collective-permute-done((f32[400,128]{1,0:T(8,128)S(1)}, f32[400,128]{1,0:T(8,128)S(1)}, u32[]{:S(2)}, u32[]{:S(2)}) %collective-permute-start.1) | collective-permute-done | bytes 204832 | tf_op jit(solution)/shard_map/ppermute | solution.py:838
  12.4 2.7 %collective-permute-done.2.refs_3_ = f32[400,128]{1,0:T(8,128)S(1)} collective-permute-done((f32[400,128]{1,0:T(8,128)S(1)}, f32[400,128]{1,0:T(8,128)S(1)}, u32[]{:S(2)}, u32[]{:S(2)}) %collective-permute-start.2) | collective-permute-done | bytes 204832 | tf_op jit(solution)/shard_map/ppermute | solution.py:838
  15.2 0.0 copy-start
  15.2 1.0 %copy-done = f32[3,32,1024]{2,1,0:T(8,128)S(1)} copy-done((f32[3,32,1024]{2,1,0:T(8,128)S(1)}, f32[3,32,1024]{2,1,0:T(8,128)}, u32[]{:S(2)}) %copy-start) | copy-done | bytes 393240
  16.2 0.2 shard_map.29
  16.3 0.1 collective-permute-start.3
  16.4 1.7 %collective-permute-start.4 = (f32[240,128]{1,0:T(8,128)S(1)}, f32[240,128]{1,0:T(8,128)S(1)}, u32[]{:S(2)}, u32[]{:S(2)}) collective-permute-start(f32[240,128]{1,0:T(8,128)S(1)} %get-tuple-element.36), channel_id=1, source_target_pairs={{1,0},{2,1},{3,2},{0,3},{5,4},{6,5},{7,6},{4,7},{9,8},{10,9},{11,1... | collective-permute-start | bytes 368648 | tf_op jit(solution)/shard_map/ppermute | solution.py:862
  18.1 0.8 %shard_map.30 = (f32[9,3,2,56,128]{4,3,2,1,0:T(8,128)S(1)}, f32[8,3,2,56,128]{4,3,2,1,0:T(8,128)S(1)}, f32[3,56,128]{2,1,0:T(8,128)S(1)}, f32[4,3,2,24,128]{4,3,2,1,0:T(8,128)S(1)}) custom-call(f32[400,128]{1,0:T(8,128)S(1)} %get-tuple-element.25.refs_0_, f32[400,128]{1,0:T(8,128)S(1)} %collective-permute-done.refs_1_, ...), custom_call_target="tpu_custom_call" | custom-call | flops 4567040 | bytes 4567040 | tf_op jit(solution)/shard_map/pallas_call | solution.py:824
  19.0 2.8 %collective-permute-start.5 = (f32[4,3,2,24,128]{4,3,2,1,0:T(8,128)S(1)}, f32[4,3,2,24,128]{4,3,2,1,0:T(8,128)S(1)}, u32[]{:S(2)}, u32[]{:S(2)}) collective-permute-start(f32[4,3,2,24,128]{4,3,2,1,0:T(8,128)S(1)} %get-tuple-element.30.refs_0_), channel_id=1, source_target_pairs={{0,16},{4,20},{8,24},{12,28},{16,0},{20,4},{24,8},{28,12},{1,17},{... | collective-permute-start | bytes 884744 | tf_op jit(solution)/shard_map/ppermute | solution.py:838
  21.8 0.0 collective-permute-done.3.refs_5_
  21.8 0.0 collective-permute-done.4.refs_6_
  21.8 0.8 %shard_map.31 = (f32[9,3,2,56,128]{4,3,2,1,0:T(8,128)S(1)}, f32[8,3,2,56,128]{4,3,2,1,0:T(8,128)S(1)}, f32[3,56,128]{2,1,0:T(8,128)S(1)}, f32[3,56,128]{2,1,0:T(8,128)S(1)}, f32[504,128]{1,0:T(8,128)S(1)}) custom-call(f32[9,3,2,56,128]{4,3,2,1,0:T(8,128)S(1)} %get-tuple-element.31.refs_0_, ...), custom_call_target="tpu_custom_call", output_to_operand_aliasing={{0}: (0, {}), {1}: (1, {}), {2}: (2, {})} | custom-call | flops 6709248 | bytes 6709248 | tf_op jit(solution)/shard_map/pallas_call | solution.py:824
  22.6 2.1 %collective-permute-start.6 = (f32[504,128]{1,0:T(8,128)S(1)}, f32[504,128]{1,0:T(8,128)S(1)}, u32[]{:S(2)}, u32[]{:S(2)}) collective-permute-start(f32[504,128]{1,0:T(8,128)S(1)} %get-tuple-element.37.refs_1_), channel_id=1, source_target_pairs={{0,16},{4,20},{8,24},{12,28},{16,0},{20,4},{24,8},{28,12},{1,17},{... | collective-permute-start | bytes 774152 | tf_op jit(solution)/shard_map/ppermute | solution.py:838
  24.7 4.4 %shard_map.32.refs_4_ = f32[8,3,2,32,128]{4,3,2,1,0:T(8,128)S(1)} custom-call(f32[8,3,2,56,128]{4,3,2,1,0:T(8,128)S(1)} %get-tuple-element.38.rhs, f32[3,56,128]{2,1,0:T(8,128)S(1)} %get-tuple-element.39.hrhs), custom_call_target="tpu_custom_call" | custom-call | flops 2248704 | bytes 2248704 | tf_op jit(solution)/shard_map/pallas_call | solution.py:824
  29.1 12.6 %collective-permute-done.5.refs_2_ = f32[4,3,2,24,128]{4,3,2,1,0:T(8,128)S(1)} collective-permute-done((f32[4,3,2,24,128]{4,3,2,1,0:T(8,128)S(1)}, f32[4,3,2,24,128]{4,3,2,1,0:T(8,128)S(1)}, u32[]{:S(2)}, u32[]{:S(2)}) %collective-permute-start.5) | collective-permute-done | bytes 294944 | tf_op jit(solution)/shard_map/ppermute | solution.py:838
  41.7 4.6 %collective-permute-done.6.refs_3_ = f32[504,128]{1,0:T(8,128)S(1)} collective-permute-done((f32[504,128]{1,0:T(8,128)S(1)}, f32[504,128]{1,0:T(8,128)S(1)}, u32[]{:S(2)}, u32[]{:S(2)}) %collective-permute-start.6) | collective-permute-done | bytes 258080 | tf_op jit(solution)/shard_map/ppermute | solution.py:838
  46.3 3.0 %shard_map.33 = (f32[384,128]{1,0:T(8,128)S(1)}, f32[384,128]{1,0:T(8,128)S(1)}, f32[384,128]{1,0:T(8,128)S(1)}, f32[384,128]{1,0:T(8,128)S(1)}) custom-call(f32[4,3,2,24,128]{4,3,2,1,0:T(8,128)S(1)} %get-tuple-element.30.refs_0_, f32[504,128]{1,0:T(8,128)S(1)} %get-tuple-element.37.refs_1_, f32[4,3,2,24,128]{4,3,2,1,0:T(8,128)S(1)} %collective-permute-done.5.refs_2_, ...), custom_call_target="tpu_custom_call" | custom-call | flops 4227072 | bytes 4227072 | tf_op jit(solution)/shard_map/pallas_call | solution.py:824
  49.3 1.6 %collective-permute-start.7 = (f32[384,128]{1,0:T(8,128)S(1)}, f32[384,128]{1,0:T(8,128)S(1)}, u32[]{:S(2)}, u32[]{:S(2)}) collective-permute-start(f32[384,128]{1,0:T(8,128)S(1)} %get-tuple-element.42), channel_id=1, source_target_pairs={{0,4},{4,0},{8,12},{12,8},{16,20},{20,16},{24,28},{28,24},{1,5},{5... | collective-permute-start | bytes 589832 | tf_op jit(solution)/shard_map/ppermute | solution.py:838
  50.8 0.7 %collective-permute-start.8 = (f32[384,128]{1,0:T(8,128)S(1)}, f32[384,128]{1,0:T(8,128)S(1)}, u32[]{:S(2)}, u32[]{:S(2)}) collective-permute-start(f32[384,128]{1,0:T(8,128)S(1)} %get-tuple-element.43), channel_id=1, source_target_pairs={{0,8},{4,12},{8,0},{12,4},{16,24},{20,28},{24,16},{28,20},{1,9},{5... | collective-permute-start | bytes 589832 | tf_op jit(solution)/shard_map/ppermute | solution.py:838
  51.5 1.3 %collective-permute-start.9 = (f32[384,128]{1,0:T(8,128)S(1)}, f32[384,128]{1,0:T(8,128)S(1)}, u32[]{:S(2)}, u32[]{:S(2)}) collective-permute-start(f32[384,128]{1,0:T(8,128)S(1)} %get-tuple-element.44), channel_id=1, source_target_pairs={{0,12},{4,8},{8,4},{12,0},{16,28},{20,24},{24,20},{28,16},{1,13},{... | collective-permute-start | bytes 589832 | tf_op jit(solution)/shard_map/ppermute | solution.py:838
  52.8 3.4 %collective-permute-done.7.refs_1_ = f32[384,128]{1,0:T(8,128)S(1)} collective-permute-done((f32[384,128]{1,0:T(8,128)S(1)}, f32[384,128]{1,0:T(8,128)S(1)}, u32[]{:S(2)}, u32[]{:S(2)}) %collective-permute-start.7) | collective-permute-done | bytes 196640 | tf_op jit(solution)/shard_map/ppermute | solution.py:838
  56.3 2.2 %collective-permute-done.8.refs_2_ = f32[384,128]{1,0:T(8,128)S(1)} collective-permute-done((f32[384,128]{1,0:T(8,128)S(1)}, f32[384,128]{1,0:T(8,128)S(1)}, u32[]{:S(2)}, u32[]{:S(2)}) %collective-permute-start.8) | collective-permute-done | bytes 196640 | tf_op jit(solution)/shard_map/ppermute | solution.py:838
  58.5 2.3 %collective-permute-done.9.refs_3_ = f32[384,128]{1,0:T(8,128)S(1)} collective-permute-done((f32[384,128]{1,0:T(8,128)S(1)}, f32[384,128]{1,0:T(8,128)S(1)}, u32[]{:S(2)}, u32[]{:S(2)}) %collective-permute-start.9) | collective-permute-done | bytes 196640 | tf_op jit(solution)/shard_map/ppermute | solution.py:838
  60.8 1.0 %shard_map.34 = f32[2,3,32,1024]{3,2,1,0:T(8,128)} custom-call(f32[384,128]{1,0:T(8,128)S(1)} %get-tuple-element.41.refs_0_, f32[384,128]{1,0:T(8,128)S(1)} %collective-permute-done.7.refs_1_, f32[384,128]{1,0:T(8,128)S(1)} %collective-permute-done.8.refs_2_, f32[384,128]{1,0:T(8,128)S(1)} %collective-permute-done.9.refs_3_), custom_call_target="tpu_custom_call" | custom-call | flops 1572864 | bytes 1572864 | tf_op jit(solution)/shard_map/pallas_call | solution.py:824
Async XLA Ops:
  0.0 1.1 %copy-start.1 = (f32[2,3,32,1024]{3,2,1,0:T(8,128)S(1)}, f32[2,3,32,1024]{3,2,1,0:T(8,128)}, u32[]{:S(2)}) copy-start(f32[2,3,32,1024]{3,2,1,0:T(8,128)} %state_ref.1) | copy-start | bytes 2359300
  1.4 8.1 %collective-permute-start = (f32[400,128]{1,0:T(8,128)S(1)}, f32[400,128]{1,0:T(8,128)S(1)}, u32[]{:S(2)}, u32[]{:S(2)}) collective-permute-start(f32[400,128]{1,0:T(8,128)S(1)} %get-tuple-element.26), channel_id=1, source_target_pairs={{0,4},{4,0},{8,12},{12,8},{16,20},{20,16},{24,28},{28,24},{1,5},{5... | collective-permute-start | bytes 614408 | tf_op jit(solution)/shard_map/ppermute | solution.py:838
  4.4 8.0 %collective-permute-start.1 = (f32[400,128]{1,0:T(8,128)S(1)}, f32[400,128]{1,0:T(8,128)S(1)}, u32[]{:S(2)}, u32[]{:S(2)}) collective-permute-start(f32[400,128]{1,0:T(8,128)S(1)} %get-tuple-element.27), channel_id=1, source_target_pairs={{0,8},{4,12},{8,0},{12,4},{16,24},{20,28},{24,16},{28,20},{1,9},{5... | collective-permute-start | bytes 614408 | tf_op jit(solution)/shard_map/ppermute | solution.py:838
  6.0 9.2 %collective-permute-start.2 = (f32[400,128]{1,0:T(8,128)S(1)}, f32[400,128]{1,0:T(8,128)S(1)}, u32[]{:S(2)}, u32[]{:S(2)}) collective-permute-start(f32[400,128]{1,0:T(8,128)S(1)} %get-tuple-element.28), channel_id=1, source_target_pairs={{0,12},{4,8},{8,4},{12,0},{16,28},{20,24},{24,20},{28,16},{1,13},{... | collective-permute-start | bytes 614408 | tf_op jit(solution)/shard_map/ppermute | solution.py:838
  15.2 1.0 %copy-start = (f32[3,32,1024]{2,1,0:T(8,128)S(1)}, f32[3,32,1024]{2,1,0:T(8,128)}, u32[]{:S(2)}) copy-start(f32[3,32,1024]{2,1,0:T(8,128)} %refs_4_.3) | copy-start | bytes 1179652
  16.3 5.5 %collective-permute-start.3 = (f32[240,128]{1,0:T(8,128)S(1)}, f32[240,128]{1,0:T(8,128)S(1)}, u32[]{:S(2)}, u32[]{:S(2)}) collective-permute-start(f32[240,128]{1,0:T(8,128)S(1)} %get-tuple-element.35), channel_id=1, source_target_pairs={{0,1},{1,2},{2,3},{3,0},{4,5},{5,6},{6,7},{7,4},{8,9},{9,10},{10,1... | collective-permute-start | bytes 368648 | tf_op jit(solution)/shard_map/ppermute | solution.py:861
  16.4 5.4 %collective-permute-start.4 = (f32[240,128]{1,0:T(8,128)S(1)}, f32[240,128]{1,0:T(8,128)S(1)}, u32[]{:S(2)}, u32[]{:S(2)}) collective-permute-start(f32[240,128]{1,0:T(8,128)S(1)} %get-tuple-element.36), channel_id=1, source_target_pairs={{1,0},{2,1},{3,2},{0,3},{5,4},{6,5},{7,6},{4,7},{9,8},{10,9},{11,1... | collective-permute-start | bytes 368648 | tf_op jit(solution)/shard_map/ppermute | solution.py:862
  19.0 22.7 %collective-permute-start.5 = (f32[4,3,2,24,128]{4,3,2,1,0:T(8,128)S(1)}, f32[4,3,2,24,128]{4,3,2,1,0:T(8,128)S(1)}, u32[]{:S(2)}, u32[]{:S(2)}) collective-permute-start(f32[4,3,2,24,128]{4,3,2,1,0:T(8,128)S(1)} %get-tuple-element.30.refs_0_), channel_id=1, source_target_pairs={{0,16},{4,20},{8,24},{12,28},{16,0},{20,4},{24,8},{28,12},{1,17},{... | collective-permute-start | bytes 884744 | tf_op jit(solution)/shard_map/ppermute | solution.py:838
  22.6 23.6 %collective-permute-start.6 = (f32[504,128]{1,0:T(8,128)S(1)}, f32[504,128]{1,0:T(8,128)S(1)}, u32[]{:S(2)}, u32[]{:S(2)}) collective-permute-start(f32[504,128]{1,0:T(8,128)S(1)} %get-tuple-element.37.refs_1_), channel_id=1, source_target_pairs={{0,16},{4,20},{8,24},{12,28},{16,0},{20,4},{24,8},{28,12},{1,17},{... | collective-permute-start | bytes 774152 | tf_op jit(solution)/shard_map/ppermute | solution.py:838
  49.3 7.0 %collective-permute-start.7 = (f32[384,128]{1,0:T(8,128)S(1)}, f32[384,128]{1,0:T(8,128)S(1)}, u32[]{:S(2)}, u32[]{:S(2)}) collective-permute-start(f32[384,128]{1,0:T(8,128)S(1)} %get-tuple-element.42), channel_id=1, source_target_pairs={{0,4},{4,0},{8,12},{12,8},{16,20},{20,16},{24,28},{28,24},{1,5},{5... | collective-permute-start | bytes 589832 | tf_op jit(solution)/shard_map/ppermute | solution.py:838
  50.8 7.7 %collective-permute-start.8 = (f32[384,128]{1,0:T(8,128)S(1)}, f32[384,128]{1,0:T(8,128)S(1)}, u32[]{:S(2)}, u32[]{:S(2)}) collective-permute-start(f32[384,128]{1,0:T(8,128)S(1)} %get-tuple-element.43), channel_id=1, source_target_pairs={{0,8},{4,12},{8,0},{12,4},{16,24},{20,28},{24,16},{28,20},{1,9},{5... | collective-permute-start | bytes 589832 | tf_op jit(solution)/shard_map/ppermute | solution.py:838
  51.5 9.3 %collective-permute-start.9 = (f32[384,128]{1,0:T(8,128)S(1)}, f32[384,128]{1,0:T(8,128)S(1)}, u32[]{:S(2)}, u32[]{:S(2)}) collective-permute-start(f32[384,128]{1,0:T(8,128)S(1)} %get-tuple-element.44), channel_id=1, source_target_pairs={{0,12},{4,8},{8,4},{12,0},{16,28},{20,24},{24,20},{28,16},{1,13},{... | collective-permute-start | bytes 589832 | tf_op jit(solution)/shard_map/ppermute | solution.py:838

commit v4 on v3

--- a/solution.py
+++ b/solution.py
@@ -256,7 +256,7 @@
         and SWEEPS * GROUP <= GROUP * steps <= LANES
         and LANES % (GROUP * steps_dev) == 0
         and band_rows % 8 == 0
-        and band_rows >= 16
+        and band_rows >= 24
         and fields == FIELDS
     )
 
@@ -319,34 +319,24 @@
             at += 8
 
 
-def edge_kernel(width_tm, steps_dev, *refs):
+def place_initial(width_tm, initial_ref, _, tiles, side_initial):
+    fields, rows, _ = initial_ref.shape
+    mine = lax.axis_index("tm") & (width_tm // 2 - 1)
+    after, prior = side_places(mine, width_tm)
+    for f, c in EACH:
+        tiles[f, c] = initial_ref[f, :, tile_at(SLABS * mine + c)]
+    lane = lanes(rows)
+    for f in range(fields):
+        side_initial[f] = jnp.where(
+            lane < LANES // 2, initial_ref[f, :, after], initial_ref[f, :, prior]
+        )
+
+
+def edge_kernel(width_tm, *refs):
     half = width_tm // 2
-    pieces, initial_ref = refs[:half], refs[half]
-    up, down, side, side_initial = refs[half + 1 :]
-    fields, rows, _ = initial_ref.shape
-    me = lax.axis_index("tm")
-    mine = me & (half - 1)
-    lane = lanes()
-    owner = step_of_lane(lane) // steps_dev
-    blocks = rows // 8
-    per_word = LANES // (GROUP * steps_dev)
-    main = SLABS * steps_dev * fields * rows
-    after, prior = side_places(mine, width_tm)
-    for g in range(fields * blocks):
-        f, r = divmod(g, blocks)
-        word, place = divmod(g, per_word)
-        found = jnp.zeros((8, LANES), jnp.float32)
-        for b in range(half):
-            source = mine ^ b
-            value = pieces[b][main + 8 * word : main + 8 * word + 8, :]
-            shift = (GROUP * steps_dev * (source - place)) & (LANES - 1)
-            found = jnp.where(owner == source, pltpu.roll(value, shift, 1), found)
-        side[f, 8 * r : 8 * r + 8, :] = found
-        side_initial[f, 8 * r : 8 * r + 8, :] = jnp.where(
-            lane < LANES // 2,
-            initial_ref[f, 8 * r : 8 * r + 8, after],
-            initial_ref[f, 8 * r : 8 * r + 8, prior],
-        )
+    pieces, (tiles, side, side_initial, up, down) = refs[:half], refs[half:]
+    fields, rows, _ = side.shape
+    main = pieces[0].shape[0] // rows * rows
     for out, part in ((up, slice(0, HALO)), (down, slice(rows - HALO, rows))):
         k = 0
         for b in range(half):
@@ -355,7 +345,7 @@
                 k += HALO
         for c in range(SLABS):
             for f in range(fields):
-                out[k : k + HALO, :] = initial_ref[f, part, tile_at(SLABS * mine + c)]
+                out[k : k + HALO, :] = tiles[f, c, part, :]
                 k += HALO
         for held in (side, side_initial):
             for f in range(fields):
@@ -422,9 +412,9 @@
 
 
 class Side:
-    def __init__(self, rows):
-        self.tall = rows + 2 * HALO
-        self.span = slice(ROW0, ROW0 + self.tall)
+    def __init__(self, first, tall):
+        self.first, self.tall = first, tall
+        self.span = slice(first, first + tall)
         lane = lanes(self.tall)
         self.step = step_of_lane(lane)
         self.after = (lane & (GROUP - 1)) == 0
@@ -432,7 +422,7 @@
 
     def parts(self, held, ends):
         own, north, south = (
-            [held[f, ROW0 + d : ROW0 + d + self.tall, :] for f in range(FIELDS)] for d in (0, -1, 1)
+            [held[f, self.first + d : self.first + d + self.tall, :] for f in range(FIELDS)] for d in (0, -1, 1)
         )
         last = [ends[f, self.span, :] for f in range(FIELDS)]
         east = [jnp.where(self.before, turn(last[f], -1), turn(own[f], -1)) for f in range(FIELDS)]
@@ -458,14 +448,6 @@
     target = lax.broadcasted_iota(jnp.int32, (LANES, LANES), 1)
     same = ((source - target) & (GROUP - 1)) == 0
     return jnp.where(same, entry(step_of_lane(source), step_of_lane(target)), 0.0)
-
-
-def step_parts(held, n, start, seam):
-    lane = lanes()
-    load = lambda d: {k: held[n, k[0], k[1], pl.ds(start + d, 8), :] for k in EACH}
-    own, north, south = load(0), load(-1), load(1)
-    east, west = {}, {}
-    return own, east, west, north, south, lane
 
 
 def neighbours(held, slot, start, seam, n):
@@ -525,11 +507,59 @@
             send(SWEEPS - 1 - j, f, c, value)
 
 
+PER_WORD = LANES // (SWEEPS * GROUP)
+
+
+def pack_sides(blocks, sent, at):
+    kind = step_of_lane(lanes()) // SWEEPS
+    for first in range(0, len(blocks), PER_WORD):
+        word = jnp.zeros((8, LANES), jnp.float32)
+        for k, block in enumerate(blocks[first : first + PER_WORD]):
+            word = jnp.where(kind == k, turn(block, SWEEPS * GROUP * k), word)
+        sent[at : at + 8, :] = word
+        at += 8
+
+
+def unpack_side(sent, at, index):
+    word, k = divmod(index, PER_WORD)
+    value = turn(sent[at + 8 * word : at + 8 * word + 8, :], -SWEEPS * GROUP * k)
+    return jnp.where(step_of_lane(lanes()) < SWEEPS, value, 0.0)
+
+
+def side_residual(sides, steps, first_half, hstate, ends, before_first, hrhs):
+    parts = sides.parts(hstate, ends)
+    value = full_tendency(*parts)
+    growth = jnp.where(
+        sides.step < steps, jnp.exp(sides.step.astype(jnp.float32) * math.log(SHIFT)), 0.0
+    )
+    held = []
+    for f in range(FIELDS):
+        first = jnp.where(first_half, before_first(f), 0.0)
+        before = jnp.where(sides.step == 0, first, turn(parts[0][f], GROUP))
+        held.append((value[f] - before) * growth)
+        hrhs[f, sides.span, :] = held[f]
+
+    def entry(source, target):
+        result = jnp.zeros((LANES, LANES), jnp.float32)
+        for p in range(SWEEPS):
+            j = SWEEPS - p
+            for n in range(steps):
+                weight = RATE ** (steps - 1 + j) * binomial(steps - 1 - n + j - 1, j - 1)
+                result = jnp.where((target == p) & (source == n), weight, result)
+        return result
+
+    handed = sides.product(held, lane_matrix(entry))
+    for f in range(FIELDS):
+        last = turn(parts[0][f], GROUP * (SWEEPS - steps))
+        handed[f] = handed[f] - jnp.where(first_half & (sides.step == SWEEPS - 1), last, 0.0)
+    return handed
+
+
 def inner_kernel(width_tm, steps_dev, *refs):
     half = width_tm // 2
-    pieces, (initial_ref, side) = refs[:half], refs[half : half + 2]
-    state, rhs, ends, sent, seams = refs[half + 2 :]
-    fields, rows, _ = initial_ref.shape
+    pieces, (tiles, side_initial) = refs[:half], refs[half : half + 2]
+    state, rhs, ends, hrhs, side, sent, seams, hstate = refs[half + 2 :]
+    fields, rows, _ = side.shape
     steps = half * steps_dev
     me = lax.axis_index("tm")
     mine = me & (half - 1)
@@ -544,24 +574,43 @@
                     state[n + 1, f, c, body, :] = pieces[b][at : at + rows, :]
                     at += rows
     for f, c in EACH:
-        state[0, f, c, body, :] = jnp.where(first_half, initial_ref[f, :, tile_at(SLABS * mine + c)], 0.0)
-    lane = lanes(rows)
-    after = (lane & (GROUP - 1)) == 0
-    for f in range(fields):
-        seams[f, body, :] = jnp.where(after, turn(side[f], 1), turn(side[f], -1))
-
-    @pl.loop(1, rows // 8)
+        state[0, f, c, body, :] = jnp.where(first_half, tiles[f, c], 0.0)
+    owner = step_of_lane(lanes()) // steps_dev
+    blocks = rows // 8
+    per_word = LANES // (GROUP * steps_dev)
+    main = SLABS * steps_dev * fields * rows
+    for g in range(fields * blocks):
+        f, r = divmod(g, blocks)
+        word, place = divmod(g, per_word)
+        found = jnp.zeros((8, LANES), jnp.float32)
+        for b in range(half):
+            source = mine ^ b
+            value = pieces[b][main + 8 * word : main + 8 * word + 8, :]
+            shift = (GROUP * steps_dev * (source - place)) & (LANES - 1)
+            found = jnp.where(owner == source, pltpu.roll(value, shift, 1), found)
+        side[f, 8 * r : 8 * r + 8, :] = found
+        hstate[f, MAIN + 8 * r : MAIN + 8 * r + 8, :] = found
+    Side(MAIN, rows).set_seams(seams, [side[f] for f in range(fields)])
+
+    @pl.loop(1, blocks)
     def _(t):
         def send(p, f, c, value):
-            sent[p, f, c, pl.ds(pl.multiple_of(8 * t - 8, 8), 8), :] = value
+            at = ((p * FIELDS + f) * SLABS + c) * (rows - 8) + 8 * t - 8
+            sent[pl.ds(pl.multiple_of(at, 8), 8), :] = value
 
         residual_tile(steps, first_half, ROW0 + 8 * t, state, rhs, seams, ends, send)
+
+    sides = Side(ROW0 + 8, rows - 8)
+    before_first = lambda f: side_initial[f, HALO : rows - HALO, :]
+    handed = side_residual(sides, steps, first_half, hstate, ends, before_first, hrhs)
+    flat = [handed[f][at : at + 8, :] for f in range(FIELDS) for at in range(0, rows - 8, 8)]
+    pack_sides(flat, sent, SWEEPS * FIELDS * SLABS * (rows - 8))
 
 
 def outer_kernel(width_tm, steps_dev, rows, *refs):
     half = width_tm // 2
-    side, side_initial, above, below = refs[3:7]
-    state, rhs, ends, hrhs, sent, hstate, hbefore, seams = refs[7:]
+    side, side_initial, above, below = refs[4:8]
+    state, rhs, ends, hrhs, sent, hstate, hbefore, seams = refs[8:]
     steps = half * steps_dev
     me = lax.axis_index("tm")
     mine = me & (half - 1)
@@ -588,47 +637,25 @@
             held[f, top, :] = above[k : k + HALO, :]
             held[f, bottom, :] = below[k : k + HALO, :]
             k += HALO
-    sides = Side(rows)
-    sides.set_seams(seams, [hstate[f, sides.span, :] for f in range(FIELDS)])
-    main = SWEEPS * FIELDS * SLABS * 16
+    whole = Side(ROW0, rows + 2 * HALO)
+    whole.set_seams(seams, [hstate[f, whole.span, :] for f in range(FIELDS)])
+    flat = []
     for which, start in enumerate((ROW0, ROW0 + rows)):
 
         def send(p, f, c, value):
-            at = ((p * FIELDS + f) * SLABS + c) * 16 + 8 * which
-            sent[at : at + 8, :] = value
+            at = (((p * FIELDS + f) * SLABS + c) * 2 + which) * 7
+            sent[at : at + 7, :] = value[1 - which : 8 - which, :]
 
         residual_tile(steps, first_half, start, state, rhs, seams, ends, send)
-    parts = sides.parts(hstate, ends)
-    value = full_tendency(*parts)
-    growth = jnp.where(
-        sides.step < steps, jnp.exp(sides.step.astype(jnp.float32) * math.log(SHIFT)), 0.0
-    )
-    held = []
-    for f in range(FIELDS):
-        first = jnp.where(first_half, hbefore[f, sides.span, :], 0.0)
-        before = jnp.where(sides.step == 0, first, turn(parts[0][f], GROUP))
-        held.append((value[f] - before) * growth)
-        hrhs[f, sides.span, :] = held[f]
-
-    def entry(source, target):
-        result = jnp.zeros((LANES, LANES), jnp.float32)
-        for p in range(SWEEPS):
-            j = SWEEPS - p
-            for n in range(steps):
-                weight = RATE ** (steps - 1 + j) * binomial(steps - 1 - n + j - 1, j - 1)
-                result = jnp.where((target == p) & (source == n), weight, result)
-        return result
-
-    handed = sides.product(held, lane_matrix(entry))
-    for f in range(FIELDS):
-        last = turn(parts[0][f], GROUP * (SWEEPS - steps))
-        last = jnp.where(first_half & (sides.step == SWEEPS - 1), last, 0.0)
-        sent[main + sides.tall * f : main + sides.tall * (f + 1), :] = handed[f] - last
+        sides = Side(start, 8)
+        before_first = lambda f: hbefore[f, start : start + 8, :]
+        flat += side_residual(sides, steps, first_half, hstate, ends, before_first, hrhs)
+    pack_sides(flat, sent, SWEEPS * FIELDS * SLABS * 14)
 
 
 def chain_kernel(steps, rows, rhs, hrhs, result, ya, yb, hya, hyb, ends, seams):
     _, ratios, _ = chain_factors()
-    sides = Side(rows)
+    sides = Side(ROW0, rows + 2 * HALO)
     blocks = sides.tall // 8
     running = lane_matrix(
         lambda source, target: jnp.where((source <= target) & (target < steps), 1.0, 0.0)
@@ -690,70 +717,81 @@
         sweep(ratios[m - 1], *old, result if final else new[0], new[1], final)
 
 
-def join_kernel(width_tm, steps_dev, rows, *refs):
+def join_kernel(width_tm, steps_dev, rows, inner_rows, *refs):
     half = width_tm // 2
-    inner_own, outer_own, inner_other, outer_other, chained, state = refs[:6]
-    outs = refs[6 : 6 + half]
-    given, pa, pb, hgiven, hpa, hpb, ends, seams, result = refs[6 + half :]
+    count = 2 if inner_rows else 4
+    given_refs, (chained, state) = refs[:count], refs[count : count + 2]
+    outs = refs[-9 - half : -9]
+    given, pa, pb, hgiven, hpa, hpb, ends, seams, result = refs[-9:]
+    inner_own, inner_other = given_refs[:2]
     steps = half * steps_dev
     me = lax.axis_index("tm")
     mine = me & (half - 1)
     gammas, _, scale = chain_factors()
     own, first, second = swap_factors(steps)
     other = [jnp.where(me < half, a, b) for a, b in zip(first, second)]
-    sides = Side(rows)
-    blocks = sides.tall // 8
-    middle = slice(ROW0 + 8, ROW0 + rows)
-    main = SWEEPS * FIELDS * SLABS * 16
-
-    def joined(pick_own, pick_other, p):
+    tiles = rows // 8
+    if inner_rows:
+        sides = Side(ROW0 + 8, rows - 8)
+        places = (tiles - 1, lambda t: ROW0 + 8 + 8 * t)
+        finals = (tiles - 2, lambda t: MAIN + 8 + 8 * t)
+    else:
+        sides = Side(ROW0, rows + 2 * HALO)
+        places = (4, lambda t: ROW0 + 8 * (t + (tiles - 3) * (t // 2)))
+        finals = (2, lambda t: MAIN + (rows - 8) * t)
+    cells = SWEEPS * FIELDS * SLABS
+
+    def joined(ref_own, ref_other, at, size, step, p):
         total = None
         for d in range(SWEEPS - p):
-            term = other[d] * pick_other(p + d) + own[d] * pick_own(p + d)
+            rows_d = slice(at + step * d, at + step * d + size)
+            term = other[d] * ref_other[rows_d, :] + own[d] * ref_own[rows_d, :]
             total = term if total is None else total + term
         return total
 
-    for f, c in EACH:
-        for p in range(SWEEPS):
-            value = joined(lambda k: inner_own[k, f, c], lambda k: inner_other[k, f, c], p)
-            given[p, f, c, middle, :] = value
-            pa[p, f, c, middle, :] = gammas[-1] * value
-            for which, start in enumerate((ROW0, ROW0 + rows)):
-
-                def pick(ref, k):
-                    at = ((k * FIELDS + f) * SLABS + c) * 16 + 8 * which
-                    return ref[at : at + 8, :]
-
-                value = joined(lambda k: pick(outer_own, k), lambda k: pick(outer_other, k), p)
-                given[p, f, c, start : start + 8, :] = value
-                pa[p, f, c, start : start + 8, :] = gammas[-1] * value
-
-    def from_later(value, d):
-        return jnp.where(sides.step < SWEEPS - d, turn(value, -GROUP * d), 0.0)
-
-    side_new = []
+    for p in range(SWEEPS):
+        for f, c in EACH:
+            cell = (p * FIELDS + f) * SLABS + c
+            found = [(ROW0 + 8, joined(inner_own, inner_other, cell * (rows - 8), rows - 8, FIELDS * SLABS * (rows - 8), p))]
+            if not inner_rows:
+                for which, start in ((0, ROW0 + 1), (1, ROW0 + rows)):
+                    at = (cell * 2 + which) * 7
+                    found.append((start, joined(*given_refs[2:], at, 7, FIELDS * SLABS * 14, p)))
+            for start, value in found:
+                given[p, f, c, start : start + value.shape[0], :] = value
+                pa[p, f, c, start : start + value.shape[0], :] = gammas[-1] * value
+
+    step8 = step_of_lane(lanes())
+
+    def from_later(value, d, step):
+        return jnp.where(step < SWEEPS - d, turn(value, -GROUP * d), 0.0)
+
+    def set_side(refs_side, at, index, f, start):
+        ours, theirs = (unpack_side(ref, at, index) for ref in refs_side)
+        value = jnp.zeros((8, LANES), jnp.float32)
+        for d in range(SWEEPS):
+            value = value + from_later(other[d] * theirs + own[d] * ours, d, step8)
+        hgiven[f, start : start + 8, :] = value
+        hpa[f, start : start + 8, :] = gammas[-1] * value
+
     for f in range(FIELDS):
-        rows_f = slice(main + sides.tall * f, main + sides.tall * (f + 1))
-        value = jnp.zeros((sides.tall, LANES), jnp.float32)
-        for d in range(SWEEPS):
-            value = value + from_later(
-                other[d] * outer_other[rows_f, :] + own[d] * outer_own[rows_f, :], d
-            )
-        hgiven[f, sides.span, :] = value
-        side_new.append(gammas[-1] * value)
-        hpa[f, sides.span, :] = side_new[f]
-    sides.set_seams(seams, side_new)
+        for r in range(tiles - 1):
+            set_side(given_refs[:2], cells * (rows - 8), f * (tiles - 1) + r, f, ROW0 + 8 + 8 * r)
+        if not inner_rows:
+            for which, start in ((0, ROW0), (1, ROW0 + rows)):
+                set_side(given_refs[2:], cells * 14, which * FIELDS + f, f, start)
+    sides.set_seams(seams, [hpa[f, sides.span, :] for f in range(FIELDS)])
 
     buffers = [(pa, hpa), (pb, hpb)]
     for k in range(1, SWEEPS):
         (old, hold), (new, hnew) = buffers[(k + 1) % 2], buffers[k % 2]
         gamma = gammas[SWEEPS - 1 - k]
         final = k == SWEEPS - 1
-        first_row = MAIN if final else ROW0
-
-        @pl.loop(0, rows // 8 if final else blocks)
+        turns, place = finals if final else places
+
+        @pl.loop(0, turns)
         def _(t):
-            start = first_row + 8 * t
+            start = place(t)
             here = pl.ds(start, 8)
             seam = [seams[f, here, :] for f in range(FIELDS)]
             last = zeros(FIELDS)
@@ -777,9 +815,10 @@
                     ends[f, here, :] = last[f]
             else:
                 at = pl.ds(pl.multiple_of(8 * t, 8), 8)
+                from_chain = pl.ds(pl.multiple_of(start - MAIN, 8), 8)
                 for f, c in EACH:
                     for n in range(steps):
-                        total = scale * chained[n, f, c, at, :]
+                        total = scale * chained[n, f, c, from_chain, :]
                         for p in range(SWEEPS):
                             total = total + binomial(n + p, p) * found[p, f, c]
                         result[n, f, c, at, :] = state[n + 1, f, c, here, :] - total * RATE**n
@@ -787,44 +826,52 @@
         if not final:
             value = off_diagonal(*sides.parts(hold, ends))
             side_next = [
-                value[f] + gamma * from_later(hgiven[f, sides.span, :], k) for f in range(FIELDS)
+                value[f] + gamma * from_later(hgiven[f, sides.span, :], k, sides.step)
+                for f in range(FIELDS)
             ]
             for f in range(FIELDS):
                 hnew[f, sides.span, :] = side_next[f]
             sides.set_seams(seams, side_next)
 
+    size = 8 * finals[0]
     for b in range(half):
         at = 0
         for c in range(SLABS):
             for i in range(steps_dev):
                 n = steps_dev * (mine ^ b) + i
                 for f in range(FIELDS):
-                    outs[b][at : at + rows, :] = result[n, f, c, :, :]
-                    at += rows
+                    outs[b][at : at + size, :] = result[n, f, c, :, :]
+                    at += size
 
 
 def unpack_kernel(width_tm, *refs):
     half = width_tm // 2
-    pieces, out = refs[:half], refs[half]
+    inner, outer, out = refs[:half], refs[half : 2 * half], refs[2 * half]
     steps_dev, fields, rows, _ = out.shape
     mine = lax.axis_index("tm") & (half - 1)
+    size = rows - 16
     for b in range(half):
-        at = 0
+        k = 0
         for c in range(SLABS):
+            here = tile_at(SLABS * (mine ^ b) + c)
             for i in range(steps_dev):
                 for f in range(fields):
-                    out[i, f, :, tile_at(SLABS * (mine ^ b) + c)] = pieces[b][at : at + rows, :]
-                    at += rows
-
-
-def call(kernel, out_shapes, operands, scratch=(), aliases=None):
+                    out[i, f, 8 : rows - 8, here] = inner[b][size * k : size * (k + 1), :]
+                    out[i, f, 0:8, here] = outer[b][16 * k : 16 * k + 8, :]
+                    out[i, f, rows - 8 : rows, here] = outer[b][16 * k + 8 : 16 * k + 16, :]
+                    k += 1
+
+
+def call(kernel, out_shapes, operands, scratch=(), aliases=None, after=()):
     whole = pl.BlockSpec(memory_space=pltpu.VMEM)
     shapes = [jax.ShapeDtypeStruct(shape, jnp.float32) for shape in out_shapes]
     moved = 4 * sum(math.prod(x.shape) for x in list(shapes) + list(operands))
+    in_specs = [whole] * len(operands) + [pl.BlockSpec(memory_space=pl.ANY)] * len(after)
+    operands = list(operands) + list(after)
     return pl.pallas_call(
         kernel,
         out_shape=shapes,
-        in_specs=[whole] * len(operands),
+        in_specs=in_specs,
         out_specs=[whole] * len(shapes),
         scratch_shapes=[pltpu.VMEM(shape, jnp.float32) for shape in scratch],
         input_output_aliases=aliases or {},
@@ -852,31 +899,44 @@
         functools.partial(pack_kernel, width_tm), [(main + 8 * words, LANES)] * half, [state]
     )
     pieces = [pieces[0]] + [swap(pieces[b], b) for b in range(1, half)]
+    tiles, side_initial = call(
+        functools.partial(place_initial, width_tm),
+        [(fields, SLABS, rows, LANES), (fields, rows, LANES)],
+        [initial],
+        after=pieces[:1],
+    )
+    flat = (fields, tall, LANES)
+    held_shapes = [
+        (steps + 1, fields, SLABS, tall, LANES),
+        (steps, fields, SLABS, tall, LANES),
+        flat,
+        flat,
+    ]
+    cells = SWEEPS * fields * SLABS
+    inner_words = -(-fields * (rows - 8) // 8 // PER_WORD)
+    outer_words = -(-2 * fields // PER_WORD)
+    *held, side, inner = call(
+        functools.partial(inner_kernel, *sized),
+        held_shapes
+        + [(fields, rows, LANES), (cells * (rows - 8) + 8 * inner_words, LANES)],
+        pieces + [tiles, side_initial],
+        [flat] * 2,
+    )
+    inner_other = swap(inner, half)
     edge_rows = -(-HALO * fields * (SLABS * (steps + 1) + 2) // 8) * 8
-    up, down, side, side_initial = call(
-        functools.partial(edge_kernel, *sized),
-        [(edge_rows, LANES)] * 2 + [(fields, rows, LANES)] * 2,
-        pieces + [initial],
+    up, down = call(
+        functools.partial(edge_kernel, width_tm),
+        [(edge_rows, LANES)] * 2,
+        pieces + [tiles, side, side_initial],
     )
     above = lax.ppermute(down, "space", [(i, (i + 1) % bands) for i in range(bands)])
     below = lax.ppermute(up, "space", [((i + 1) % bands, i) for i in range(bands)])
-    flat = (fields, tall, LANES)
-    held = [(steps + 1, fields, SLABS, tall, LANES), (steps, fields, SLABS, tall, LANES), flat]
-    held_shapes = held
-    *held, inner = call(
-        functools.partial(inner_kernel, *sized),
-        held_shapes + [(SWEEPS, fields, SLABS, rows - 8, LANES)],
-        pieces + [initial, side],
-        [flat],
-    )
-    inner_other = swap(inner, half)
-    tall_rows = rows + 2 * HALO
     solved, rhs, _, hrhs, outer = call(
         functools.partial(outer_kernel, *sized, rows),
-        held_shapes + [flat, (SWEEPS * fields * SLABS * 16 + fields * tall_rows, LANES)],
+        held_shapes + [(cells * 14 + 8 * outer_words, LANES)],
         held + [side, side_initial, above, below],
         [flat] * 3,
-        aliases={0: 0, 1: 1, 2: 2},
+        aliases={0: 0, 1: 1, 2: 2, 3: 3},
     )
     outer_other = swap(outer, half)
     (chained,) = call(
@@ -886,13 +946,19 @@
         [held_shapes[1]] * 2 + [flat] * 4,
     )
     four = (SWEEPS, fields, SLABS, tall, LANES)
-    results = call(
-        functools.partial(join_kernel, *sized, rows),
-        [(main, LANES)] * half,
-        [inner, outer, inner_other, outer_other, chained, solved],
-        [four] * 3 + [flat] * 5 + [(steps, fields, SLABS, rows, LANES)],
-    )
-    results = [results[0]] + [swap(results[b], b) for b in range(1, half)]
+    results = []
+    for given, size in (
+        ([inner, inner_other], rows - 16),
+        ([inner, inner_other, outer, outer_other], 16),
+    ):
+        parts = call(
+            functools.partial(join_kernel, *sized, rows, len(given) == 2),
+            [(SLABS * steps_dev * fields * size, LANES)] * half,
+            given + [chained, solved],
+            [four] * 3 + [flat] * 5 + [(steps, fields, SLABS, size, LANES)],
+            after=results[:1],
+        )
+        results += [parts[0]] + [swap(parts[b], b) for b in range(1, half)]
     (updated,) = call(functools.partial(unpack_kernel, width_tm), [state.shape], results)
     return updated
 

time: 61.9 us -> 53.3 us (0.86)
  waiting for transfers between devices: 34.3 us -> 22.1 us
  starting transfers between devices: 14.8 us -> 16.7 us
  Pallas kernels: 10.4 us -> 12.1 us
    ppermute x8 -> x11, waiting for transfers between devices: 34.3 us -> 19.2 us  [swap(): return lax.ppermute(piece, 'tm', [(k, k ^ b) for k in range(count)])]
    ppermute x1, waiting for transfers between devices: 0.01 us -> 2.56 us  [fast_on_device(): lax.ppermute(down, 'space', [(i, (i + 1) % bands) for i in range(bands)])]
    ppermute x8 -> x11, starting transfers between devices: 13 us -> 14.9 us  [swap(): return lax.ppermute(piece, 'tm', [(k, k ^ b) for k in range(count)])]
    pallas_call x7 -> x9, Pallas kernels: 10.4 us -> 12.1 us  [call(): pl.pallas_call(kernel, out_shape=shapes, in_specs=in_specs, out_specs=[wh...]
  transfers between devices with their start and end apart: 10 -> 13, of which waited for: 8 -> 9; matrix products, arithmetic and copies ran while one was open for 0% -> 0% of each run, Pallas kernels for 10% -> 18%
where the time goes in v4:
time: 53.3 us; the launch traced here: 53.1 us
  waiting for transfers between devices  22.1 us (41%)
  starting transfers between devices  16.7 us (31%)
  Pallas kernels  12.1 us (23%)
  local copies, waits for them, and re-layouts  2.13 us (4%)
    ppermute x11, waiting for transfers between devices, swap(): return lax.ppermute(piece, 'tm', [(k, k ^ b) for k in range(count)])  19.2 us
    ppermute x11, starting transfers between devices, swap(): return lax.ppermute(piece, 'tm', [(k, k ^ b) for k in range(count)])  14.9 us
    pallas_call x9, Pallas kernels, call(): pl.pallas_call(kernel, out_shape=shapes, in_specs=in_specs, out_specs=[wh...  12.1 us
    ppermute x1, waiting for transfers between devices, fast_on_device(): lax.ppermute(down, 'space', [(i, (i + 1) % bands) for i in range(bands)])  2.56 us
    unnamed x4, local copies, waits for them, and re-layouts  2.13 us
    ppermute x1, starting transfers between devices, fast_on_device(): lax.ppermute(up, 'space', [((i + 1) % bands, i) for i in range(bands)])  1.73 us
  transfers between devices with their start and end apart: 13, of which 9 were waited for; matrix products, arithmetic and copies ran while one was open for 0% of the time, Pallas kernels for 18%

profile of v4, /device:TPU:0, one launch (start us, length us, event | category | flops | bytes accessed | tf_op | source)
XLA Modules:
  0.0 53.1 jit_solution(10804807155293127329)
XLA Ops:
  0.0 1.1 %copy-done = f32[2,3,32,1024]{3,2,1,0:T(8,128)S(1)} copy-done((f32[2,3,32,1024]{3,2,1,0:T(8,128)S(1)}, f32[2,3,32,1024]{3,2,1,0:T(8,128)}, u32[]{:S(2)}) %copy-start) | copy-done | bytes 786456
  1.1 0.3 shard_map.28
  1.4 3.0 %collective-permute-start = (f32[400,128]{1,0:T(8,128)S(1)}, f32[400,128]{1,0:T(8,128)S(1)}, u32[]{:S(2)}, u32[]{:S(2)}) collective-permute-start(f32[400,128]{1,0:T(8,128)S(1)} %get-tuple-element.32), channel_id=1, source_target_pairs={{0,4},{4,0},{8,12},{12,8},{16,20},{20,16},{24,28},{28,24},{1,5},{5... | collective-permute-start | bytes 614408 | tf_op jit(solution)/shard_map/ppermute | solution.py:885
  4.4 1.6 %collective-permute-start.1 = (f32[400,128]{1,0:T(8,128)S(1)}, f32[400,128]{1,0:T(8,128)S(1)}, u32[]{:S(2)}, u32[]{:S(2)}) collective-permute-start(f32[400,128]{1,0:T(8,128)S(1)} %get-tuple-element.33), channel_id=1, source_target_pairs={{0,8},{4,12},{8,0},{12,4},{16,24},{20,28},{24,16},{28,20},{1,9},{5... | collective-permute-start | bytes 614408 | tf_op jit(solution)/shard_map/ppermute | solution.py:885
  6.0 0.0 collective-permute-start.2
  6.0 1.0 %copy-done.1 = f32[3,32,1024]{2,1,0:T(8,128)S(1)} copy-done((f32[3,32,1024]{2,1,0:T(8,128)S(1)}, f32[3,32,1024]{2,1,0:T(8,128)}, u32[]{:S(2)}) %copy-start.1) | copy-done | bytes 393240
  7.0 2.5 %collective-permute-done.refs_1_ = f32[400,128]{1,0:T(8,128)S(1)} collective-permute-done((f32[400,128]{1,0:T(8,128)S(1)}, f32[400,128]{1,0:T(8,128)S(1)}, u32[]{:S(2)}, u32[]{:S(2)}) %collective-permute-start) | collective-permute-done | bytes 204832 | tf_op jit(solution)/shard_map/ppermute | solution.py:885
  9.5 2.9 %collective-permute-done.1.refs_2_ = f32[400,128]{1,0:T(8,128)S(1)} collective-permute-done((f32[400,128]{1,0:T(8,128)S(1)}, f32[400,128]{1,0:T(8,128)S(1)}, u32[]{:S(2)}, u32[]{:S(2)}) %collective-permute-start.1) | collective-permute-done | bytes 204832 | tf_op jit(solution)/shard_map/ppermute | solution.py:885
  12.4 2.7 %collective-permute-done.2.refs_3_ = f32[400,128]{1,0:T(8,128)S(1)} collective-permute-done((f32[400,128]{1,0:T(8,128)S(1)}, f32[400,128]{1,0:T(8,128)S(1)}, u32[]{:S(2)}, u32[]{:S(2)}) %collective-permute-start.2) | collective-permute-done | bytes 204832 | tf_op jit(solution)/shard_map/ppermute | solution.py:885
  15.2 1.5 %shard_map.30 = (f32[9,3,2,56,128]{4,3,2,1,0:T(8,128)S(1)}, f32[8,3,2,56,128]{4,3,2,1,0:T(8,128)S(1)}, f32[3,56,128]{2,1,0:T(8,128)S(1)}, f32[3,56,128]{2,1,0:T(...) custom-call(f32[400,128]{1,0:T(8,128)S(1)} %get-tuple-element.31._.refs_0_, ...), custom_call_target="tpu_custom_call" | custom-call | flops 4419584 | bytes 4419584 | tf_op jit(solution)/shard_map/pallas_call | solution.py:871
  16.6 2.8 %collective-permute-start.3 = (f32[600,128]{1,0:T(8,128)S(1)}, f32[600,128]{1,0:T(8,128)S(1)}, u32[]{:S(2)}, u32[]{:S(2)}) collective-permute-start(f32[600,128]{1,0:T(8,128)S(1)} %get-tuple-element.37.refs_0_), channel_id=1, source_target_pairs={{0,16},{4,20},{8,24},{12,28},{16,0},{20,4},{24,8},{28,12},{1,17},{... | collective-permute-start | bytes 921608 | tf_op jit(solution)/shard_map/ppermute | solution.py:885
  19.5 0.1 collective-permute-start.4
  19.5 1.7 %collective-permute-start.5 = (f32[240,128]{1,0:T(8,128)S(1)}, f32[240,128]{1,0:T(8,128)S(1)}, u32[]{:S(2)}, u32[]{:S(2)}) collective-permute-start(f32[240,128]{1,0:T(8,128)S(1)} %get-tuple-element.44), channel_id=1, source_target_pairs={{1,0},{2,1},{3,2},{0,3},{5,4},{6,5},{7,6},{4,7},{9,8},{10,9},{11,1... | collective-permute-start | bytes 368648 | tf_op jit(solution)/shard_map/ppermute | solution.py:933
  21.3 2.6 %collective-permute-done.4.refs_6_ = f32[240,128]{1,0:T(8,128)S(1)} collective-permute-done((f32[240,128]{1,0:T(8,128)S(1)}, f32[240,128]{1,0:T(8,128)S(1)}, u32[]{:S(2)}, u32[]{:S(2)}) %collective-permute-start.4) | collective-permute-done | bytes 122912 | tf_op jit(solution)/shard_map/ppermute | solution.py:932
  23.8 0.4 collective-permute-done.5.refs_7_
  24.2 0.7 %shard_map.32 = (f32[9,3,2,56,128]{4,3,2,1,0:T(8,128)S(1)}, f32[8,3,2,56,128]{4,3,2,1,0:T(8,128)S(1)}, f32[3,56,128]{2,1,0:T(8,128)S(1)}, f32[3,56,128]{2,1,0:T(8,128)S(1)}, f32[352,128]{1,0:T(8,128)S(1)}) custom-call(f32[9,3,2,56,128]{4,3,2,1,0:T(8,128)S(1)} %get-tuple-element.38.refs_0_, ...), custom_call_target="tpu_custom_call", output_to_operand_aliasing={{0}: (0, {}), {1}: (1, {}), {2}: (2, {}), {3}: (3, {})} | custom-call | flops 6717440 | bytes 6717440 | tf_op jit(solution)/shard_map/pallas_call | solution.py:871
  24.9 0.4 collective-permute-start.9
  25.3 4.4 %shard_map.33.refs_2_.refs_4_ = f32[8,3,2,32,128]{4,3,2,1,0:T(8,128)S(1)} custom-call(f32[8,3,2,56,128]{4,3,2,1,0:T(8,128)S(1)} %get-tuple-element.45.rhs, f32[3,56,128]{2,1,0:T(8,128)S(1)} %get-tuple-element.46.hrhs), custom_call_target="tpu_custom_call" | custom-call | flops 2248704 | bytes 2248704 | tf_op jit(solution)/shard_map/pallas_call | solution.py:871
  29.7 7.5 %collective-permute-done.3.refs_1_ = f32[600,128]{1,0:T(8,128)S(1)} collective-permute-done((f32[600,128]{1,0:T(8,128)S(1)}, f32[600,128]{1,0:T(8,128)S(1)}, u32[]{:S(2)}, u32[]{:S(2)}) %collective-permute-start.3) | collective-permute-done | bytes 307232 | tf_op jit(solution)/shard_map/ppermute | solution.py:885
  37.2 1.9 %shard_map.34 = (f32[192,128]{1,0:T(8,128)S(1)}, f32[192,128]{1,0:T(8,128)S(1)}, f32[192,128]{1,0:T(8,128)S(1)}, f32[192,128]{1,0:T(8,128)S(1)}) custom-call(f32[600,128]{1,0:T(8,128)S(1)} %get-tuple-element.37.refs_0_, f32[600,128]{1,0:T(8,128)S(1)} %collective-permute-done.3.refs_1_, f32[8,3,2,32,128]{4,3,2,1,0:T(8,128)S(1)} %shard_map.33.refs_2_.refs_4_, ...), custom_call_target="tpu_custom_call" | custom-call | flops 3342336 | bytes 3342336 | tf_op jit(solution)/shard_map/pallas_call | solution.py:871
  39.0 1.6 %collective-permute-start.6 = (f32[192,128]{1,0:T(8,128)S(1)}, f32[192,128]{1,0:T(8,128)S(1)}, u32[]{:S(2)}, u32[]{:S(2)}) collective-permute-start(f32[192,128]{1,0:T(8,128)S(1)} %get-tuple-element.49), channel_id=1, source_target_pairs={{0,4},{4,0},{8,12},{12,8},{16,20},{20,16},{24,28},{28,24},{1,5},{5... | collective-permute-start | bytes 294920 | tf_op jit(solution)/shard_map/ppermute | solution.py:885
  40.6 2.0 %collective-permute-start.8 = (f32[192,128]{1,0:T(8,128)S(1)}, f32[192,128]{1,0:T(8,128)S(1)}, u32[]{:S(2)}, u32[]{:S(2)}) collective-permute-start(f32[192,128]{1,0:T(8,128)S(1)} %get-tuple-element.51), channel_id=1, source_target_pairs={{0,12},{4,8},{8,4},{12,0},{16,28},{20,24},{24,20},{28,16},{1,13},{... | collective-permute-start | bytes 294920 | tf_op jit(solution)/shard_map/ppermute | solution.py:885
  42.6 0.0 collective-permute-done.9.refs_3_
  42.6 2.3 %shard_map.35 = (f32[192,128]{1,0:T(8,128)S(1)}, f32[192,128]{1,0:T(8,128)S(1)}, f32[192,128]{1,0:T(8,128)S(1)}, f32[192,128]{1,0:T(8,128)S(1)}) custom-call(f32[600,128]{1,0:T(8,128)S(1)} %get-tuple-element.37.refs_0_, f32[600,128]{1,0:T(8,128)S(1)} %collective-permute-done.3.refs_1_, f32[352,128]{1,0:T(8,128)S(1)} %get-tuple-element.52.refs_2_, ...), custom_call_target="tpu_custom_call" | custom-call | flops 3702784 | bytes 3702784 | tf_op jit(solution)/shard_map/pallas_call | solution.py:871
  44.9 1.6 %collective-permute-start.10 = (f32[192,128]{1,0:T(8,128)S(1)}, f32[192,128]{1,0:T(8,128)S(1)}, u32[]{:S(2)}, u32[]{:S(2)}) collective-permute-start(f32[192,128]{1,0:T(8,128)S(1)} %get-tuple-element.54), channel_id=1, source_target_pairs={{0,4},{4,0},{8,12},{12,8},{16,20},{20,16},{24,28},{28,24},{1,5},{5... | collective-permute-start | bytes 294920 | tf_op jit(solution)/shard_map/ppermute | solution.py:885
  46.5 0.0 collective-permute-start.11
  46.5 2.0 %collective-permute-start.12 = (f32[192,128]{1,0:T(8,128)S(1)}, f32[192,128]{1,0:T(8,128)S(1)}, u32[]{:S(2)}, u32[]{:S(2)}) collective-permute-start(f32[192,128]{1,0:T(8,128)S(1)} %get-tuple-element.56), channel_id=1, source_target_pairs={{0,12},{4,8},{8,4},{12,0},{16,28},{20,24},{24,20},{28,16},{1,13},{... | collective-permute-start | bytes 294920 | tf_op jit(solution)/shard_map/ppermute | solution.py:885
  48.5 0.0 collective-permute-done.7.refs_2_
  48.5 1.7 %collective-permute-done.10.refs_5_ = f32[192,128]{1,0:T(8,128)S(1)} collective-permute-done((f32[192,128]{1,0:T(8,128)S(1)}, f32[192,128]{1,0:T(8,128)S(1)}, u32[]{:S(2)}, u32[]{:S(2)}) %collective-permute-start.10) | collective-permute-done | bytes 98336 | tf_op jit(solution)/shard_map/ppermute | solution.py:885
  50.2 0.9 %collective-permute-done.11.refs_6_ = f32[192,128]{1,0:T(8,128)S(1)} collective-permute-done((f32[192,128]{1,0:T(8,128)S(1)}, f32[192,128]{1,0:T(8,128)S(1)}, u32[]{:S(2)}, u32[]{:S(2)}) %collective-permute-start.11) | collective-permute-done | bytes 98336 | tf_op jit(solution)/shard_map/ppermute | solution.py:885
  51.1 1.0 %collective-permute-done.12.refs_7_ = f32[192,128]{1,0:T(8,128)S(1)} collective-permute-done((f32[192,128]{1,0:T(8,128)S(1)}, f32[192,128]{1,0:T(8,128)S(1)}, u32[]{:S(2)}, u32[]{:S(2)}) %collective-permute-start.12) | collective-permute-done | bytes 98336 | tf_op jit(solution)/shard_map/ppermute | solution.py:885
  52.1 1.0 %shard_map.36 = f32[2,3,32,1024]{3,2,1,0:T(8,128)} custom-call(f32[192,128]{1,0:T(8,128)S(1)} %get-tuple-element.48.refs_6_.refs_0_, f32[192,128]{1,0:T(8,128)S(1)} %collective-permute-done.6.refs_1_, f32[192,128]{1,0:T(8,128)S(1)} %collective-permute-done.7.refs_2_, f32[192,128]{1,0:T(8,128)S(1)} %collective-permute-done.8.refs_3_, ...), custom_call_target="tpu_custom_call" | custom-call | flops 1572864 | bytes 1572864 | tf_op jit(solution)/shard_map/pallas_call | solution.py:871
  (7 shorter events, 0.1 us)
Async XLA Ops:
  0.0 1.1 %copy-start = (f32[2,3,32,1024]{3,2,1,0:T(8,128)S(1)}, f32[2,3,32,1024]{3,2,1,0:T(8,128)}, u32[]{:S(2)}) copy-start(f32[2,3,32,1024]{3,2,1,0:T(8,128)} %state_ref.1) | copy-start | bytes 2359300
  1.4 8.1 %collective-permute-start = (f32[400,128]{1,0:T(8,128)S(1)}, f32[400,128]{1,0:T(8,128)S(1)}, u32[]{:S(2)}, u32[]{:S(2)}) collective-permute-start(f32[400,128]{1,0:T(8,128)S(1)} %get-tuple-element.32), channel_id=1, source_target_pairs={{0,4},{4,0},{8,12},{12,8},{16,20},{20,16},{24,28},{28,24},{1,5},{5... | collective-permute-start | bytes 614408 | tf_op jit(solution)/shard_map/ppermute | solution.py:885
  4.4 8.0 %collective-permute-start.1 = (f32[400,128]{1,0:T(8,128)S(1)}, f32[400,128]{1,0:T(8,128)S(1)}, u32[]{:S(2)}, u32[]{:S(2)}) collective-permute-start(f32[400,128]{1,0:T(8,128)S(1)} %get-tuple-element.33), channel_id=1, source_target_pairs={{0,8},{4,12},{8,0},{12,4},{16,24},{20,28},{24,16},{28,20},{1,9},{5... | collective-permute-start | bytes 614408 | tf_op jit(solution)/shard_map/ppermute | solution.py:885
  6.0 9.2 %collective-permute-start.2 = (f32[400,128]{1,0:T(8,128)S(1)}, f32[400,128]{1,0:T(8,128)S(1)}, u32[]{:S(2)}, u32[]{:S(2)}) collective-permute-start(f32[400,128]{1,0:T(8,128)S(1)} %get-tuple-element.34), channel_id=1, source_target_pairs={{0,12},{4,8},{8,4},{12,0},{16,28},{20,24},{24,20},{28,16},{1,13},{... | collective-permute-start | bytes 614408 | tf_op jit(solution)/shard_map/ppermute | solution.py:885
  6.0 1.0 %copy-start.1 = (f32[3,32,1024]{2,1,0:T(8,128)S(1)}, f32[3,32,1024]{2,1,0:T(8,128)}, u32[]{:S(2)}) copy-start(f32[3,32,1024]{2,1,0:T(8,128)} %initial_ref.1) | copy-start | bytes 1179652
  16.6 20.5 %collective-permute-start.3 = (f32[600,128]{1,0:T(8,128)S(1)}, f32[600,128]{1,0:T(8,128)S(1)}, u32[]{:S(2)}, u32[]{:S(2)}) collective-permute-start(f32[600,128]{1,0:T(8,128)S(1)} %get-tuple-element.37.refs_0_), channel_id=1, source_target_pairs={{0,16},{4,20},{8,24},{12,28},{16,0},{20,4},{24,8},{28,12},{1,17},{... | collective-permute-start | bytes 921608 | tf_op jit(solution)/shard_map/ppermute | solution.py:885
  19.5 4.4 %collective-permute-start.4 = (f32[240,128]{1,0:T(8,128)S(1)}, f32[240,128]{1,0:T(8,128)S(1)}, u32[]{:S(2)}, u32[]{:S(2)}) collective-permute-start(f32[240,128]{1,0:T(8,128)S(1)} %get-tuple-element.43), channel_id=1, source_target_pairs={{0,1},{1,2},{2,3},{3,0},{4,5},{5,6},{6,7},{7,4},{8,9},{9,10},{10,1... | collective-permute-start | bytes 368648 | tf_op jit(solution)/shard_map/ppermute | solution.py:932
  19.5 4.6 %collective-permute-start.5 = (f32[240,128]{1,0:T(8,128)S(1)}, f32[240,128]{1,0:T(8,128)S(1)}, u32[]{:S(2)}, u32[]{:S(2)}) collective-permute-start(f32[240,128]{1,0:T(8,128)S(1)} %get-tuple-element.44), channel_id=1, source_target_pairs={{1,0},{2,1},{3,2},{0,3},{5,4},{6,5},{7,6},{4,7},{9,8},{10,9},{11,1... | collective-permute-start | bytes 368648 | tf_op jit(solution)/shard_map/ppermute | solution.py:933
  24.9 17.7 %collective-permute-start.9 = (f32[352,128]{1,0:T(8,128)S(1)}, f32[352,128]{1,0:T(8,128)S(1)}, u32[]{:S(2)}, u32[]{:S(2)}) collective-permute-start(f32[352,128]{1,0:T(8,128)S(1)} %get-tuple-element.52.refs_2_), channel_id=1, source_target_pairs={{0,16},{4,20},{8,24},{12,28},{16,0},{20,4},{24,8},{28,12},{1,17},{... | collective-permute-start | bytes 540680 | tf_op jit(solution)/shard_map/ppermute | solution.py:885
  39.0 7.5 %collective-permute-start.6 = (f32[192,128]{1,0:T(8,128)S(1)}, f32[192,128]{1,0:T(8,128)S(1)}, u32[]{:S(2)}, u32[]{:S(2)}) collective-permute-start(f32[192,128]{1,0:T(8,128)S(1)} %get-tuple-element.49), channel_id=1, source_target_pairs={{0,4},{4,0},{8,12},{12,8},{16,20},{20,16},{24,28},{28,24},{1,5},{5... | collective-permute-start | bytes 294920 | tf_op jit(solution)/shard_map/ppermute | solution.py:885
  40.6 7.9 %collective-permute-start.7 = (f32[192,128]{1,0:T(8,128)S(1)}, f32[192,128]{1,0:T(8,128)S(1)}, u32[]{:S(2)}, u32[]{:S(2)}) collective-permute-start(f32[192,128]{1,0:T(8,128)S(1)} %get-tuple-element.50), channel_id=1, source_target_pairs={{0,8},{4,12},{8,0},{12,4},{16,24},{20,28},{24,16},{28,20},{1,9},{5... | collective-permute-start | bytes 294920 | tf_op jit(solution)/shard_map/ppermute | solution.py:885
  40.6 7.9 %collective-permute-start.8 = (f32[192,128]{1,0:T(8,128)S(1)}, f32[192,128]{1,0:T(8,128)S(1)}, u32[]{:S(2)}, u32[]{:S(2)}) collective-permute-start(f32[192,128]{1,0:T(8,128)S(1)} %get-tuple-element.51), channel_id=1, source_target_pairs={{0,12},{4,8},{8,4},{12,0},{16,28},{20,24},{24,20},{28,16},{1,13},{... | collective-permute-start | bytes 294920 | tf_op jit(solution)/shard_map/ppermute | solution.py:885
  44.9 5.3 %collective-permute-start.10 = (f32[192,128]{1,0:T(8,128)S(1)}, f32[192,128]{1,0:T(8,128)S(1)}, u32[]{:S(2)}, u32[]{:S(2)}) collective-permute-start(f32[192,128]{1,0:T(8,128)S(1)} %get-tuple-element.54), channel_id=1, source_target_pairs={{0,4},{4,0},{8,12},{12,8},{16,20},{20,16},{24,28},{28,24},{1,5},{5... | collective-permute-start | bytes 294920 | tf_op jit(solution)/shard_map/ppermute | solution.py:885
  46.5 4.6 %collective-permute-start.11 = (f32[192,128]{1,0:T(8,128)S(1)}, f32[192,128]{1,0:T(8,128)S(1)}, u32[]{:S(2)}, u32[]{:S(2)}) collective-permute-start(f32[192,128]{1,0:T(8,128)S(1)} %get-tuple-element.55), channel_id=1, source_target_pairs={{0,8},{4,12},{8,0},{12,4},{16,24},{20,28},{24,16},{28,20},{1,9},{5... | collective-permute-start | bytes 294920 | tf_op jit(solution)/shard_map/ppermute | solution.py:885
  46.5 5.6 %collective-permute-start.12 = (f32[192,128]{1,0:T(8,128)S(1)}, f32[192,128]{1,0:T(8,128)S(1)}, u32[]{:S(2)}, u32[]{:S(2)}) collective-permute-start(f32[192,128]{1,0:T(8,128)S(1)} %get-tuple-element.56), channel_id=1, source_target_pairs={{0,12},{4,8},{8,4},{12,0},{16,28},{20,24},{24,20},{28,16},{1,13},{... | collective-permute-start | bytes 294920 | tf_op jit(solution)/shard_map/ppermute | solution.py:885

commit v5 on v4

--- a/solution.py
+++ b/solution.py
@@ -540,13 +540,13 @@
         hrhs[f, sides.span, :] = held[f]
 
     def entry(source, target):
+        after = (steps - 1 - source).astype(jnp.float32)
+        weight = jnp.full((LANES, LANES), RATE**steps, jnp.float32)
         result = jnp.zeros((LANES, LANES), jnp.float32)
-        for p in range(SWEEPS):
-            j = SWEEPS - p
-            for n in range(steps):
-                weight = RATE ** (steps - 1 + j) * binomial(steps - 1 - n + j - 1, j - 1)
-                result = jnp.where((target == p) & (source == n), weight, result)
-        return result
+        for j in range(1, SWEEPS + 1):
+            result = jnp.where(target == SWEEPS - j, weight, result)
+            weight = weight * (after + float(j)) * (RATE / j)
+        return jnp.where(source < steps, result, 0.0)
 
     handed = sides.product(held, lane_matrix(entry))
     for f in range(FIELDS):
@@ -592,11 +592,11 @@
         hstate[f, MAIN + 8 * r : MAIN + 8 * r + 8, :] = found
     Side(MAIN, rows).set_seams(seams, [side[f] for f in range(fields)])
 
-    @pl.loop(1, blocks)
-    def _(t):
+    for t in range(1, blocks):
+
         def send(p, f, c, value):
             at = ((p * FIELDS + f) * SLABS + c) * (rows - 8) + 8 * t - 8
-            sent[pl.ds(pl.multiple_of(at, 8), 8), :] = value
+            sent[at : at + 8, :] = value
 
         residual_tile(steps, first_half, ROW0 + 8 * t, state, rhs, seams, ends, send)
 
@@ -789,8 +789,7 @@
         final = k == SWEEPS - 1
         turns, place = finals if final else places
 
-        @pl.loop(0, turns)
-        def _(t):
+        for t in range(turns):
             start = place(t)
             here = pl.ds(start, 8)
             seam = [seams[f, here, :] for f in range(FIELDS)]
@@ -814,8 +813,8 @@
                 for f in range(FIELDS):
                     ends[f, here, :] = last[f]
             else:
-                at = pl.ds(pl.multiple_of(8 * t, 8), 8)
-                from_chain = pl.ds(pl.multiple_of(start - MAIN, 8), 8)
+                at = pl.ds(8 * t, 8)
+                from_chain = pl.ds(start - MAIN, 8)
                 for f, c in EACH:
                     for n in range(steps):
                         total = scale * chained[n, f, c, from_chain, :]

time: 53.3 us -> 51.7 us (0.970)
  Pallas kernels: 12.1 us -> 10.4 us
    pallas_call x9, Pallas kernels: 12.1 us -> 10.4 us  [call(): pl.pallas_call(kernel, out_shape=shapes, in_specs=in_specs, out_specs=[wh...]
  transfers between devices with their start and end apart: 13 -> 13, of which waited for: 9 -> 9; matrix products, arithmetic and copies ran while one was open for 0% -> 0% of each run, Pallas kernels for 18% -> 16%
where the time goes in v5:
time: 51.7 us; the launch traced here: 51.5 us
  waiting for transfers between devices  22.2 us (43%)
  starting transfers between devices  16.7 us (32%)
  Pallas kernels  10.4 us (20%)
  local copies, waits for them, and re-layouts  2.13 us (4%)
    ppermute x11, waiting for transfers between devices, swap(): return lax.ppermute(piece, 'tm', [(k, k ^ b) for k in range(count)])  19.3 us
    ppermute x11, starting transfers between devices, swap(): return lax.ppermute(piece, 'tm', [(k, k ^ b) for k in range(count)])  14.9 us
    pallas_call x9, Pallas kernels, call(): pl.pallas_call(kernel, out_shape=shapes, in_specs=in_specs, out_specs=[wh...  10.4 us
    ppermute x1, waiting for transfers between devices, fast_on_device(): lax.ppermute(down, 'space', [(i, (i + 1) % bands) for i in range(bands)])  2.56 us
    unnamed x4, local copies, waits for them, and re-layouts  2.13 us
    ppermute x1, starting transfers between devices, fast_on_device(): lax.ppermute(up, 'space', [((i + 1) % bands, i) for i in range(bands)])  1.73 us
  transfers between devices with their start and end apart: 13, of which 9 were waited for; matrix products, arithmetic and copies ran while one was open for 0% of the time, Pallas kernels for 16%

profile of v5, /device:TPU:0, one launch (start us, length us, event | category | flops | bytes accessed | tf_op | source)
XLA Modules:
  0.0 51.5 jit_solution(851947105207978990)
XLA Ops:
  0.0 1.1 %copy-done = f32[2,3,32,1024]{3,2,1,0:T(8,128)S(1)} copy-done((f32[2,3,32,1024]{3,2,1,0:T(8,128)S(1)}, f32[2,3,32,1024]{3,2,1,0:T(8,128)}, u32[]{:S(2)}) %copy-start) | copy-done | bytes 786456
  1.1 0.3 shard_map.28
  1.4 3.0 %collective-permute-start = (f32[400,128]{1,0:T(8,128)S(1)}, f32[400,128]{1,0:T(8,128)S(1)}, u32[]{:S(2)}, u32[]{:S(2)}) collective-permute-start(f32[400,128]{1,0:T(8,128)S(1)} %get-tuple-element.32), channel_id=1, source_target_pairs={{0,4},{4,0},{8,12},{12,8},{16,20},{20,16},{24,28},{28,24},{1,5},{5... | collective-permute-start | bytes 614408 | tf_op jit(solution)/shard_map/ppermute | solution.py:884
  4.4 1.6 %collective-permute-start.1 = (f32[400,128]{1,0:T(8,128)S(1)}, f32[400,128]{1,0:T(8,128)S(1)}, u32[]{:S(2)}, u32[]{:S(2)}) collective-permute-start(f32[400,128]{1,0:T(8,128)S(1)} %get-tuple-element.33), channel_id=1, source_target_pairs={{0,8},{4,12},{8,0},{12,4},{16,24},{20,28},{24,16},{28,20},{1,9},{5... | collective-permute-start | bytes 614408 | tf_op jit(solution)/shard_map/ppermute | solution.py:884
  6.0 0.0 collective-permute-start.2
  6.0 1.0 %copy-done.1 = f32[3,32,1024]{2,1,0:T(8,128)S(1)} copy-done((f32[3,32,1024]{2,1,0:T(8,128)S(1)}, f32[3,32,1024]{2,1,0:T(8,128)}, u32[]{:S(2)}) %copy-start.1) | copy-done | bytes 393240
  7.0 2.5 %collective-permute-done.refs_1_ = f32[400,128]{1,0:T(8,128)S(1)} collective-permute-done((f32[400,128]{1,0:T(8,128)S(1)}, f32[400,128]{1,0:T(8,128)S(1)}, u32[]{:S(2)}, u32[]{:S(2)}) %collective-permute-start) | collective-permute-done | bytes 204832 | tf_op jit(solution)/shard_map/ppermute | solution.py:884
  9.5 2.9 %collective-permute-done.1.refs_2_ = f32[400,128]{1,0:T(8,128)S(1)} collective-permute-done((f32[400,128]{1,0:T(8,128)S(1)}, f32[400,128]{1,0:T(8,128)S(1)}, u32[]{:S(2)}, u32[]{:S(2)}) %collective-permute-start.1) | collective-permute-done | bytes 204832 | tf_op jit(solution)/shard_map/ppermute | solution.py:884
  12.4 2.7 %collective-permute-done.2.refs_3_ = f32[400,128]{1,0:T(8,128)S(1)} collective-permute-done((f32[400,128]{1,0:T(8,128)S(1)}, f32[400,128]{1,0:T(8,128)S(1)}, u32[]{:S(2)}, u32[]{:S(2)}) %collective-permute-start.2) | collective-permute-done | bytes 204832 | tf_op jit(solution)/shard_map/ppermute | solution.py:884
  15.2 1.0 %shard_map.30 = (f32[9,3,2,56,128]{4,3,2,1,0:T(8,128)S(1)}, f32[8,3,2,56,128]{4,3,2,1,0:T(8,128)S(1)}, f32[3,56,128]{2,1,0:T(8,128)S(1)}, f32[3,56,128]{2,1,0:T(...) custom-call(f32[400,128]{1,0:T(8,128)S(1)} %get-tuple-element.31._.refs_0_, ...), custom_call_target="tpu_custom_call" | custom-call | flops 4419584 | bytes 4419584 | tf_op jit(solution)/shard_map/pallas_call | solution.py:870
  16.1 2.8 %collective-permute-start.3 = (f32[600,128]{1,0:T(8,128)S(1)}, f32[600,128]{1,0:T(8,128)S(1)}, u32[]{:S(2)}, u32[]{:S(2)}) collective-permute-start(f32[600,128]{1,0:T(8,128)S(1)} %get-tuple-element.37.refs_0_), channel_id=1, source_target_pairs={{0,16},{4,20},{8,24},{12,28},{16,0},{20,4},{24,8},{28,12},{1,17},{... | collective-permute-start | bytes 921608 | tf_op jit(solution)/shard_map/ppermute | solution.py:884
  19.0 0.1 collective-permute-start.4
  19.1 1.7 %collective-permute-start.5 = (f32[240,128]{1,0:T(8,128)S(1)}, f32[240,128]{1,0:T(8,128)S(1)}, u32[]{:S(2)}, u32[]{:S(2)}) collective-permute-start(f32[240,128]{1,0:T(8,128)S(1)} %get-tuple-element.44), channel_id=1, source_target_pairs={{1,0},{2,1},{3,2},{0,3},{5,4},{6,5},{7,6},{4,7},{9,8},{10,9},{11,1... | collective-permute-start | bytes 368648 | tf_op jit(solution)/shard_map/ppermute | solution.py:932
  20.8 2.6 %collective-permute-done.4.refs_6_ = f32[240,128]{1,0:T(8,128)S(1)} collective-permute-done((f32[240,128]{1,0:T(8,128)S(1)}, f32[240,128]{1,0:T(8,128)S(1)}, u32[]{:S(2)}, u32[]{:S(2)}) %collective-permute-start.4) | collective-permute-done | bytes 122912 | tf_op jit(solution)/shard_map/ppermute | solution.py:931
  23.4 0.4 collective-permute-done.5.refs_7_
  23.7 0.6 %shard_map.32 = (f32[9,3,2,56,128]{4,3,2,1,0:T(8,128)S(1)}, f32[8,3,2,56,128]{4,3,2,1,0:T(8,128)S(1)}, f32[3,56,128]{2,1,0:T(8,128)S(1)}, f32[3,56,128]{2,1,0:T(8,128)S(1)}, f32[352,128]{1,0:T(8,128)S(1)}) custom-call(f32[9,3,2,56,128]{4,3,2,1,0:T(8,128)S(1)} %get-tuple-element.38.refs_0_, ...), custom_call_target="tpu_custom_call", output_to_operand_aliasing={{0}: (0, {}), {1}: (1, {}), {2}: (2, {}), {3}: (3, {})} | custom-call | flops 6717440 | bytes 6717440 | tf_op jit(solution)/shard_map/pallas_call | solution.py:870
  24.4 0.4 collective-permute-start.9
  24.8 4.4 %shard_map.33.refs_2_.refs_4_ = f32[8,3,2,32,128]{4,3,2,1,0:T(8,128)S(1)} custom-call(f32[8,3,2,56,128]{4,3,2,1,0:T(8,128)S(1)} %get-tuple-element.45.rhs, f32[3,56,128]{2,1,0:T(8,128)S(1)} %get-tuple-element.46.hrhs), custom_call_target="tpu_custom_call" | custom-call | flops 2248704 | bytes 2248704 | tf_op jit(solution)/shard_map/pallas_call | solution.py:870
  29.1 7.6 %collective-permute-done.3.refs_1_ = f32[600,128]{1,0:T(8,128)S(1)} collective-permute-done((f32[600,128]{1,0:T(8,128)S(1)}, f32[600,128]{1,0:T(8,128)S(1)}, u32[]{:S(2)}, u32[]{:S(2)}) %collective-permute-start.3) | collective-permute-done | bytes 307232 | tf_op jit(solution)/shard_map/ppermute | solution.py:884
  36.7 1.4 %shard_map.34 = (f32[192,128]{1,0:T(8,128)S(1)}, f32[192,128]{1,0:T(8,128)S(1)}, f32[192,128]{1,0:T(8,128)S(1)}, f32[192,128]{1,0:T(8,128)S(1)}) custom-call(f32[600,128]{1,0:T(8,128)S(1)} %get-tuple-element.37.refs_0_, f32[600,128]{1,0:T(8,128)S(1)} %collective-permute-done.3.refs_1_, f32[8,3,2,32,128]{4,3,2,1,0:T(8,128)S(1)} %shard_map.33.refs_2_.refs_4_, ...), custom_call_target="tpu_custom_call" | custom-call | flops 3342336 | bytes 3342336 | tf_op jit(solution)/shard_map/pallas_call | solution.py:870
  38.1 1.6 %collective-permute-start.6 = (f32[192,128]{1,0:T(8,128)S(1)}, f32[192,128]{1,0:T(8,128)S(1)}, u32[]{:S(2)}, u32[]{:S(2)}) collective-permute-start(f32[192,128]{1,0:T(8,128)S(1)} %get-tuple-element.49), channel_id=1, source_target_pairs={{0,4},{4,0},{8,12},{12,8},{16,20},{20,16},{24,28},{28,24},{1,5},{5... | collective-permute-start | bytes 294920 | tf_op jit(solution)/shard_map/ppermute | solution.py:884
  39.6 2.0 %collective-permute-start.8 = (f32[192,128]{1,0:T(8,128)S(1)}, f32[192,128]{1,0:T(8,128)S(1)}, u32[]{:S(2)}, u32[]{:S(2)}) collective-permute-start(f32[192,128]{1,0:T(8,128)S(1)} %get-tuple-element.51), channel_id=1, source_target_pairs={{0,12},{4,8},{8,4},{12,0},{16,28},{20,24},{24,20},{28,16},{1,13},{... | collective-permute-start | bytes 294920 | tf_op jit(solution)/shard_map/ppermute | solution.py:884
  41.6 1.7 %shard_map.35 = (f32[192,128]{1,0:T(8,128)S(1)}, f32[192,128]{1,0:T(8,128)S(1)}, f32[192,128]{1,0:T(8,128)S(1)}, f32[192,128]{1,0:T(8,128)S(1)}) custom-call(f32[600,128]{1,0:T(8,128)S(1)} %get-tuple-element.37.refs_0_, f32[600,128]{1,0:T(8,128)S(1)} %collective-permute-done.3.refs_1_, f32[352,128]{1,0:T(8,128)S(1)} %get-tuple-element.52.refs_2_, ...), custom_call_target="tpu_custom_call" | custom-call | flops 3702784 | bytes 3702784 | tf_op jit(solution)/shard_map/pallas_call | solution.py:870
  43.3 1.6 %collective-permute-start.10 = (f32[192,128]{1,0:T(8,128)S(1)}, f32[192,128]{1,0:T(8,128)S(1)}, u32[]{:S(2)}, u32[]{:S(2)}) collective-permute-start(f32[192,128]{1,0:T(8,128)S(1)} %get-tuple-element.54), channel_id=1, source_target_pairs={{0,4},{4,0},{8,12},{12,8},{16,20},{20,16},{24,28},{28,24},{1,5},{5... | collective-permute-start | bytes 294920 | tf_op jit(solution)/shard_map/ppermute | solution.py:884
  44.9 0.0 collective-permute-start.11
  44.9 0.0 collective-permute-done.6.refs_1_
  44.9 2.0 %collective-permute-start.12 = (f32[192,128]{1,0:T(8,128)S(1)}, f32[192,128]{1,0:T(8,128)S(1)}, u32[]{:S(2)}, u32[]{:S(2)}) collective-permute-start(f32[192,128]{1,0:T(8,128)S(1)} %get-tuple-element.56), channel_id=1, source_target_pairs={{0,12},{4,8},{8,4},{12,0},{16,28},{20,24},{24,20},{28,16},{1,13},{... | collective-permute-start | bytes 294920 | tf_op jit(solution)/shard_map/ppermute | solution.py:884
  46.9 0.0 collective-permute-done.7.refs_2_
  46.9 1.7 %collective-permute-done.10.refs_5_ = f32[192,128]{1,0:T(8,128)S(1)} collective-permute-done((f32[192,128]{1,0:T(8,128)S(1)}, f32[192,128]{1,0:T(8,128)S(1)}, u32[]{:S(2)}, u32[]{:S(2)}) %collective-permute-start.10) | collective-permute-done | bytes 98336 | tf_op jit(solution)/shard_map/ppermute | solution.py:884
  48.6 0.9 %collective-permute-done.11.refs_6_ = f32[192,128]{1,0:T(8,128)S(1)} collective-permute-done((f32[192,128]{1,0:T(8,128)S(1)}, f32[192,128]{1,0:T(8,128)S(1)}, u32[]{:S(2)}, u32[]{:S(2)}) %collective-permute-start.11) | collective-permute-done | bytes 98336 | tf_op jit(solution)/shard_map/ppermute | solution.py:884
  49.5 1.0 %collective-permute-done.12.refs_7_ = f32[192,128]{1,0:T(8,128)S(1)} collective-permute-done((f32[192,128]{1,0:T(8,128)S(1)}, f32[192,128]{1,0:T(8,128)S(1)}, u32[]{:S(2)}, u32[]{:S(2)}) %collective-permute-start.12) | collective-permute-done | bytes 98336 | tf_op jit(solution)/shard_map/ppermute | solution.py:884
  50.5 1.0 %shard_map.36 = f32[2,3,32,1024]{3,2,1,0:T(8,128)} custom-call(f32[192,128]{1,0:T(8,128)S(1)} %get-tuple-element.48.refs_6_.refs_0_, f32[192,128]{1,0:T(8,128)S(1)} %collective-permute-done.6.refs_1_, f32[192,128]{1,0:T(8,128)S(1)} %collective-permute-done.7.refs_2_, f32[192,128]{1,0:T(8,128)S(1)} %collective-permute-done.8.refs_3_, ...), custom_call_target="tpu_custom_call" | custom-call | flops 1572864 | bytes 1572864 | tf_op jit(solution)/shard_map/pallas_call | solution.py:870
  (7 shorter events, 0.1 us)
Async XLA Ops:
  0.0 1.1 %copy-start = (f32[2,3,32,1024]{3,2,1,0:T(8,128)S(1)}, f32[2,3,32,1024]{3,2,1,0:T(8,128)}, u32[]{:S(2)}) copy-start(f32[2,3,32,1024]{3,2,1,0:T(8,128)} %state_ref.1) | copy-start | bytes 2359300
  1.4 8.1 %collective-permute-start = (f32[400,128]{1,0:T(8,128)S(1)}, f32[400,128]{1,0:T(8,128)S(1)}, u32[]{:S(2)}, u32[]{:S(2)}) collective-permute-start(f32[400,128]{1,0:T(8,128)S(1)} %get-tuple-element.32), channel_id=1, source_target_pairs={{0,4},{4,0},{8,12},{12,8},{16,20},{20,16},{24,28},{28,24},{1,5},{5... | collective-permute-start | bytes 614408 | tf_op jit(solution)/shard_map/ppermute | solution.py:884
  4.4 8.0 %collective-permute-start.1 = (f32[400,128]{1,0:T(8,128)S(1)}, f32[400,128]{1,0:T(8,128)S(1)}, u32[]{:S(2)}, u32[]{:S(2)}) collective-permute-start(f32[400,128]{1,0:T(8,128)S(1)} %get-tuple-element.33), channel_id=1, source_target_pairs={{0,8},{4,12},{8,0},{12,4},{16,24},{20,28},{24,16},{28,20},{1,9},{5... | collective-permute-start | bytes 614408 | tf_op jit(solution)/shard_map/ppermute | solution.py:884
  6.0 9.2 %collective-permute-start.2 = (f32[400,128]{1,0:T(8,128)S(1)}, f32[400,128]{1,0:T(8,128)S(1)}, u32[]{:S(2)}, u32[]{:S(2)}) collective-permute-start(f32[400,128]{1,0:T(8,128)S(1)} %get-tuple-element.34), channel_id=1, source_target_pairs={{0,12},{4,8},{8,4},{12,0},{16,28},{20,24},{24,20},{28,16},{1,13},{... | collective-permute-start | bytes 614408 | tf_op jit(solution)/shard_map/ppermute | solution.py:884
  6.0 1.0 %copy-start.1 = (f32[3,32,1024]{2,1,0:T(8,128)S(1)}, f32[3,32,1024]{2,1,0:T(8,128)}, u32[]{:S(2)}) copy-start(f32[3,32,1024]{2,1,0:T(8,128)} %initial_ref.1) | copy-start | bytes 1179652
  16.1 20.6 %collective-permute-start.3 = (f32[600,128]{1,0:T(8,128)S(1)}, f32[600,128]{1,0:T(8,128)S(1)}, u32[]{:S(2)}, u32[]{:S(2)}) collective-permute-start(f32[600,128]{1,0:T(8,128)S(1)} %get-tuple-element.37.refs_0_), channel_id=1, source_target_pairs={{0,16},{4,20},{8,24},{12,28},{16,0},{20,4},{24,8},{28,12},{1,17},{... | collective-permute-start | bytes 921608 | tf_op jit(solution)/shard_map/ppermute | solution.py:884
  19.0 4.4 %collective-permute-start.4 = (f32[240,128]{1,0:T(8,128)S(1)}, f32[240,128]{1,0:T(8,128)S(1)}, u32[]{:S(2)}, u32[]{:S(2)}) collective-permute-start(f32[240,128]{1,0:T(8,128)S(1)} %get-tuple-element.43), channel_id=1, source_target_pairs={{0,1},{1,2},{2,3},{3,0},{4,5},{5,6},{6,7},{7,4},{8,9},{9,10},{10,1... | collective-permute-start | bytes 368648 | tf_op jit(solution)/shard_map/ppermute | solution.py:931
  19.1 4.6 %collective-permute-start.5 = (f32[240,128]{1,0:T(8,128)S(1)}, f32[240,128]{1,0:T(8,128)S(1)}, u32[]{:S(2)}, u32[]{:S(2)}) collective-permute-start(f32[240,128]{1,0:T(8,128)S(1)} %get-tuple-element.44), channel_id=1, source_target_pairs={{1,0},{2,1},{3,2},{0,3},{5,4},{6,5},{7,6},{4,7},{9,8},{10,9},{11,1... | collective-permute-start | bytes 368648 | tf_op jit(solution)/shard_map/ppermute | solution.py:932
  24.4 17.3 %collective-permute-start.9 = (f32[352,128]{1,0:T(8,128)S(1)}, f32[352,128]{1,0:T(8,128)S(1)}, u32[]{:S(2)}, u32[]{:S(2)}) collective-permute-start(f32[352,128]{1,0:T(8,128)S(1)} %get-tuple-element.52.refs_2_), channel_id=1, source_target_pairs={{0,16},{4,20},{8,24},{12,28},{16,0},{20,4},{24,8},{28,12},{1,17},{... | collective-permute-start | bytes 540680 | tf_op jit(solution)/shard_map/ppermute | solution.py:884
  38.1 6.8 %collective-permute-start.6 = (f32[192,128]{1,0:T(8,128)S(1)}, f32[192,128]{1,0:T(8,128)S(1)}, u32[]{:S(2)}, u32[]{:S(2)}) collective-permute-start(f32[192,128]{1,0:T(8,128)S(1)} %get-tuple-element.49), channel_id=1, source_target_pairs={{0,4},{4,0},{8,12},{12,8},{16,20},{20,16},{24,28},{28,24},{1,5},{5... | collective-permute-start | bytes 294920 | tf_op jit(solution)/shard_map/ppermute | solution.py:884
  39.6 7.2 %collective-permute-start.7 = (f32[192,128]{1,0:T(8,128)S(1)}, f32[192,128]{1,0:T(8,128)S(1)}, u32[]{:S(2)}, u32[]{:S(2)}) collective-permute-start(f32[192,128]{1,0:T(8,128)S(1)} %get-tuple-element.50), channel_id=1, source_target_pairs={{0,8},{4,12},{8,0},{12,4},{16,24},{20,28},{24,16},{28,20},{1,9},{5... | collective-permute-start | bytes 294920 | tf_op jit(solution)/shard_map/ppermute | solution.py:884
  39.6 7.2 %collective-permute-start.8 = (f32[192,128]{1,0:T(8,128)S(1)}, f32[192,128]{1,0:T(8,128)S(1)}, u32[]{:S(2)}, u32[]{:S(2)}) collective-permute-start(f32[192,128]{1,0:T(8,128)S(1)} %get-tuple-element.51), channel_id=1, source_target_pairs={{0,12},{4,8},{8,4},{12,0},{16,28},{20,24},{24,20},{28,16},{1,13},{... | collective-permute-start | bytes 294920 | tf_op jit(solution)/shard_map/ppermute | solution.py:884
  43.3 5.3 %collective-permute-start.10 = (f32[192,128]{1,0:T(8,128)S(1)}, f32[192,128]{1,0:T(8,128)S(1)}, u32[]{:S(2)}, u32[]{:S(2)}) collective-permute-start(f32[192,128]{1,0:T(8,128)S(1)} %get-tuple-element.54), channel_id=1, source_target_pairs={{0,4},{4,0},{8,12},{12,8},{16,20},{20,16},{24,28},{28,24},{1,5},{5... | collective-permute-start | bytes 294920 | tf_op jit(solution)/shard_map/ppermute | solution.py:884
  44.9 4.6 %collective-permute-start.11 = (f32[192,128]{1,0:T(8,128)S(1)}, f32[192,128]{1,0:T(8,128)S(1)}, u32[]{:S(2)}, u32[]{:S(2)}) collective-permute-start(f32[192,128]{1,0:T(8,128)S(1)} %get-tuple-element.55), channel_id=1, source_target_pairs={{0,8},{4,12},{8,0},{12,4},{16,24},{20,28},{24,16},{28,20},{1,9},{5... | collective-permute-start | bytes 294920 | tf_op jit(solution)/shard_map/ppermute | solution.py:884
  44.9 5.6 %collective-permute-start.12 = (f32[192,128]{1,0:T(8,128)S(1)}, f32[192,128]{1,0:T(8,128)S(1)}, u32[]{:S(2)}, u32[]{:S(2)}) collective-permute-start(f32[192,128]{1,0:T(8,128)S(1)} %get-tuple-element.56), channel_id=1, source_target_pairs={{0,12},{4,8},{8,4},{12,0},{16,28},{20,24},{24,20},{28,16},{1,13},{... | collective-permute-start | bytes 294920 | tf_op jit(solution)/shard_map/ppermute | solution.py:884

commit v6 on v5

--- a/solution.py
+++ b/solution.py
@@ -843,22 +843,34 @@
                     at += size
 
 
-def unpack_kernel(width_tm, *refs):
+def unpack_kernel(width_tm, size, *refs):
     half = width_tm // 2
-    inner, outer, out = refs[:half], refs[half : 2 * half], refs[2 * half]
-    steps_dev, fields, rows, _ = out.shape
+    out = refs[-1]
+    steps_dev, fields, _, _ = out.shape
     mine = lax.axis_index("tm") & (half - 1)
-    size = rows - 16
+    t = pl.program_id(0)
     for b in range(half):
-        k = 0
+        at = 0
         for c in range(SLABS):
             here = tile_at(SLABS * (mine ^ b) + c)
             for i in range(steps_dev):
                 for f in range(fields):
-                    out[i, f, 8 : rows - 8, here] = inner[b][size * k : size * (k + 1), :]
-                    out[i, f, 0:8, here] = outer[b][16 * k : 16 * k + 8, :]
-                    out[i, f, rows - 8 : rows, here] = outer[b][16 * k + 8 : 16 * k + 16, :]
-                    k += 1
+                    out[i, f, :, here] = refs[b][pl.ds(pl.multiple_of(at + 8 * t, 8), 8), :]
+                    at += size
+
+
+def unpack(width_tm, shape, pieces, size, place, held=()):
+    steps_dev, fields, _, columns = shape
+    return pl.pallas_call(
+        functools.partial(unpack_kernel, width_tm, size),
+        grid=(size // 8,),
+        out_shape=jax.ShapeDtypeStruct(shape, jnp.float32),
+        in_specs=[pl.BlockSpec(memory_space=pltpu.VMEM)] * len(pieces)
+        + [pl.BlockSpec(memory_space=pl.ANY)] * len(held),
+        out_specs=pl.BlockSpec((steps_dev, fields, 8, columns), lambda t: (0, 0, place(t), 0)),
+        input_output_aliases={len(pieces): 0} if held else {},
+        compiler_params=pltpu.CompilerParams(vmem_limit_bytes=VMEM_BYTES),
+    )(*pieces, *held)
 
 
 def call(kernel, out_shapes, operands, scratch=(), aliases=None, after=()):
@@ -958,7 +970,10 @@
             after=results[:1],
         )
         results += [parts[0]] + [swap(parts[b], b) for b in range(1, half)]
-    (updated,) = call(functools.partial(unpack_kernel, width_tm), [state.shape], results)
+    updated = unpack(width_tm, state.shape, results[:half], rows - 16, lambda t: t + 1)
+    updated = unpack(
+        width_tm, state.shape, results[half:], 16, lambda t: t * (rows // 8 - 1), (updated,)
+    )
     return updated
 
 

time: 51.7 us -> 51.5 us (level)
  waiting for transfers between devices: 22.2 us -> 21.5 us
    pallas_call x0 -> x2, Pallas kernels: none -> 1.53 us  [unpack(): pl.pallas_call(functools.partial(unpack_kernel, width_tm, size), grid=(si...]
    pallas_call x9 -> x8, Pallas kernels: 10.4 us -> 9.37 us  [call(): pl.pallas_call(kernel, out_shape=shapes, in_specs=in_specs, out_specs=[wh...]
    ppermute x11, waiting for transfers between devices: 19.3 us -> 18.6 us  [swap(): return lax.ppermute(piece, 'tm', [(k, k ^ b) for k in range(count)])]
  transfers between devices with their start and end apart: 13 -> 13, of which waited for: 9 -> 9; matrix products, arithmetic and copies ran while one was open for 0% -> 0% of each run, Pallas kernels for 16% -> 17%
where the time goes in v6:
time: 51.5 us; the launch traced here: 51.3 us
  waiting for transfers between devices  21.5 us (42%)
  starting transfers between devices  16.7 us (32%)
  Pallas kernels  10.9 us (21%)
  local copies, waits for them, and re-layouts  2.13 us (4%)
    ppermute x11, waiting for transfers between devices, swap(): return lax.ppermute(piece, 'tm', [(k, k ^ b) for k in range(count)])  18.6 us
    ppermute x11, starting transfers between devices, swap(): return lax.ppermute(piece, 'tm', [(k, k ^ b) for k in range(count)])  14.9 us
    pallas_call x8, Pallas kernels, call(): pl.pallas_call(kernel, out_shape=shapes, in_specs=in_specs, out_specs=[wh...  9.37 us
    ppermute x1, waiting for transfers between devices, fast_on_device(): lax.ppermute(down, 'space', [(i, (i + 1) % bands) for i in range(bands)])  2.56 us
    unnamed x4, local copies, waits for them, and re-layouts  2.13 us
    ppermute x1, starting transfers between devices, fast_on_device(): lax.ppermute(up, 'space', [((i + 1) % bands, i) for i in range(bands)])  1.73 us
    pallas_call x2, Pallas kernels, unpack(): pl.pallas_call(functools.partial(unpack_kernel, width_tm, size), grid=(si...  1.53 us
  transfers between devices with their start and end apart: 13, of which 9 were waited for; matrix products, arithmetic and copies ran while one was open for 0% of the time, Pallas kernels for 17%

profile of v6, /device:TPU:0, one launch (start us, length us, event | category | flops | bytes accessed | tf_op | source)
XLA Modules:
  0.0 51.3 jit_solution(7437587167334849399)
XLA Ops:
  0.0 1.1 %copy-done = f32[2,3,32,1024]{3,2,1,0:T(8,128)S(1)} copy-done((f32[2,3,32,1024]{3,2,1,0:T(8,128)S(1)}, f32[2,3,32,1024]{3,2,1,0:T(8,128)}, u32[]{:S(2)}) %copy-start) | copy-done | bytes 786456
  1.1 0.3 shard_map.28
  1.4 3.0 %collective-permute-start = (f32[400,128]{1,0:T(8,128)S(1)}, f32[400,128]{1,0:T(8,128)S(1)}, u32[]{:S(2)}, u32[]{:S(2)}) collective-permute-start(f32[400,128]{1,0:T(8,128)S(1)} %get-tuple-element.32), channel_id=1, source_target_pairs={{0,4},{4,0},{8,12},{12,8},{16,20},{20,16},{24,28},{28,24},{1,5},{5... | collective-permute-start | bytes 614408 | tf_op jit(solution)/shard_map/ppermute | solution.py:896
  4.4 1.6 %collective-permute-start.1 = (f32[400,128]{1,0:T(8,128)S(1)}, f32[400,128]{1,0:T(8,128)S(1)}, u32[]{:S(2)}, u32[]{:S(2)}) collective-permute-start(f32[400,128]{1,0:T(8,128)S(1)} %get-tuple-element.33), channel_id=1, source_target_pairs={{0,8},{4,12},{8,0},{12,4},{16,24},{20,28},{24,16},{28,20},{1,9},{5... | collective-permute-start | bytes 614408 | tf_op jit(solution)/shard_map/ppermute | solution.py:896
  6.0 1.0 %copy-done.1 = f32[3,32,1024]{2,1,0:T(8,128)S(1)} copy-done((f32[3,32,1024]{2,1,0:T(8,128)S(1)}, f32[3,32,1024]{2,1,0:T(8,128)}, u32[]{:S(2)}) %copy-start.1) | copy-done | bytes 393240
  7.0 2.5 %collective-permute-done.refs_1_ = f32[400,128]{1,0:T(8,128)S(1)} collective-permute-done((f32[400,128]{1,0:T(8,128)S(1)}, f32[400,128]{1,0:T(8,128)S(1)}, u32[]{:S(2)}, u32[]{:S(2)}) %collective-permute-start) | collective-permute-done | bytes 204832 | tf_op jit(solution)/shard_map/ppermute | solution.py:896
  9.5 2.9 %collective-permute-done.1.refs_2_ = f32[400,128]{1,0:T(8,128)S(1)} collective-permute-done((f32[400,128]{1,0:T(8,128)S(1)}, f32[400,128]{1,0:T(8,128)S(1)}, u32[]{:S(2)}, u32[]{:S(2)}) %collective-permute-start.1) | collective-permute-done | bytes 204832 | tf_op jit(solution)/shard_map/ppermute | solution.py:896
  12.4 2.7 %collective-permute-done.2.refs_3_ = f32[400,128]{1,0:T(8,128)S(1)} collective-permute-done((f32[400,128]{1,0:T(8,128)S(1)}, f32[400,128]{1,0:T(8,128)S(1)}, u32[]{:S(2)}, u32[]{:S(2)}) %collective-permute-start.2) | collective-permute-done | bytes 204832 | tf_op jit(solution)/shard_map/ppermute | solution.py:896
  15.2 1.0 %shard_map.30 = (f32[9,3,2,56,128]{4,3,2,1,0:T(8,128)S(1)}, f32[8,3,2,56,128]{4,3,2,1,0:T(8,128)S(1)}, f32[3,56,128]{2,1,0:T(8,128)S(1)}, f32[3,56,128]{2,1,0:T(...) custom-call(f32[400,128]{1,0:T(8,128)S(1)} %get-tuple-element.31._.refs_0_, ...), custom_call_target="tpu_custom_call" | custom-call | flops 4419584 | bytes 4419584 | tf_op jit(solution)/shard_map/pallas_call | solution.py:882
  16.1 2.8 %collective-permute-start.3 = (f32[600,128]{1,0:T(8,128)S(1)}, f32[600,128]{1,0:T(8,128)S(1)}, u32[]{:S(2)}, u32[]{:S(2)}) collective-permute-start(f32[600,128]{1,0:T(8,128)S(1)} %get-tuple-element.37.refs_0_), channel_id=1, source_target_pairs={{0,16},{4,20},{8,24},{12,28},{16,0},{20,4},{24,8},{28,12},{1,17},{... | collective-permute-start | bytes 921608 | tf_op jit(solution)/shard_map/ppermute | solution.py:896
  19.0 0.1 collective-permute-start.4
  19.1 1.7 %collective-permute-start.5 = (f32[240,128]{1,0:T(8,128)S(1)}, f32[240,128]{1,0:T(8,128)S(1)}, u32[]{:S(2)}, u32[]{:S(2)}) collective-permute-start(f32[240,128]{1,0:T(8,128)S(1)} %get-tuple-element.44), channel_id=1, source_target_pairs={{1,0},{2,1},{3,2},{0,3},{5,4},{6,5},{7,6},{4,7},{9,8},{10,9},{11,1... | collective-permute-start | bytes 368648 | tf_op jit(solution)/shard_map/ppermute | solution.py:944
  20.8 2.6 %collective-permute-done.4.refs_6_ = f32[240,128]{1,0:T(8,128)S(1)} collective-permute-done((f32[240,128]{1,0:T(8,128)S(1)}, f32[240,128]{1,0:T(8,128)S(1)}, u32[]{:S(2)}, u32[]{:S(2)}) %collective-permute-start.4) | collective-permute-done | bytes 122912 | tf_op jit(solution)/shard_map/ppermute | solution.py:943
  23.4 0.4 collective-permute-done.5.refs_7_
  23.7 0.6 %shard_map.32 = (f32[9,3,2,56,128]{4,3,2,1,0:T(8,128)S(1)}, f32[8,3,2,56,128]{4,3,2,1,0:T(8,128)S(1)}, f32[3,56,128]{2,1,0:T(8,128)S(1)}, f32[3,56,128]{2,1,0:T(8,128)S(1)}, f32[352,128]{1,0:T(8,128)S(1)}) custom-call(f32[9,3,2,56,128]{4,3,2,1,0:T(8,128)S(1)} %get-tuple-element.38.refs_0_, ...), custom_call_target="tpu_custom_call", output_to_operand_aliasing={{0}: (0, {}), {1}: (1, {}), {2}: (2, {}), {3}: (3, {})} | custom-call | flops 6717440 | bytes 6717440 | tf_op jit(solution)/shard_map/pallas_call | solution.py:882
  24.4 0.4 collective-permute-start.6
  24.8 4.4 %shard_map.33.refs_2_.refs_4_ = f32[8,3,2,32,128]{4,3,2,1,0:T(8,128)S(1)} custom-call(f32[8,3,2,56,128]{4,3,2,1,0:T(8,128)S(1)} %get-tuple-element.46.rhs, f32[3,56,128]{2,1,0:T(8,128)S(1)} %get-tuple-element.47.hrhs), custom_call_target="tpu_custom_call" | custom-call | flops 2248704 | bytes 2248704 | tf_op jit(solution)/shard_map/pallas_call | solution.py:882
  29.1 7.6 %collective-permute-done.3.refs_1_ = f32[600,128]{1,0:T(8,128)S(1)} collective-permute-done((f32[600,128]{1,0:T(8,128)S(1)}, f32[600,128]{1,0:T(8,128)S(1)}, u32[]{:S(2)}, u32[]{:S(2)}) %collective-permute-start.3) | collective-permute-done | bytes 307232 | tf_op jit(solution)/shard_map/ppermute | solution.py:896
  36.7 1.4 %shard_map.34 = (f32[192,128]{1,0:T(8,128)S(1)}, f32[192,128]{1,0:T(8,128)S(1)}, f32[192,128]{1,0:T(8,128)S(1)}, f32[192,128]{1,0:T(8,128)S(1)}) custom-call(f32[600,128]{1,0:T(8,128)S(1)} %get-tuple-element.37.refs_0_, f32[600,128]{1,0:T(8,128)S(1)} %collective-permute-done.3.refs_1_, f32[8,3,2,32,128]{4,3,2,1,0:T(8,128)S(1)} %shard_map.33.refs_2_.refs_4_, ...), custom_call_target="tpu_custom_call" | custom-call | flops 3342336 | bytes 3342336 | tf_op jit(solution)/shard_map/pallas_call | solution.py:882
  38.1 1.6 %collective-permute-start.10 = (f32[192,128]{1,0:T(8,128)S(1)}, f32[192,128]{1,0:T(8,128)S(1)}, u32[]{:S(2)}, u32[]{:S(2)}) collective-permute-start(f32[192,128]{1,0:T(8,128)S(1)} %get-tuple-element.54), channel_id=1, source_target_pairs={{0,4},{4,0},{8,12},{12,8},{16,20},{20,16},{24,28},{28,24},{1,5},{5... | collective-permute-start | bytes 294920 | tf_op jit(solution)/shard_map/ppermute | solution.py:896
  39.6 0.0 collective-permute-start.11
  39.6 2.0 %collective-permute-start.12 = (f32[192,128]{1,0:T(8,128)S(1)}, f32[192,128]{1,0:T(8,128)S(1)}, u32[]{:S(2)}, u32[]{:S(2)}) collective-permute-start(f32[192,128]{1,0:T(8,128)S(1)} %get-tuple-element.56), channel_id=1, source_target_pairs={{0,12},{4,8},{8,4},{12,0},{16,28},{20,24},{24,20},{28,16},{1,13},{... | collective-permute-start | bytes 294920 | tf_op jit(solution)/shard_map/ppermute | solution.py:896
  41.6 0.0 collective-permute-done.6.refs_3_
  41.6 1.7 %shard_map.35 = (f32[192,128]{1,0:T(8,128)S(1)}, f32[192,128]{1,0:T(8,128)S(1)}, f32[192,128]{1,0:T(8,128)S(1)}, f32[192,128]{1,0:T(8,128)S(1)}) custom-call(f32[600,128]{1,0:T(8,128)S(1)} %get-tuple-element.37.refs_0_, f32[600,128]{1,0:T(8,128)S(1)} %collective-permute-done.3.refs_1_, f32[352,128]{1,0:T(8,128)S(1)} %get-tuple-element.45.refs_2_, ...), custom_call_target="tpu_custom_call" | custom-call | flops 3702784 | bytes 3702784 | tf_op jit(solution)/shard_map/pallas_call | solution.py:882
  43.3 1.6 %collective-permute-start.7 = (f32[192,128]{1,0:T(8,128)S(1)}, f32[192,128]{1,0:T(8,128)S(1)}, u32[]{:S(2)}, u32[]{:S(2)}) collective-permute-start(f32[192,128]{1,0:T(8,128)S(1)} %get-tuple-element.51), channel_id=1, source_target_pairs={{0,4},{4,0},{8,12},{12,8},{16,20},{20,16},{24,28},{28,24},{1,5},{5... | collective-permute-start | bytes 294920 | tf_op jit(solution)/shard_map/ppermute | solution.py:896
  44.9 0.0 collective-permute-start.8
  44.9 2.0 %collective-permute-start.9 = (f32[192,128]{1,0:T(8,128)S(1)}, f32[192,128]{1,0:T(8,128)S(1)}, u32[]{:S(2)}, u32[]{:S(2)}) collective-permute-start(f32[192,128]{1,0:T(8,128)S(1)} %get-tuple-element.53), channel_id=1, source_target_pairs={{0,12},{4,8},{8,4},{12,0},{16,28},{20,24},{24,20},{28,16},{1,13},{... | collective-permute-start | bytes 294920 | tf_op jit(solution)/shard_map/ppermute | solution.py:896
  46.9 0.8 %shard_map.36.refs_4_ = f32[2,3,32,1024]{3,2,1,0:T(8,128)} custom-call(f32[192,128]{1,0:T(8,128)S(1)} %get-tuple-element.49.refs_6_.refs_0_, f32[192,128]{1,0:T(8,128)S(1)} %collective-permute-done.10.refs_1_, f32[192,128]{1,0:T(8,128)S(1)} %collective-permute-done.11.refs_2_, f32[192,128]{1,0:T(8,128)S(1)} %collective-permute-done.12.refs_3_), custom_call_target="tpu_custom_call" | custom-call | tf_op jit(solution)/shard_map/pallas_call | solution.py:864
  47.6 1.0 %collective-permute-done.7.refs_1_ = f32[192,128]{1,0:T(8,128)S(1)} collective-permute-done((f32[192,128]{1,0:T(8,128)S(1)}, f32[192,128]{1,0:T(8,128)S(1)}, u32[]{:S(2)}, u32[]{:S(2)}) %collective-permute-start.7) | collective-permute-done | bytes 98336 | tf_op jit(solution)/shard_map/ppermute | solution.py:896
  48.6 0.9 %collective-permute-done.8.refs_2_ = f32[192,128]{1,0:T(8,128)S(1)} collective-permute-done((f32[192,128]{1,0:T(8,128)S(1)}, f32[192,128]{1,0:T(8,128)S(1)}, u32[]{:S(2)}, u32[]{:S(2)}) %collective-permute-start.8) | collective-permute-done | bytes 98336 | tf_op jit(solution)/shard_map/ppermute | solution.py:896
  49.5 1.0 %collective-permute-done.9.refs_3_ = f32[192,128]{1,0:T(8,128)S(1)} collective-permute-done((f32[192,128]{1,0:T(8,128)S(1)}, f32[192,128]{1,0:T(8,128)S(1)}, u32[]{:S(2)}, u32[]{:S(2)}) %collective-permute-start.9) | collective-permute-done | bytes 98336 | tf_op jit(solution)/shard_map/ppermute | solution.py:896
  50.5 0.8 %shard_map.37 = f32[2,3,32,1024]{3,2,1,0:T(8,128)} custom-call(f32[192,128]{1,0:T(8,128)S(1)} %get-tuple-element.50.refs_0_, f32[192,128]{1,0:T(8,128)S(1)} %collective-permute-done.7.refs_1_, f32[192,128]{1,0:T(8,128)S(1)} %collective-permute-done.8.refs_2_, f32[192,128]{1,0:T(8,128)S(1)} %collective-permute-done.9.refs_3_, ...), custom_call_target="tpu_custom_call", output_to_operand_aliasing={{}: (4, {})} | custom-call | tf_op jit(solution)/shard_map/pallas_call | solution.py:864
  (8 shorter events, 0.1 us)
Async XLA Ops:
  0.0 1.1 %copy-start = (f32[2,3,32,1024]{3,2,1,0:T(8,128)S(1)}, f32[2,3,32,1024]{3,2,1,0:T(8,128)}, u32[]{:S(2)}) copy-start(f32[2,3,32,1024]{3,2,1,0:T(8,128)} %state_ref.1) | copy-start | bytes 2359300
  1.4 8.1 %collective-permute-start = (f32[400,128]{1,0:T(8,128)S(1)}, f32[400,128]{1,0:T(8,128)S(1)}, u32[]{:S(2)}, u32[]{:S(2)}) collective-permute-start(f32[400,128]{1,0:T(8,128)S(1)} %get-tuple-element.32), channel_id=1, source_target_pairs={{0,4},{4,0},{8,12},{12,8},{16,20},{20,16},{24,28},{28,24},{1,5},{5... | collective-permute-start | bytes 614408 | tf_op jit(solution)/shard_map/ppermute | solution.py:896
  4.4 8.0 %collective-permute-start.1 = (f32[400,128]{1,0:T(8,128)S(1)}, f32[400,128]{1,0:T(8,128)S(1)}, u32[]{:S(2)}, u32[]{:S(2)}) collective-permute-start(f32[400,128]{1,0:T(8,128)S(1)} %get-tuple-element.33), channel_id=1, source_target_pairs={{0,8},{4,12},{8,0},{12,4},{16,24},{20,28},{24,16},{28,20},{1,9},{5... | collective-permute-start | bytes 614408 | tf_op jit(solution)/shard_map/ppermute | solution.py:896
  6.0 9.2 %collective-permute-start.2 = (f32[400,128]{1,0:T(8,128)S(1)}, f32[400,128]{1,0:T(8,128)S(1)}, u32[]{:S(2)}, u32[]{:S(2)}) collective-permute-start(f32[400,128]{1,0:T(8,128)S(1)} %get-tuple-element.34), channel_id=1, source_target_pairs={{0,12},{4,8},{8,4},{12,0},{16,28},{20,24},{24,20},{28,16},{1,13},{... | collective-permute-start | bytes 614408 | tf_op jit(solution)/shard_map/ppermute | solution.py:896
  6.0 1.0 %copy-start.1 = (f32[3,32,1024]{2,1,0:T(8,128)S(1)}, f32[3,32,1024]{2,1,0:T(8,128)}, u32[]{:S(2)}) copy-start(f32[3,32,1024]{2,1,0:T(8,128)} %initial_ref.1) | copy-start | bytes 1179652
  16.1 20.6 %collective-permute-start.3 = (f32[600,128]{1,0:T(8,128)S(1)}, f32[600,128]{1,0:T(8,128)S(1)}, u32[]{:S(2)}, u32[]{:S(2)}) collective-permute-start(f32[600,128]{1,0:T(8,128)S(1)} %get-tuple-element.37.refs_0_), channel_id=1, source_target_pairs={{0,16},{4,20},{8,24},{12,28},{16,0},{20,4},{24,8},{28,12},{1,17},{... | collective-permute-start | bytes 921608 | tf_op jit(solution)/shard_map/ppermute | solution.py:896
  19.0 4.4 %collective-permute-start.4 = (f32[240,128]{1,0:T(8,128)S(1)}, f32[240,128]{1,0:T(8,128)S(1)}, u32[]{:S(2)}, u32[]{:S(2)}) collective-permute-start(f32[240,128]{1,0:T(8,128)S(1)} %get-tuple-element.43), channel_id=1, source_target_pairs={{0,1},{1,2},{2,3},{3,0},{4,5},{5,6},{6,7},{7,4},{8,9},{9,10},{10,1... | collective-permute-start | bytes 368648 | tf_op jit(solution)/shard_map/ppermute | solution.py:943
  19.1 4.6 %collective-permute-start.5 = (f32[240,128]{1,0:T(8,128)S(1)}, f32[240,128]{1,0:T(8,128)S(1)}, u32[]{:S(2)}, u32[]{:S(2)}) collective-permute-start(f32[240,128]{1,0:T(8,128)S(1)} %get-tuple-element.44), channel_id=1, source_target_pairs={{1,0},{2,1},{3,2},{0,3},{5,4},{6,5},{7,6},{4,7},{9,8},{10,9},{11,1... | collective-permute-start | bytes 368648 | tf_op jit(solution)/shard_map/ppermute | solution.py:944
  24.4 17.3 %collective-permute-start.6 = (f32[352,128]{1,0:T(8,128)S(1)}, f32[352,128]{1,0:T(8,128)S(1)}, u32[]{:S(2)}, u32[]{:S(2)}) collective-permute-start(f32[352,128]{1,0:T(8,128)S(1)} %get-tuple-element.45.refs_2_), channel_id=1, source_target_pairs={{0,16},{4,20},{8,24},{12,28},{16,0},{20,4},{24,8},{28,12},{1,17},{... | collective-permute-start | bytes 540680 | tf_op jit(solution)/shard_map/ppermute | solution.py:896
  38.1 6.8 %collective-permute-start.10 = (f32[192,128]{1,0:T(8,128)S(1)}, f32[192,128]{1,0:T(8,128)S(1)}, u32[]{:S(2)}, u32[]{:S(2)}) collective-permute-start(f32[192,128]{1,0:T(8,128)S(1)} %get-tuple-element.54), channel_id=1, source_target_pairs={{0,4},{4,0},{8,12},{12,8},{16,20},{20,16},{24,28},{28,24},{1,5},{5... | collective-permute-start | bytes 294920 | tf_op jit(solution)/shard_map/ppermute | solution.py:896
  39.6 7.2 %collective-permute-start.11 = (f32[192,128]{1,0:T(8,128)S(1)}, f32[192,128]{1,0:T(8,128)S(1)}, u32[]{:S(2)}, u32[]{:S(2)}) collective-permute-start(f32[192,128]{1,0:T(8,128)S(1)} %get-tuple-element.55), channel_id=1, source_target_pairs={{0,8},{4,12},{8,0},{12,4},{16,24},{20,28},{24,16},{28,20},{1,9},{5... | collective-permute-start | bytes 294920 | tf_op jit(solution)/shard_map/ppermute | solution.py:896
  39.6 7.2 %collective-permute-start.12 = (f32[192,128]{1,0:T(8,128)S(1)}, f32[192,128]{1,0:T(8,128)S(1)}, u32[]{:S(2)}, u32[]{:S(2)}) collective-permute-start(f32[192,128]{1,0:T(8,128)S(1)} %get-tuple-element.56), channel_id=1, source_target_pairs={{0,12},{4,8},{8,4},{12,0},{16,28},{20,24},{24,20},{28,16},{1,13},{... | collective-permute-start | bytes 294920 | tf_op jit(solution)/shard_map/ppermute | solution.py:896
  43.3 5.3 %collective-permute-start.7 = (f32[192,128]{1,0:T(8,128)S(1)}, f32[192,128]{1,0:T(8,128)S(1)}, u32[]{:S(2)}, u32[]{:S(2)}) collective-permute-start(f32[192,128]{1,0:T(8,128)S(1)} %get-tuple-element.51), channel_id=1, source_target_pairs={{0,4},{4,0},{8,12},{12,8},{16,20},{20,16},{24,28},{28,24},{1,5},{5... | collective-permute-start | bytes 294920 | tf_op jit(solution)/shard_map/ppermute | solution.py:896
  44.9 4.6 %collective-permute-start.8 = (f32[192,128]{1,0:T(8,128)S(1)}, f32[192,128]{1,0:T(8,128)S(1)}, u32[]{:S(2)}, u32[]{:S(2)}) collective-permute-start(f32[192,128]{1,0:T(8,128)S(1)} %get-tuple-element.52), channel_id=1, source_target_pairs={{0,8},{4,12},{8,0},{12,4},{16,24},{20,28},{24,16},{28,20},{1,9},{5... | collective-permute-start | bytes 294920 | tf_op jit(solution)/shard_map/ppermute | solution.py:896
  44.9 5.6 %collective-permute-start.9 = (f32[192,128]{1,0:T(8,128)S(1)}, f32[192,128]{1,0:T(8,128)S(1)}, u32[]{:S(2)}, u32[]{:S(2)}) collective-permute-start(f32[192,128]{1,0:T(8,128)S(1)} %get-tuple-element.53), channel_id=1, source_target_pairs={{0,12},{4,8},{8,4},{12,0},{16,28},{20,24},{24,20},{28,16},{1,13},{... | collective-permute-start | bytes 294920 | tf_op jit(solution)/shard_map/ppermute | solution.py:896

commit v7 on v6

--- a/solution.py
+++ b/solution.py
@@ -817,10 +817,10 @@
                 from_chain = pl.ds(start - MAIN, 8)
                 for f, c in EACH:
                     for n in range(steps):
-                        total = scale * chained[n, f, c, from_chain, :]
+                        total = (scale * RATE**n) * chained[n, f, c, from_chain, :]
                         for p in range(SWEEPS):
-                            total = total + binomial(n + p, p) * found[p, f, c]
-                        result[n, f, c, at, :] = state[n + 1, f, c, here, :] - total * RATE**n
+                            total = total + (binomial(n + p, p) * RATE**n) * found[p, f, c]
+                        result[n, f, c, at, :] = state[n + 1, f, c, here, :] - total
 
         if not final:
             value = off_diagonal(*sides.parts(hold, ends))

time: 51.5 us -> 51.4 us (level)
  no operation moved by 1% of the time
where the time goes in v7:
time: 51.4 us; the launch traced here: 51.2 us
  waiting for transfers between devices  21.5 us (42%)
  starting transfers between devices  16.7 us (32%)
  Pallas kernels  10.9 us (21%)
  local copies, waits for them, and re-layouts  2.13 us (4%)
    ppermute x11, waiting for transfers between devices, swap(): return lax.ppermute(piece, 'tm', [(k, k ^ b) for k in range(count)])  18.6 us
    ppermute x11, starting transfers between devices, swap(): return lax.ppermute(piece, 'tm', [(k, k ^ b) for k in range(count)])  14.9 us
    pallas_call x8, Pallas kernels, call(): pl.pallas_call(kernel, out_shape=shapes, in_specs=in_specs, out_specs=[wh...  9.34 us
    ppermute x1, waiting for transfers between devices, fast_on_device(): lax.ppermute(down, 'space', [(i, (i + 1) % bands) for i in range(bands)])  2.56 us
    unnamed x4, local copies, waits for them, and re-layouts  2.13 us
    ppermute x1, starting transfers between devices, fast_on_device(): lax.ppermute(up, 'space', [((i + 1) % bands, i) for i in range(bands)])  1.73 us
    pallas_call x2, Pallas kernels, unpack(): pl.pallas_call(functools.partial(unpack_kernel, width_tm, size), grid=(si...  1.53 us
  transfers between devices with their start and end apart: 13, of which 9 were waited for; matrix products, arithmetic and copies ran while one was open for 0% of the time, Pallas kernels for 17%

profile of v7, /device:TPU:0, one launch (start us, length us, event | category | flops | bytes accessed | tf_op | source)
XLA Modules:
  0.0 51.2 jit_solution(10044987480479051626)
XLA Ops:
  0.0 1.1 %copy-done = f32[2,3,32,1024]{3,2,1,0:T(8,128)S(1)} copy-done((f32[2,3,32,1024]{3,2,1,0:T(8,128)S(1)}, f32[2,3,32,1024]{3,2,1,0:T(8,128)}, u32[]{:S(2)}) %copy-start) | copy-done | bytes 786456
  1.1 0.3 shard_map.28
  1.4 3.0 %collective-permute-start = (f32[400,128]{1,0:T(8,128)S(1)}, f32[400,128]{1,0:T(8,128)S(1)}, u32[]{:S(2)}, u32[]{:S(2)}) collective-permute-start(f32[400,128]{1,0:T(8,128)S(1)} %get-tuple-element.32), channel_id=1, source_target_pairs={{0,4},{4,0},{8,12},{12,8},{16,20},{20,16},{24,28},{28,24},{1,5},{5... | collective-permute-start | bytes 614408 | tf_op jit(solution)/shard_map/ppermute | solution.py:896
  4.4 1.6 %collective-permute-start.1 = (f32[400,128]{1,0:T(8,128)S(1)}, f32[400,128]{1,0:T(8,128)S(1)}, u32[]{:S(2)}, u32[]{:S(2)}) collective-permute-start(f32[400,128]{1,0:T(8,128)S(1)} %get-tuple-element.33), channel_id=1, source_target_pairs={{0,8},{4,12},{8,0},{12,4},{16,24},{20,28},{24,16},{28,20},{1,9},{5... | collective-permute-start | bytes 614408 | tf_op jit(solution)/shard_map/ppermute | solution.py:896
  6.0 1.0 %copy-done.1 = f32[3,32,1024]{2,1,0:T(8,128)S(1)} copy-done((f32[3,32,1024]{2,1,0:T(8,128)S(1)}, f32[3,32,1024]{2,1,0:T(8,128)}, u32[]{:S(2)}) %copy-start.1) | copy-done | bytes 393240
  7.0 2.5 %collective-permute-done.refs_1_ = f32[400,128]{1,0:T(8,128)S(1)} collective-permute-done((f32[400,128]{1,0:T(8,128)S(1)}, f32[400,128]{1,0:T(8,128)S(1)}, u32[]{:S(2)}, u32[]{:S(2)}) %collective-permute-start) | collective-permute-done | bytes 204832 | tf_op jit(solution)/shard_map/ppermute | solution.py:896
  9.5 2.9 %collective-permute-done.1.refs_2_ = f32[400,128]{1,0:T(8,128)S(1)} collective-permute-done((f32[400,128]{1,0:T(8,128)S(1)}, f32[400,128]{1,0:T(8,128)S(1)}, u32[]{:S(2)}, u32[]{:S(2)}) %collective-permute-start.1) | collective-permute-done | bytes 204832 | tf_op jit(solution)/shard_map/ppermute | solution.py:896
  12.4 2.7 %collective-permute-done.2.refs_3_ = f32[400,128]{1,0:T(8,128)S(1)} collective-permute-done((f32[400,128]{1,0:T(8,128)S(1)}, f32[400,128]{1,0:T(8,128)S(1)}, u32[]{:S(2)}, u32[]{:S(2)}) %collective-permute-start.2) | collective-permute-done | bytes 204832 | tf_op jit(solution)/shard_map/ppermute | solution.py:896
  15.2 1.0 %shard_map.30 = (f32[9,3,2,56,128]{4,3,2,1,0:T(8,128)S(1)}, f32[8,3,2,56,128]{4,3,2,1,0:T(8,128)S(1)}, f32[3,56,128]{2,1,0:T(8,128)S(1)}, f32[3,56,128]{2,1,0:T(...) custom-call(f32[400,128]{1,0:T(8,128)S(1)} %get-tuple-element.31._.refs_0_, ...), custom_call_target="tpu_custom_call" | custom-call | flops 4419584 | bytes 4419584 | tf_op jit(solution)/shard_map/pallas_call | solution.py:882
  16.1 2.8 %collective-permute-start.3 = (f32[600,128]{1,0:T(8,128)S(1)}, f32[600,128]{1,0:T(8,128)S(1)}, u32[]{:S(2)}, u32[]{:S(2)}) collective-permute-start(f32[600,128]{1,0:T(8,128)S(1)} %get-tuple-element.37.refs_0_), channel_id=1, source_target_pairs={{0,16},{4,20},{8,24},{12,28},{16,0},{20,4},{24,8},{28,12},{1,17},{... | collective-permute-start | bytes 921608 | tf_op jit(solution)/shard_map/ppermute | solution.py:896
  19.0 0.1 collective-permute-start.4
  19.1 1.7 %collective-permute-start.5 = (f32[240,128]{1,0:T(8,128)S(1)}, f32[240,128]{1,0:T(8,128)S(1)}, u32[]{:S(2)}, u32[]{:S(2)}) collective-permute-start(f32[240,128]{1,0:T(8,128)S(1)} %get-tuple-element.44), channel_id=1, source_target_pairs={{1,0},{2,1},{3,2},{0,3},{5,4},{6,5},{7,6},{4,7},{9,8},{10,9},{11,1... | collective-permute-start | bytes 368648 | tf_op jit(solution)/shard_map/ppermute | solution.py:944
  20.8 2.6 %collective-permute-done.4.refs_6_ = f32[240,128]{1,0:T(8,128)S(1)} collective-permute-done((f32[240,128]{1,0:T(8,128)S(1)}, f32[240,128]{1,0:T(8,128)S(1)}, u32[]{:S(2)}, u32[]{:S(2)}) %collective-permute-start.4) | collective-permute-done | bytes 122912 | tf_op jit(solution)/shard_map/ppermute | solution.py:943
  23.4 0.4 collective-permute-done.5.refs_7_
  23.7 0.6 %shard_map.32 = (f32[9,3,2,56,128]{4,3,2,1,0:T(8,128)S(1)}, f32[8,3,2,56,128]{4,3,2,1,0:T(8,128)S(1)}, f32[3,56,128]{2,1,0:T(8,128)S(1)}, f32[3,56,128]{2,1,0:T(8,128)S(1)}, f32[352,128]{1,0:T(8,128)S(1)}) custom-call(f32[9,3,2,56,128]{4,3,2,1,0:T(8,128)S(1)} %get-tuple-element.38.refs_0_, ...), custom_call_target="tpu_custom_call", output_to_operand_aliasing={{0}: (0, {}), {1}: (1, {}), {2}: (2, {}), {3}: (3, {})} | custom-call | flops 6717440 | bytes 6717440 | tf_op jit(solution)/shard_map/pallas_call | solution.py:882
  24.4 0.4 collective-permute-start.6
  24.8 4.4 %shard_map.33.refs_2_.refs_4_ = f32[8,3,2,32,128]{4,3,2,1,0:T(8,128)S(1)} custom-call(f32[8,3,2,56,128]{4,3,2,1,0:T(8,128)S(1)} %get-tuple-element.46.rhs, f32[3,56,128]{2,1,0:T(8,128)S(1)} %get-tuple-element.47.hrhs), custom_call_target="tpu_custom_call" | custom-call | flops 2248704 | bytes 2248704 | tf_op jit(solution)/shard_map/pallas_call | solution.py:882
  29.1 7.6 %collective-permute-done.3.refs_1_ = f32[600,128]{1,0:T(8,128)S(1)} collective-permute-done((f32[600,128]{1,0:T(8,128)S(1)}, f32[600,128]{1,0:T(8,128)S(1)}, u32[]{:S(2)}, u32[]{:S(2)}) %collective-permute-start.3) | collective-permute-done | bytes 307232 | tf_op jit(solution)/shard_map/ppermute | solution.py:896
  36.7 1.4 %shard_map.34 = (f32[192,128]{1,0:T(8,128)S(1)}, f32[192,128]{1,0:T(8,128)S(1)}, f32[192,128]{1,0:T(8,128)S(1)}, f32[192,128]{1,0:T(8,128)S(1)}) custom-call(f32[600,128]{1,0:T(8,128)S(1)} %get-tuple-element.37.refs_0_, f32[600,128]{1,0:T(8,128)S(1)} %collective-permute-done.3.refs_1_, f32[8,3,2,32,128]{4,3,2,1,0:T(8,128)S(1)} %shard_map.33.refs_2_.refs_4_, ...), custom_call_target="tpu_custom_call" | custom-call | flops 3342336 | bytes 3342336 | tf_op jit(solution)/shard_map/pallas_call | solution.py:882
  38.1 1.6 %collective-permute-start.10 = (f32[192,128]{1,0:T(8,128)S(1)}, f32[192,128]{1,0:T(8,128)S(1)}, u32[]{:S(2)}, u32[]{:S(2)}) collective-permute-start(f32[192,128]{1,0:T(8,128)S(1)} %get-tuple-element.54), channel_id=1, source_target_pairs={{0,4},{4,0},{8,12},{12,8},{16,20},{20,16},{24,28},{28,24},{1,5},{5... | collective-permute-start | bytes 294920 | tf_op jit(solution)/shard_map/ppermute | solution.py:896
  39.6 0.0 collective-permute-start.11
  39.6 2.0 %collective-permute-start.12 = (f32[192,128]{1,0:T(8,128)S(1)}, f32[192,128]{1,0:T(8,128)S(1)}, u32[]{:S(2)}, u32[]{:S(2)}) collective-permute-start(f32[192,128]{1,0:T(8,128)S(1)} %get-tuple-element.56), channel_id=1, source_target_pairs={{0,12},{4,8},{8,4},{12,0},{16,28},{20,24},{24,20},{28,16},{1,13},{... | collective-permute-start | bytes 294920 | tf_op jit(solution)/shard_map/ppermute | solution.py:896
  41.6 0.0 collective-permute-done.6.refs_3_
  41.6 1.7 %shard_map.35 = (f32[192,128]{1,0:T(8,128)S(1)}, f32[192,128]{1,0:T(8,128)S(1)}, f32[192,128]{1,0:T(8,128)S(1)}, f32[192,128]{1,0:T(8,128)S(1)}) custom-call(f32[600,128]{1,0:T(8,128)S(1)} %get-tuple-element.37.refs_0_, f32[600,128]{1,0:T(8,128)S(1)} %collective-permute-done.3.refs_1_, f32[352,128]{1,0:T(8,128)S(1)} %get-tuple-element.45.refs_2_, ...), custom_call_target="tpu_custom_call" | custom-call | flops 3702784 | bytes 3702784 | tf_op jit(solution)/shard_map/pallas_call | solution.py:882
  43.3 1.6 %collective-permute-start.7 = (f32[192,128]{1,0:T(8,128)S(1)}, f32[192,128]{1,0:T(8,128)S(1)}, u32[]{:S(2)}, u32[]{:S(2)}) collective-permute-start(f32[192,128]{1,0:T(8,128)S(1)} %get-tuple-element.51), channel_id=1, source_target_pairs={{0,4},{4,0},{8,12},{12,8},{16,20},{20,16},{24,28},{28,24},{1,5},{5... | collective-permute-start | bytes 294920 | tf_op jit(solution)/shard_map/ppermute | solution.py:896
  44.8 0.0 collective-permute-start.8
  44.9 2.0 %collective-permute-start.9 = (f32[192,128]{1,0:T(8,128)S(1)}, f32[192,128]{1,0:T(8,128)S(1)}, u32[]{:S(2)}, u32[]{:S(2)}) collective-permute-start(f32[192,128]{1,0:T(8,128)S(1)} %get-tuple-element.53), channel_id=1, source_target_pairs={{0,12},{4,8},{8,4},{12,0},{16,28},{20,24},{24,20},{28,16},{1,13},{... | collective-permute-start | bytes 294920 | tf_op jit(solution)/shard_map/ppermute | solution.py:896
  46.8 0.8 %shard_map.36.refs_4_ = f32[2,3,32,1024]{3,2,1,0:T(8,128)} custom-call(f32[192,128]{1,0:T(8,128)S(1)} %get-tuple-element.49.refs_6_.refs_0_, f32[192,128]{1,0:T(8,128)S(1)} %collective-permute-done.10.refs_1_, f32[192,128]{1,0:T(8,128)S(1)} %collective-permute-done.11.refs_2_, f32[192,128]{1,0:T(8,128)S(1)} %collective-permute-done.12.refs_3_), custom_call_target="tpu_custom_call" | custom-call | tf_op jit(solution)/shard_map/pallas_call | solution.py:864
  47.6 1.0 %collective-permute-done.7.refs_1_ = f32[192,128]{1,0:T(8,128)S(1)} collective-permute-done((f32[192,128]{1,0:T(8,128)S(1)}, f32[192,128]{1,0:T(8,128)S(1)}, u32[]{:S(2)}, u32[]{:S(2)}) %collective-permute-start.7) | collective-permute-done | bytes 98336 | tf_op jit(solution)/shard_map/ppermute | solution.py:896
  48.6 0.9 %collective-permute-done.8.refs_2_ = f32[192,128]{1,0:T(8,128)S(1)} collective-permute-done((f32[192,128]{1,0:T(8,128)S(1)}, f32[192,128]{1,0:T(8,128)S(1)}, u32[]{:S(2)}, u32[]{:S(2)}) %collective-permute-start.8) | collective-permute-done | bytes 98336 | tf_op jit(solution)/shard_map/ppermute | solution.py:896
  49.5 1.0 %collective-permute-done.9.refs_3_ = f32[192,128]{1,0:T(8,128)S(1)} collective-permute-done((f32[192,128]{1,0:T(8,128)S(1)}, f32[192,128]{1,0:T(8,128)S(1)}, u32[]{:S(2)}, u32[]{:S(2)}) %collective-permute-start.9) | collective-permute-done | bytes 98336 | tf_op jit(solution)/shard_map/ppermute | solution.py:896
  50.5 0.8 %shard_map.37 = f32[2,3,32,1024]{3,2,1,0:T(8,128)} custom-call(f32[192,128]{1,0:T(8,128)S(1)} %get-tuple-element.50.refs_0_, f32[192,128]{1,0:T(8,128)S(1)} %collective-permute-done.7.refs_1_, f32[192,128]{1,0:T(8,128)S(1)} %collective-permute-done.8.refs_2_, f32[192,128]{1,0:T(8,128)S(1)} %collective-permute-done.9.refs_3_, ...), custom_call_target="tpu_custom_call", output_to_operand_aliasing={{}: (4, {})} | custom-call | tf_op jit(solution)/shard_map/pallas_call | solution.py:864
  (8 shorter events, 0.1 us)
Async XLA Ops:
  0.0 1.1 %copy-start = (f32[2,3,32,1024]{3,2,1,0:T(8,128)S(1)}, f32[2,3,32,1024]{3,2,1,0:T(8,128)}, u32[]{:S(2)}) copy-start(f32[2,3,32,1024]{3,2,1,0:T(8,128)} %state_ref.1) | copy-start | bytes 2359300
  1.4 8.1 %collective-permute-start = (f32[400,128]{1,0:T(8,128)S(1)}, f32[400,128]{1,0:T(8,128)S(1)}, u32[]{:S(2)}, u32[]{:S(2)}) collective-permute-start(f32[400,128]{1,0:T(8,128)S(1)} %get-tuple-element.32), channel_id=1, source_target_pairs={{0,4},{4,0},{8,12},{12,8},{16,20},{20,16},{24,28},{28,24},{1,5},{5... | collective-permute-start | bytes 614408 | tf_op jit(solution)/shard_map/ppermute | solution.py:896
  4.4 8.0 %collective-permute-start.1 = (f32[400,128]{1,0:T(8,128)S(1)}, f32[400,128]{1,0:T(8,128)S(1)}, u32[]{:S(2)}, u32[]{:S(2)}) collective-permute-start(f32[400,128]{1,0:T(8,128)S(1)} %get-tuple-element.33), channel_id=1, source_target_pairs={{0,8},{4,12},{8,0},{12,4},{16,24},{20,28},{24,16},{28,20},{1,9},{5... | collective-permute-start | bytes 614408 | tf_op jit(solution)/shard_map/ppermute | solution.py:896
  6.0 9.2 %collective-permute-start.2 = (f32[400,128]{1,0:T(8,128)S(1)}, f32[400,128]{1,0:T(8,128)S(1)}, u32[]{:S(2)}, u32[]{:S(2)}) collective-permute-start(f32[400,128]{1,0:T(8,128)S(1)} %get-tuple-element.34), channel_id=1, source_target_pairs={{0,12},{4,8},{8,4},{12,0},{16,28},{20,24},{24,20},{28,16},{1,13},{... | collective-permute-start | bytes 614408 | tf_op jit(solution)/shard_map/ppermute | solution.py:896
  6.0 1.0 %copy-start.1 = (f32[3,32,1024]{2,1,0:T(8,128)S(1)}, f32[3,32,1024]{2,1,0:T(8,128)}, u32[]{:S(2)}) copy-start(f32[3,32,1024]{2,1,0:T(8,128)} %initial_ref.1) | copy-start | bytes 1179652
  16.1 20.6 %collective-permute-start.3 = (f32[600,128]{1,0:T(8,128)S(1)}, f32[600,128]{1,0:T(8,128)S(1)}, u32[]{:S(2)}, u32[]{:S(2)}) collective-permute-start(f32[600,128]{1,0:T(8,128)S(1)} %get-tuple-element.37.refs_0_), channel_id=1, source_target_pairs={{0,16},{4,20},{8,24},{12,28},{16,0},{20,4},{24,8},{28,12},{1,17},{... | collective-permute-start | bytes 921608 | tf_op jit(solution)/shard_map/ppermute | solution.py:896
  19.0 4.4 %collective-permute-start.4 = (f32[240,128]{1,0:T(8,128)S(1)}, f32[240,128]{1,0:T(8,128)S(1)}, u32[]{:S(2)}, u32[]{:S(2)}) collective-permute-start(f32[240,128]{1,0:T(8,128)S(1)} %get-tuple-element.43), channel_id=1, source_target_pairs={{0,1},{1,2},{2,3},{3,0},{4,5},{5,6},{6,7},{7,4},{8,9},{9,10},{10,1... | collective-permute-start | bytes 368648 | tf_op jit(solution)/shard_map/ppermute | solution.py:943
  19.1 4.6 %collective-permute-start.5 = (f32[240,128]{1,0:T(8,128)S(1)}, f32[240,128]{1,0:T(8,128)S(1)}, u32[]{:S(2)}, u32[]{:S(2)}) collective-permute-start(f32[240,128]{1,0:T(8,128)S(1)} %get-tuple-element.44), channel_id=1, source_target_pairs={{1,0},{2,1},{3,2},{0,3},{5,4},{6,5},{7,6},{4,7},{9,8},{10,9},{11,1... | collective-permute-start | bytes 368648 | tf_op jit(solution)/shard_map/ppermute | solution.py:944
  24.4 17.3 %collective-permute-start.6 = (f32[352,128]{1,0:T(8,128)S(1)}, f32[352,128]{1,0:T(8,128)S(1)}, u32[]{:S(2)}, u32[]{:S(2)}) collective-permute-start(f32[352,128]{1,0:T(8,128)S(1)} %get-tuple-element.45.refs_2_), channel_id=1, source_target_pairs={{0,16},{4,20},{8,24},{12,28},{16,0},{20,4},{24,8},{28,12},{1,17},{... | collective-permute-start | bytes 540680 | tf_op jit(solution)/shard_map/ppermute | solution.py:896
  38.1 6.8 %collective-permute-start.10 = (f32[192,128]{1,0:T(8,128)S(1)}, f32[192,128]{1,0:T(8,128)S(1)}, u32[]{:S(2)}, u32[]{:S(2)}) collective-permute-start(f32[192,128]{1,0:T(8,128)S(1)} %get-tuple-element.54), channel_id=1, source_target_pairs={{0,4},{4,0},{8,12},{12,8},{16,20},{20,16},{24,28},{28,24},{1,5},{5... | collective-permute-start | bytes 294920 | tf_op jit(solution)/shard_map/ppermute | solution.py:896
  39.6 7.2 %collective-permute-start.11 = (f32[192,128]{1,0:T(8,128)S(1)}, f32[192,128]{1,0:T(8,128)S(1)}, u32[]{:S(2)}, u32[]{:S(2)}) collective-permute-start(f32[192,128]{1,0:T(8,128)S(1)} %get-tuple-element.55), channel_id=1, source_target_pairs={{0,8},{4,12},{8,0},{12,4},{16,24},{20,28},{24,16},{28,20},{1,9},{5... | collective-permute-start | bytes 294920 | tf_op jit(solution)/shard_map/ppermute | solution.py:896
  39.6 7.2 %collective-permute-start.12 = (f32[192,128]{1,0:T(8,128)S(1)}, f32[192,128]{1,0:T(8,128)S(1)}, u32[]{:S(2)}, u32[]{:S(2)}) collective-permute-start(f32[192,128]{1,0:T(8,128)S(1)} %get-tuple-element.56), channel_id=1, source_target_pairs={{0,12},{4,8},{8,4},{12,0},{16,28},{20,24},{24,20},{28,16},{1,13},{... | collective-permute-start | bytes 294920 | tf_op jit(solution)/shard_map/ppermute | solution.py:896
  43.3 5.3 %collective-permute-start.7 = (f32[192,128]{1,0:T(8,128)S(1)}, f32[192,128]{1,0:T(8,128)S(1)}, u32[]{:S(2)}, u32[]{:S(2)}) collective-permute-start(f32[192,128]{1,0:T(8,128)S(1)} %get-tuple-element.51), channel_id=1, source_target_pairs={{0,4},{4,0},{8,12},{12,8},{16,20},{20,16},{24,28},{28,24},{1,5},{5... | collective-permute-start | bytes 294920 | tf_op jit(solution)/shard_map/ppermute | solution.py:896
  44.8 4.6 %collective-permute-start.8 = (f32[192,128]{1,0:T(8,128)S(1)}, f32[192,128]{1,0:T(8,128)S(1)}, u32[]{:S(2)}, u32[]{:S(2)}) collective-permute-start(f32[192,128]{1,0:T(8,128)S(1)} %get-tuple-element.52), channel_id=1, source_target_pairs={{0,8},{4,12},{8,0},{12,4},{16,24},{20,28},{24,16},{28,20},{1,9},{5... | collective-permute-start | bytes 294920 | tf_op jit(solution)/shard_map/ppermute | solution.py:896
  44.9 5.6 %collective-permute-start.9 = (f32[192,128]{1,0:T(8,128)S(1)}, f32[192,128]{1,0:T(8,128)S(1)}, u32[]{:S(2)}, u32[]{:S(2)}) collective-permute-start(f32[192,128]{1,0:T(8,128)S(1)} %get-tuple-element.53), channel_id=1, source_target_pairs={{0,12},{4,8},{8,4},{12,0},{16,28},{20,24},{24,20},{28,16},{1,13},{... | collective-permute-start | bytes 294920 | tf_op jit(solution)/shard_map/ppermute | solution.py:896
